TPU v7x, 128 devices: a whole 4x4x4 slice. The times are simulated.
128 devices in a mesh: layer: 4 (over y), strip: 32 (over x, z, core).
Axes of the slice: x: 4, y: 4, z: 4, core: 2. Of those that a mesh axis runs over, the one named last changes fastest.
Arguments:
- launch: bfloat16 [2, 2, 1024, 1024], P(None, None, 'strip'), may hold values from -6 to 6
- screens: float32 [4, 1024, 1024], P('layer', 'strip'), may hold values from -3.140625 to 3.140625
- distance: float32 [4], P('layer'), may hold values from 1024 to 2048
- templates: bfloat16 [1024, 16], replicated, may hold values from -0.1875 to 0.1875
- send_table: int32 [32, 32, 4], P('strip', None, 'layer'), may hold values from 0 to 127, as said below
- send_counts: int32 [32, 32], P('strip'), may hold values from 0 to 4, as said below
Outputs:
- pupil: bfloat16 [2, 2, 1024, 1024], P(None, None, 'strip')
- correlation: float32 [32, 32, 4, 2, 16], P('strip', None, 'layer')
Inputs may be any that keep to these rules, and one draw needn't show every extreme that they name: For each source strip s the 32 x 4 entries send_table[s] are distinct subaperture numbers local to that strip (row by row over its 128 subapertures). `send_counts`: some owner receives 4 live slots from every source.
All inputs are finite; a program needn't handle non-finite values.
Results may differ from a plain program's by a relative error of at most 0.03.
Values may be sent and summed in bfloat16 or wider, within the bound.
No kernel may reach another device: no remote copies, remote signals or barrier semaphores. Data moves between devices by JAX's collectives and lax.ppermute only.
A program may use at most 64 MiB of HBM per device.

v0:
```python
import math

import jax
import jax.numpy as jnp
from jax import lax
from jax.sharding import PartitionSpec as P

SUB = 16


def passed_along(value, axis, steps):
    count = lax.axis_size(axis)
    first, last = (max(0, -steps), min(count, count - steps))
    return lax.ppermute(value, axis, [(source, source + steps) for source in range(first, last)])


def broadcast(x, axis, root):
    mine = lax.axis_index(axis) == root
    return lax.psum(jnp.where(mine, x, jnp.zeros_like(x)), axis)


def fourier_tables(length):
    counter = jnp.arange(length, dtype=jnp.int32)
    product = counter[:, None] * counter[None, :] % length
    angles = product.astype(jnp.float32) * (2.0 * math.pi / length)
    factor = 1.0 / math.sqrt(length)
    return (
        (jnp.cos(angles) * factor).astype(jnp.bfloat16),
        (jnp.sin(angles) * factor).astype(jnp.bfloat16),
    )


def spectral_factor(distance_value, length):
    counter = jnp.arange(length, dtype=jnp.int32)
    signed = jnp.where(counter < length // 2, counter, counter - length).astype(jnp.float32)
    phases = -distance_value * math.pi * signed * signed / float(length * length)
    return (jnp.cos(phases), jnp.sin(phases))


def spot_table(subsize):
    spotsize = 2 * subsize
    outer = jnp.arange(spotsize, dtype=jnp.int32)
    inner = jnp.arange(subsize, dtype=jnp.int32)
    angles = (inner[:, None] * outer[None, :] % spotsize).astype(jnp.float32) * (
        2.0 * math.pi / spotsize
    )
    wave_re = jnp.cos(angles) / math.sqrt(subsize)
    wave_im = -jnp.sin(angles) / math.sqrt(subsize)
    kron_re = (
        wave_re[:, None, :, None] * wave_re[None, :, None, :]
        - wave_im[:, None, :, None] * wave_im[None, :, None, :]
    )
    kron_im = (
        wave_re[:, None, :, None] * wave_im[None, :, None, :]
        + wave_im[:, None, :, None] * wave_re[None, :, None, :]
    )
    kron_re = kron_re.reshape(subsize * subsize, spotsize * spotsize)
    kron_im = kron_im.reshape(subsize * subsize, spotsize * spotsize)
    upper = jnp.concatenate([kron_re, kron_im], axis=1)
    lower = jnp.concatenate([-kron_im, kron_re], axis=1)
    return jnp.concatenate([upper, lower], axis=0).astype(jnp.bfloat16)


def correlate_slots(slots, big_table, templates):
    pixels = templates.shape[0]
    fields_count = slots.shape[-1] // big_table.shape[0]
    shaped = slots.reshape(slots.shape[:-1] + (fields_count, big_table.shape[0]))
    spot_field = jnp.einsum("...i,io->...o", shaped, big_table, preferred_element_type=jnp.float32)
    intensity = (
        spot_field[..., :pixels] * spot_field[..., :pixels]
        + spot_field[..., pixels:] * spot_field[..., pixels:]
    )
    intensity = intensity.astype(jnp.bfloat16)
    return jnp.einsum("...i,io->...o", intensity, templates, preferred_element_type=jnp.float32)


def layer_step(field, screen, distance_value, cosine_table, sine_table, pieces):
    strip_rows = field.shape[1]
    length = field.shape[2]
    real_part = field[0].astype(jnp.float32)
    imag_part = field[1].astype(jnp.float32)
    screen_cos = jnp.cos(screen)
    screen_sin = jnp.sin(screen)
    screened = jnp.stack(
        [
            real_part * screen_cos - imag_part * screen_sin,
            real_part * screen_sin + imag_part * screen_cos,
        ]
    ).astype(jnp.bfloat16)
    factor_re, factor_im = spectral_factor(distance_value, length)
    along_cos = jnp.einsum(
        "prj,jk->kpr", screened, cosine_table, preferred_element_type=jnp.float32
    )
    along_sin = jnp.einsum("prj,jk->kpr", screened, sine_table, preferred_element_type=jnp.float32)
    freq_re = along_cos[:, 0] + along_sin[:, 1]
    freq_im = along_cos[:, 1] - along_sin[:, 0]
    column_re = factor_re[:, None]
    column_im = factor_im[:, None]
    spectrum = jnp.stack(
        [freq_re * column_re - freq_im * column_im, freq_re * column_im + freq_im * column_re],
        axis=1,
    ).astype(jnp.bfloat16)
    spectrum = spectrum.reshape(pieces, length // pieces, 2, strip_rows)
    columns = lax.all_to_all(spectrum, "strip", split_axis=0, concat_axis=3, tiled=True)
    row_cos = jnp.einsum("acpj,jk->acpk", columns, cosine_table, preferred_element_type=jnp.float32)
    row_sin = jnp.einsum("acpj,jk->acpk", columns, sine_table, preferred_element_type=jnp.float32)
    wave_re = row_cos[:, :, 0] + row_sin[:, :, 1]
    wave_im = row_cos[:, :, 1] - row_sin[:, :, 0]
    phased = jnp.stack(
        [wave_re * factor_re - wave_im * factor_im, wave_re * factor_im + wave_im * factor_re],
        axis=2,
    ).astype(jnp.bfloat16)
    back_cos = jnp.einsum("acpj,kj->acpk", phased, cosine_table, preferred_element_type=jnp.float32)
    back_sin = jnp.einsum("acpj,kj->acpk", phased, sine_table, preferred_element_type=jnp.float32)
    columns_done = jnp.stack(
        [back_cos[:, :, 0] - back_sin[:, :, 1], back_cos[:, :, 1] + back_sin[:, :, 0]], axis=2
    ).astype(jnp.bfloat16)
    column_count = columns_done.shape[1]
    regrouped = columns_done.reshape(column_count, 2, pieces, strip_rows)
    returned = lax.all_to_all(regrouped, "strip", split_axis=2, concat_axis=0, tiled=True)
    returned = returned.reshape(length, 2, strip_rows)
    final_cos = jnp.einsum(
        "kpr,kj->prj", returned, cosine_table, preferred_element_type=jnp.float32
    )
    final_sin = jnp.einsum("kpr,kj->prj", returned, sine_table, preferred_element_type=jnp.float32)
    return jnp.stack([final_cos[0] - final_sin[1], final_cos[1] + final_sin[0]]).astype(
        jnp.bfloat16
    )


def per_device(launch, screens, distance, templates, send_table, send_counts):
    sections = lax.axis_size("layer")
    strips = lax.axis_size("strip")
    section_index = lax.axis_index("layer")
    fields = launch.shape[0]
    length = launch.shape[3]
    cosine_table, sine_table = fourier_tables(length)
    steps_total = fields * sections

    def route(moment):
        entering = moment // sections
        leaving = moment // sections
        finishing = moment % sections == sections - 1
        return (entering, leaving, finishing)

    def advance(moment, carry):
        arrived, finished = carry
        entering, leaving, finishing = route(moment)
        loaded = lax.dynamic_index_in_dim(launch, entering, 0, keepdims=False)
        current = jnp.where(section_index == 0, loaded, arrived)
        current = layer_step(current, screens[0], distance[0], cosine_table, sine_table, strips)
        keeping = jnp.logical_and(finishing, section_index == sections - 1)
        placed = lax.dynamic_update_index_in_dim(
            finished, current, jnp.clip(leaving, 0, fields - 1), 0
        )
        finished = jnp.where(keeping, placed, finished)
        arrived = passed_along(current, "layer", 1)
        return (arrived, finished)

    start_field = jnp.zeros(launch.shape[1:], jnp.bfloat16)
    carried = lax.fori_loop(0, steps_total, advance, (start_field, jnp.zeros_like(launch)))
    pupil = broadcast(carried[1], "layer", sections - 1)
    strip_rows = pupil.shape[2]
    blocks = pupil.reshape(fields, 2, strip_rows // SUB, SUB, length // SUB, SUB)
    blocks = blocks.transpose(2, 4, 0, 1, 3, 5).reshape(
        strip_rows // SUB * (length // SUB), fields * 2 * SUB * SUB
    )
    picks = send_table[0]
    live_counts = send_counts[0]
    slots_here = picks.shape[1]
    slot_number = section_index * slots_here + jnp.arange(slots_here, dtype=jnp.int32)
    live = slot_number[None, :] < live_counts[:, None]
    outgoing = jnp.where(live[:, :, None], blocks[picks], jnp.zeros((), jnp.bfloat16))
    big_table = spot_table(SUB)
    received = correlate_slots(
        lax.all_to_all(outgoing, "strip", split_axis=0, concat_axis=0, tiled=True),
        big_table,
        templates,
    )
    return (pupil, received[None])


def solution(mesh):
    placed = (
        P(None, None, "strip", None),
        P("layer", "strip", None),
        P("layer"),
        P(),
        P("strip", None, "layer"),
        P("strip", None),
    )
    return jax.shard_map(
        per_device,
        mesh=mesh,
        in_specs=placed,
        out_specs=(P(None, None, "strip", None), P("strip", None, "layer", None, None)),
        check_vma=False,
    )
```

profile of v0, /device:TPU:1, one launch (start us, length us, event | category | flops | bytes accessed | tf_op | source)
XLA Modules:
  0.0 1428.8 jit_solution(8110256557971793687)
XLA Ops:
  9.3 1338.7 %while.20 = (s32[]{:T(128)}, bf16[2,32,1024]{2,1,0:T(8,128)(2,1)S(1)}, bf16[2,2,32,1024]{3,2,1,0:T(8,128)(2,1)S(1)}, pred[]{:T(512)}, bf16[2,2,32,1024]{3,2,1,0:...) while((s32[]{:T(128)}, ...), condition=%wide.region_1.2_spmd.clone.clone, body=%wide.region_0.1_spmd.clone.clone.sunk | while | flops 1210063872 | bytes 12607868 | solution.py:161
  10.7 16.2 %fusion.176 = f32[1024,2,32]{0,2,1:T(8,128)S(1)} fusion(bf16[1,32,1024]{2,1,0:T(8,128)(2,1)S(1)} %get-tuple-element.469, bf16[1,32,1024]{2,1,0:T(8,128)(2,1)S(1)} %get-tuple-element.470), kind=kOutput, calls=%fused_computation.27.clone.1 | convolution fusion | flops 151060480 | bytes 393216 | tf_op jit(solution)/shard_map/while/body/eval_jaxpr/prj,jk->kpr/dot_general | solution.py:94
  44.1 17.1 %all_to_all.97 = bf16[32,2,1024]{2,1,0:T(2,128)(2,1)S(1)} all-to-all(bf16[32,2,1024]{2,1,0:T(2,128)(2,1)S(1)} %reshape.574), channel_id=1, replica_groups=mesh['layer'=4,'strip'=32] {'strip'}, dimensions={0} | all-to-all | bytes 262144 | tf_op jit(solution)/shard_map/while/body/eval_jaxpr/all_to_all | solution.py:104
  79.0 16.4 %fusion.180 = f32[1,32,2,1024]{3,1,2,0:T(8,128)S(1)} fusion(bf16[32,2,1024]{2,0,1:T(8,128)(2,1)S(1)} %reshape.576), kind=kOutput, calls=%fused_computation.25.clone.1 | convolution fusion | flops 150994944 | bytes 393216 | tf_op jit(solution)/shard_map/while/body/eval_jaxpr/acpj,jk->acpk/dot_general | solution.py:105
  141.8 16.1 %fusion.186 = f32[2,32,1024]{2,1,0:T(8,128)S(1)} fusion(bf16[1024,2,32]{0,2,1:T(8,128)(2,1)S(1)} %reshape.579), kind=kOutput, calls=%fused_computation.16.clone.1 | convolution fusion | flops 150994944 | bytes 393216 | tf_op jit(solution)/shard_map/while/body/eval_jaxpr/kpr,kj->prj/dot_general | solution.py:125
  228.0 16.1 %fusion.179 = f32[1,32,2,1024]{3,1,2,0:T(8,128)S(1)} fusion(bf16[32,2,1024]{2,0,1:T(8,128)(2,1)S(1)} %reshape.576), kind=kOutput, calls=%fused_computation.28.clone.1 | convolution fusion | flops 150994944 | bytes 393216 | tf_op jit(solution)/shard_map/while/body/eval_jaxpr/acpj,jk->acpk/dot_general | solution.py:106
  244.1 16.2 %fusion.180 = f32[1,32,2,1024]{3,1,2,0:T(8,128)S(1)} fusion(bf16[32,2,1024]{2,0,1:T(8,128)(2,1)S(1)} %reshape.576), kind=kOutput, calls=%fused_computation.25.clone.1 | convolution fusion | flops 150994944 | bytes 393216 | tf_op jit(solution)/shard_map/while/body/eval_jaxpr/acpj,jk->acpk/dot_general | solution.py:105
  260.4 16.2 %fusion.182 = f32[1,32,2,1024]{3,1,2,0:T(8,128)S(1)} fusion(bf16[32,1,1024]{2,0,1:T(8,128)(2,1)S(1)} %get-tuple-element.473, bf16[32,1,1024]{2,0,1:T(8,128)(2,1)S(1)} %get-tuple-element.474), kind=kOutput, calls=%fused_computation.29.clone.1 | convolution fusion | flops 151060480 | bytes 393216 | tf_op jit(solution)/shard_map/while/body/eval_jaxpr/acpj,kj->acpk/dot_general | solution.py:114
  394.1 16.1 %fusion.179 = f32[1,32,2,1024]{3,1,2,0:T(8,128)S(1)} fusion(bf16[32,2,1024]{2,0,1:T(8,128)(2,1)S(1)} %reshape.576), kind=kOutput, calls=%fused_computation.28.clone.1 | convolution fusion | flops 150994944 | bytes 393216 | tf_op jit(solution)/shard_map/while/body/eval_jaxpr/acpj,jk->acpk/dot_general | solution.py:106
  410.2 16.1 %fusion.180 = f32[1,32,2,1024]{3,1,2,0:T(8,128)S(1)} fusion(bf16[32,2,1024]{2,0,1:T(8,128)(2,1)S(1)} %reshape.576), kind=kOutput, calls=%fused_computation.25.clone.1 | convolution fusion | flops 150994944 | bytes 393216 | tf_op jit(solution)/shard_map/while/body/eval_jaxpr/acpj,jk->acpk/dot_general | solution.py:105
  512.8 16.2 %fusion.176 = f32[1024,2,32]{0,2,1:T(8,128)S(1)} fusion(bf16[1,32,1024]{2,1,0:T(8,128)(2,1)S(1)} %get-tuple-element.469, bf16[1,32,1024]{2,1,0:T(8,128)(2,1)S(1)} %get-tuple-element.470), kind=kOutput, calls=%fused_computation.27.clone.1 | convolution fusion | flops 151060480 | bytes 393216 | tf_op jit(solution)/shard_map/while/body/eval_jaxpr/prj,jk->kpr/dot_general | solution.py:94
  560.0 16.1 %fusion.179 = f32[1,32,2,1024]{3,1,2,0:T(8,128)S(1)} fusion(bf16[32,2,1024]{2,0,1:T(8,128)(2,1)S(1)} %reshape.576), kind=kOutput, calls=%fused_computation.28.clone.1 | convolution fusion | flops 150994944 | bytes 393216 | tf_op jit(solution)/shard_map/while/body/eval_jaxpr/acpj,jk->acpk/dot_general | solution.py:106
  576.1 16.4 %fusion.180 = f32[1,32,2,1024]{3,1,2,0:T(8,128)S(1)} fusion(bf16[32,2,1024]{2,0,1:T(8,128)(2,1)S(1)} %reshape.576), kind=kOutput, calls=%fused_computation.25.clone.1 | convolution fusion | flops 150994944 | bytes 393216 | tf_op jit(solution)/shard_map/while/body/eval_jaxpr/acpj,jk->acpk/dot_general | solution.py:105
  638.9 16.1 %fusion.186 = f32[2,32,1024]{2,1,0:T(8,128)S(1)} fusion(bf16[1024,2,32]{0,2,1:T(8,128)(2,1)S(1)} %reshape.579), kind=kOutput, calls=%fused_computation.16.clone.1 | convolution fusion | flops 150994944 | bytes 393216 | tf_op jit(solution)/shard_map/while/body/eval_jaxpr/kpr,kj->prj/dot_general | solution.py:125
  742.1 16.2 %fusion.180 = f32[1,32,2,1024]{3,1,2,0:T(8,128)S(1)} fusion(bf16[32,2,1024]{2,0,1:T(8,128)(2,1)S(1)} %reshape.576), kind=kOutput, calls=%fused_computation.25.clone.1 | convolution fusion | flops 150994944 | bytes 393216 | tf_op jit(solution)/shard_map/while/body/eval_jaxpr/acpj,jk->acpk/dot_general | solution.py:105
  758.4 16.2 %fusion.182 = f32[1,32,2,1024]{3,1,2,0:T(8,128)S(1)} fusion(bf16[32,1,1024]{2,0,1:T(8,128)(2,1)S(1)} %get-tuple-element.473, bf16[32,1,1024]{2,0,1:T(8,128)(2,1)S(1)} %get-tuple-element.474), kind=kOutput, calls=%fused_computation.29.clone.1 | convolution fusion | flops 151060480 | bytes 393216 | tf_op jit(solution)/shard_map/while/body/eval_jaxpr/acpj,kj->acpk/dot_general | solution.py:114
  908.2 16.1 %fusion.180 = f32[1,32,2,1024]{3,1,2,0:T(8,128)S(1)} fusion(bf16[32,2,1024]{2,0,1:T(8,128)(2,1)S(1)} %reshape.576), kind=kOutput, calls=%fused_computation.25.clone.1 | convolution fusion | flops 150994944 | bytes 393216 | tf_op jit(solution)/shard_map/while/body/eval_jaxpr/acpj,jk->acpk/dot_general | solution.py:105
  1010.7 16.2 %fusion.176 = f32[1024,2,32]{0,2,1:T(8,128)S(1)} fusion(bf16[1,32,1024]{2,1,0:T(8,128)(2,1)S(1)} %get-tuple-element.469, bf16[1,32,1024]{2,1,0:T(8,128)(2,1)S(1)} %get-tuple-element.470), kind=kOutput, calls=%fused_computation.27.clone.1 | convolution fusion | flops 151060480 | bytes 393216 | tf_op jit(solution)/shard_map/while/body/eval_jaxpr/prj,jk->kpr/dot_general | solution.py:94
  1057.9 16.1 %fusion.179 = f32[1,32,2,1024]{3,1,2,0:T(8,128)S(1)} fusion(bf16[32,2,1024]{2,0,1:T(8,128)(2,1)S(1)} %reshape.576), kind=kOutput, calls=%fused_computation.28.clone.1 | convolution fusion | flops 150994944 | bytes 393216 | tf_op jit(solution)/shard_map/while/body/eval_jaxpr/acpj,jk->acpk/dot_general | solution.py:106
  1074.1 16.4 %fusion.180 = f32[1,32,2,1024]{3,1,2,0:T(8,128)S(1)} fusion(bf16[32,2,1024]{2,0,1:T(8,128)(2,1)S(1)} %reshape.576), kind=kOutput, calls=%fused_computation.25.clone.1 | convolution fusion | flops 150994944 | bytes 393216 | tf_op jit(solution)/shard_map/while/body/eval_jaxpr/acpj,jk->acpk/dot_general | solution.py:105
  1136.9 16.1 %fusion.186 = f32[2,32,1024]{2,1,0:T(8,128)S(1)} fusion(bf16[1024,2,32]{0,2,1:T(8,128)(2,1)S(1)} %reshape.579), kind=kOutput, calls=%fused_computation.16.clone.1 | convolution fusion | flops 150994944 | bytes 393216 | tf_op jit(solution)/shard_map/while/body/eval_jaxpr/kpr,kj->prj/dot_general | solution.py:125
  1240.1 16.2 %fusion.180 = f32[1,32,2,1024]{3,1,2,0:T(8,128)S(1)} fusion(bf16[32,2,1024]{2,0,1:T(8,128)(2,1)S(1)} %reshape.576), kind=kOutput, calls=%fused_computation.25.clone.1 | convolution fusion | flops 150994944 | bytes 393216 | tf_op jit(solution)/shard_map/while/body/eval_jaxpr/acpj,jk->acpk/dot_general | solution.py:105
  1256.3 16.2 %fusion.182 = f32[1,32,2,1024]{3,1,2,0:T(8,128)S(1)} fusion(bf16[32,1,1024]{2,0,1:T(8,128)(2,1)S(1)} %get-tuple-element.473, bf16[32,1,1024]{2,0,1:T(8,128)(2,1)S(1)} %get-tuple-element.474), kind=kOutput, calls=%fused_computation.29.clone.1 | convolution fusion | flops 151060480 | bytes 393216 | tf_op jit(solution)/shard_map/while/body/eval_jaxpr/acpj,kj->acpk/dot_general | solution.py:114
  1348.9 38.7 %all-reduce.2.cloned.1.call-done = bf16[2,2,32,1024]{3,2,1,0:T(8,128)(2,1)} async-done(((bf16[2,2,32,1024]{3,2,1,0:T(8,128)(2,1)}), bf16[2,2,32,1024]{3,2,1,0:T(8,128)(2,1)}) %all-reduce.2.cloned.1.call-update) | async-done | bytes 262160 | tf_op jit(solution)/shard_map/psum | solution.py:19
  (344 shorter events, 1007.2 us)
Async XLA Ops:
  7.2 1413.1 %copy-start = (bf16[1024,16]{0,1:T(8,128)(2,1)S(1)}, bf16[1024,16]{0,1:T(8,128)(2,1)}, u32[]{:S(2)}) copy-start(bf16[1024,16]{0,1:T(8,128)(2,1)} %param.11) | copy-start | bytes 98308
  7.2 1380.5 %all-reduce.2.cloned.1.call-start = ((), (), s32[]{:S(2)}) async-start(), calls=%async_computation.3 | async-start | bytes 524288 | tf_op jit(solution)/shard_map/psum | solution.py:19
  9.3 1339.6 %copy-start.2 = (s32[1,32,1]{1,2,0:T(1,128)S(1)}, s32[1,32,1]{1,2,0:T(1,128)}, u32[]{:S(2)}) copy-start(s32[1,32,1]{1,2,0:T(1,128)} %param.12) | copy-start | bytes 388
  9.3 1339.6 %copy-start.3 = (s32[1,32]{1,0:T(1,128)S(1)}, s32[1,32]{1,0:T(1,128)}, u32[]{:S(2)}) copy-start(s32[1,32]{1,0:T(1,128)} %param.13) | copy-start | bytes 388
  174.0 5.7 collective-permute-start
  338.9 6.6 collective-permute-start
  505.0 6.6 collective-permute-start
  671.1 6.6 collective-permute-start
  836.9 6.6 collective-permute-start
  1003.0 6.6 collective-permute-start
  1169.0 6.6 collective-permute-start
  1334.9 6.6 collective-permute-start
  1394.7 23.6 %all-to-all-start.2 = ((bf16[32,2,512]{2,1,0:T(2,128)(2,1)}), bf16[32,2,512]{2,1,0:T(2,128)(2,1)S(1)}, u32[]{:S(2)}, u32[]{:S(2)}) async-start(bf16[32,2,512]{2,1,0:T(2,128)(2,1)} %reshape.566), calls=%async_computation.2 | async-start | bytes 131072 | tf_op jit(solution)/shard_map/all_to_all | solution.py:176
  1418.7 2.4 copy-start.1
Sparse Core Ops, SparseCore 0:
  1348.9 38.6 all-reduce.1
where the time goes:
time: 1430 us
  matrix products  1030 us (72%)
  blocking collectives  195 us (14%)
  local copies, waits for them, and re-layouts  61.9 us (4%)
  waiting for transfers between devices  57.9 us (4%)
  starting transfers between devices  41.8 us (3%)
  other arithmetic  17.3 us (1%)
  between operations  15.1 us (1%)
    dot_general x8, matrix products, layer_step(): jnp.einsum('acpj,jk->acpk', columns, cosine_table, preferred_element_type...  130 us
    dot_general x8, matrix products, layer_step(): jnp.einsum('acpj,jk->acpk', columns, sine_table, preferred_element_type=j...  129 us
    dot_general x8, matrix products, layer_step(): jnp.einsum('kpr,kj->prj', returned, sine_table, preferred_element_type=jn...  129 us
    dot_general x8, matrix products, layer_step(): jnp.einsum('prj,jk->kpr', screened, sine_table, preferred_element_type=jn...  128 us
    dot_general x8, matrix products, layer_step(): jnp.einsum('acpj,kj->acpk', phased, sine_table, preferred_element_type=jn...  128 us
    dot_general x8, matrix products, layer_step(): jnp.einsum('kpr,kj->prj', returned, cosine_table, preferred_element_type=...  128 us
    dot_general x8, matrix products, layer_step(): jnp.einsum('prj,jk->kpr', screened, cosine_table, preferred_element_type=...  127 us
    dot_general x8, matrix products, layer_step(): jnp.einsum('acpj,kj->acpk', phased, cosine_table, preferred_element_type=...  127 us
  transfers between devices with their start and end apart: 10, of which 9 were waited for; matrix products, arithmetic and copies ran while one was open for 1% of the time, Pallas kernels for 0%

commit v1 on v0

v1 whole, which is shorter than its diff:
```python
import math

import jax
import jax.numpy as jnp
import numpy as np
from jax import lax
from jax.experimental import pallas as pl
from jax.experimental.pallas import tpu as pltpu
from jax.sharding import PartitionSpec as P

N = 1024
Q = 256
SUB = 16
SPOT = 2 * SUB
BF = jnp.bfloat16
F32 = jnp.float32


def bf16(table):
    return np.asarray(table, np.float32).astype(jnp.bfloat16)


def angle_tables():
    n = np.arange(Q)
    turn = 2.0 * np.pi * ((n[:, None] * n[None, :]) % Q) / Q
    cos, sin = np.cos(turn) / 16.0, np.sin(turn) / 16.0
    forward = np.block([[cos, -sin], [sin, cos]])
    inverse = np.block([[cos, sin], [-sin, cos]])
    k1 = np.arange(4)
    tw = 2.0 * np.pi * (k1[:, None] * n[None, :]) / N
    twiddle = np.stack([np.cos(tw), np.sin(tw)])
    index = (n[None, :, None] * (4 * n[None, None, :] + k1[:, None, None])) % N
    full = 2.0 * np.pi * index / N
    turned = np.concatenate([np.cos(full), np.sin(full)], axis=2) / 16.0
    order = (np.arange(SUB)[None, :] * SUB + np.arange(SUB)[:, None]).reshape(-1)
    both = np.concatenate([order, Q + order])
    return {
        "forward": bf16(forward),
        "inverse": bf16(inverse),
        "turned": bf16(turned),
        "twiddle": twiddle.astype(np.float32),
        "inverse_sub": bf16(inverse[:, both]),
        "twiddle_sub": twiddle[:, :, order].astype(np.float32),
    }


def spot_table():
    turn = 2.0 * np.pi * ((np.arange(SPOT)[:, None] * np.arange(SUB)[None, :]) % SPOT) / SPOT
    wave = (np.cos(turn) - 1j * np.sin(turn)) / math.sqrt(SUB)
    kron = wave[:, None, None, :] * wave[None, :, :, None]
    kron = kron.reshape(SPOT * SPOT, SUB * SUB)
    return bf16(np.block([[kron.real, -kron.imag], [kron.imag, kron.real]]))


def sincos(x):
    y = 0.5 * x
    z = y * y
    s = -1.0 / 39916800.0
    for c in (1.0 / 362880.0, -1.0 / 5040.0, 1.0 / 120.0, -1.0 / 6.0, 1.0):
        s = s * z + c
    s = s * y
    c = 1.0 / 479001600.0
    for a in (-1.0 / 3628800.0, 1.0 / 40320.0, -1.0 / 720.0, 1.0 / 24.0, -0.5, 1.0):
        c = c * z + a
    return 1.0 - 2.0 * s * s, 2.0 * s * c


def spectral(shared, layer):
    tail = shared[layer, 32:48, :].astype(F32)
    d = (tail[0:1] + tail[1:2]) + tail[2:3]
    place = lax.broadcasted_iota(jnp.int32, (1, N), 1)
    k = 4 * (place % Q) + place // Q
    m = jnp.where(k < N // 2, k, k - N).astype(F32)
    turns = d * (m * m * (0.5 / (N * N)))
    frac = turns - jnp.floor(turns + 0.5)
    cos, sin = sincos(frac * (2.0 * math.pi))
    return 0.25 * cos, -0.25 * sin


def granules(parts, width):
    parts = list(parts)
    lane = lax.broadcasted_iota(jnp.int32, parts[0].shape, 1) // width
    bit = 1
    while bit < len(parts):
        high = (lane & bit) != 0
        for i in range(len(parts)):
            if i & bit:
                continue
            a, b = parts[i], parts[i | bit]
            parts[i] = jnp.where(high, pltpu.roll(b, width * bit, 1), a)
            parts[i | bit] = jnp.where(high, b, pltpu.roll(a, 128 - width * bit, 1))
        bit *= 2
    return parts


def gathered(block, first, rows):
    columns = []
    for start in range(0, 32, 4):
        parts = [block[start + t, first : first + rows, :].astype(F32) for t in range(4)]
        columns.append(granules(parts, 32))
    return [jnp.concatenate([c[g] for c in columns], axis=1) for g in range(4)]


def quarters(x):
    return [x[:, Q * n : Q * n + Q] for n in range(4)]


def forward(re, im, h, twiddle, table):
    ar, ai = re[0] + re[2], im[0] + im[2]
    br, bi = re[0] - re[2], im[0] - im[2]
    cr, ci = re[1] + re[3], im[1] + im[3]
    dr, di = re[1] - re[3], im[1] - im[3]
    outs = [
        (ar + cr, ai + ci),
        (br + di, bi - dr),
        (ar - cr, ai - ci),
        (br - di, bi + dr),
    ]
    rows = []
    for k1, (r, m) in enumerate(outs):
        if k1:
            c, s = twiddle[0, k1 : k1 + 1, :], twiddle[1, k1 : k1 + 1, :]
            r, m = r * c + m * s, m * c - r * s
        rows.append(jnp.concatenate([r, m], axis=1).astype(BF))
    z = jnp.dot(jnp.concatenate(rows, axis=0), table[...], preferred_element_type=F32)
    spectrum = []
    for k1 in range(4):
        zr, zi = z[64 * k1 : 64 * k1 + 64, :Q], z[64 * k1 : 64 * k1 + 64, Q:]
        hr, hi = h[0][:, Q * k1 : Q * k1 + Q], h[1][:, Q * k1 : Q * k1 + Q]
        spectrum.append(((zr * hr - zi * hi).astype(BF), (zr * hi + zi * hr).astype(BF)))
    return spectrum


def inverse(spectrum, twiddle, table):
    stacked = jnp.concatenate([jnp.concatenate(s, axis=1) for s in spectrum], axis=0)
    y = jnp.dot(stacked, table[...], preferred_element_type=F32)
    outs = []
    for k1 in range(4):
        r, m = y[64 * k1 : 64 * k1 + 64, :Q], y[64 * k1 : 64 * k1 + 64, Q:]
        if k1:
            c, s = twiddle[0, k1 : k1 + 1, :], twiddle[1, k1 : k1 + 1, :]
            r, m = r * c - m * s, m * c + r * s
        outs.append((r, m))
    (r0, i0), (r1, i1), (r2, i2), (r3, i3) = outs
    ar, ai, br, bi = r0 + r2, i0 + i2, r0 - r2, i0 - i2
    cr, ci, dr, di = r1 + r3, i1 + i3, r1 - r3, i1 - i3
    re = [ar + cr, br - di, ar - cr, br + di]
    im = [ai + ci, bi + dr, ai - ci, bi - dr]
    return re, im


def inverse_turned(spectrum, turned, out):
    ys = []
    for k1 in range(4):
        r, m = spectrum[k1]
        rows = jnp.concatenate(
            [jnp.concatenate([r, -m], axis=1), jnp.concatenate([m, r], axis=1)], axis=0
        )
        ys.append(
            lax.dot_general(
                turned[k1], rows, (((1,), (1,)), ((), ())), preferred_element_type=F32
            )
        )
    a, b, c, d = ys[0] + ys[2], ys[0] - ys[2], ys[1] + ys[3], ys[1] - ys[3]
    lane = lax.broadcasted_iota(jnp.int32, d.shape, 1)
    swapped = pltpu.roll(d, 64, 1)
    d = jnp.where(lane < 64, -swapped, swapped)
    for n1, x in enumerate((a + c, b + d, a - c, b - d)):
        out[8 * n1 : 8 * n1 + 8, 0:32, :] = x.astype(BF).reshape(8, 32, 128)


def through_screen(re, im, phase):
    cos, sin = sincos(phase)
    out_re, out_im = [], []
    for n in range(4):
        c, s = cos[:, Q * n : Q * n + Q], sin[:, Q * n : Q * n + Q]
        c, s = jnp.concatenate([c, c], axis=0), jnp.concatenate([s, s], axis=0)
        out_re.append(re[n] * c - im[n] * s)
        out_im.append(re[n] * s + im[n] * c)
    return out_re, out_im


def first_kernel(launch, shared, twiddle, table, turned, out):
    re = quarters(jnp.concatenate([launch[0, 0], launch[1, 0]], axis=0).astype(F32))
    im = quarters(jnp.concatenate([launch[0, 1], launch[1, 1]], axis=0).astype(F32))
    re, im = through_screen(re, im, shared[0, 0:32, :].astype(F32))
    spectrum = forward(re, im, spectral(shared, 0), twiddle, table)
    inverse_turned(spectrum, turned, out)
    both = jnp.concatenate([shared[1, 0:32, :], shared[3, 0:32, :]], axis=0).astype(F32)
    for block in range(8):
        piece = both[:, 128 * block : 128 * block + 128].T.reshape(4, 2, 16, 64)
        out[4 * block : 4 * block + 4, 32:48, :] = jnp.concatenate(
            [piece[:, 0], piece[:, 1]], axis=2
        ).astype(BF)


def halves(groups):
    re = jnp.concatenate([groups[0], groups[1]], axis=0)
    im = jnp.concatenate([groups[2], groups[3]], axis=0)
    return quarters(re), quarters(im)


def column_kernel(layer, came, carried, shared, twiddle, table, back, turned, out):
    groups = gathered(carried, 32, 16)
    which = layer // 2
    phase = jnp.concatenate([groups[which], groups[2 + which]], axis=0)
    re, im = halves(gathered(came, 0, 32))
    spectrum = forward(re, im, spectral(shared, layer), twiddle, table)
    re, im = inverse(spectrum, twiddle, back)
    re, im = through_screen(re, im, phase)
    spectrum = forward(re, im, spectral(shared, layer + 1), twiddle, table)
    inverse_turned(spectrum, turned, out)


def row_kernel(layer, came, shared, twiddle, table, back, turned, out):
    re, im = halves(gathered(came, 0, 32))
    spectrum = forward(re, im, spectral(shared, layer), twiddle, table)
    re, im = inverse(spectrum, twiddle, back)
    re, im = through_screen(re, im, shared[layer + 1, 0:32, :].astype(F32))
    spectrum = forward(re, im, spectral(shared, layer + 1), twiddle, table)
    inverse_turned(spectrum, turned, out)


def last_kernel(
    came, shared, twiddle, table, back, twiddle_sub, back_sub, spots, templates, picks,
    pupil, result, cells,
):
    re, im = halves(gathered(came, 0, 32))
    spectrum = forward(re, im, spectral(shared, 3), twiddle, table)
    re, im = inverse(spectrum, twiddle, back)
    for n in range(4):
        for field in range(2):
            rows = slice(32 * field, 32 * field + 32)
            pupil[field, 0, :, Q * n : Q * n + Q] = re[n][rows].astype(BF)
            pupil[field, 1, :, Q * n : Q * n + Q] = im[n][rows].astype(BF)
    for part, x in enumerate(inverse(spectrum, twiddle_sub, back_sub)):
        for field in range(2):
            for upper in range(2):
                parts = [
                    x[n1][32 * field + 16 * a : 32 * field + 16 * a + 16,
                          128 * upper : 128 * upper + 128]
                    for a in range(2)
                    for n1 in range(4)
                ]
                for k, piece in enumerate(granules(parts, 16)):
                    row = part * 256 + (upper * 8 + k) * 16
                    cells[row : row + 16, 128 * field : 128 * field + 128] = piece.astype(BF)
    total = jnp.zeros((16, 256), F32)
    step = 256
    for start in range(0, 1024, step):
        sre = jnp.dot(spots[start : start + step, :], cells[...], preferred_element_type=F32)
        sim = jnp.dot(
            spots[1024 + start : 1024 + start + step, :], cells[...], preferred_element_type=F32
        )
        intensity = (sre * sre + sim * sim).astype(BF)
        total += jnp.dot(
            templates[:, start : start + step], intensity, preferred_element_type=F32
        )
    lane = lax.broadcasted_iota(jnp.int32, (32, 128), 1)
    chosen = jnp.where(lane == picks[...], 1.0, 0.0).astype(F32)
    for field in range(2):
        result[:, 16 * field : 16 * field + 16] = lax.dot_general(
            chosen,
            total[:, 128 * field : 128 * field + 128],
            (((1,), (1,)), ((), ())),
            precision=lax.Precision.HIGHEST,
            preferred_element_type=F32,
        )


def call(kernel, shapes, *operands, scratch=(), name=None):
    return pl.pallas_call(
        kernel,
        out_shape=shapes,
        scratch_shapes=list(scratch),
        compiler_params=pltpu.CompilerParams(vmem_limit_bytes=48 * 1024 * 1024),
        name=name,
    )(*operands)


def exchanged(block):
    return lax.all_to_all(block, "strip", split_axis=0, concat_axis=0, tiled=True)


def per_device(launch, screens, distance, templates, send_table, send_counts):
    tables = {name: jnp.asarray(value) for name, value in angle_tables().items()}
    twiddle, table = tables["twiddle"], tables["forward"]
    back, turned = tables["inverse"], tables["turned"]

    d = distance.reshape(1, 1)
    high = lax.reduce_precision(d, 8, 7)
    middle = lax.reduce_precision(d - high, 8, 7)
    low = (d - high) - middle
    row = lax.broadcasted_iota(jnp.int32, (16, N), 0)
    tail = jnp.where(row == 0, high, jnp.where(row == 1, middle, jnp.where(row == 2, low, 0.0)))
    mine = jnp.concatenate([screens[0], tail], axis=0).astype(BF)
    shared = lax.all_to_all(
        jnp.broadcast_to(mine[None], (4, 48, N)), "layer", split_axis=0, concat_axis=0, tiled=True
    )

    wide = jax.ShapeDtypeStruct((32, 48, 128), BF)
    plain = jax.ShapeDtypeStruct((32, 32, 128), BF)
    sent = call(first_kernel, wide, launch, shared, twiddle, table, turned, name="rows0")
    carried = exchanged(sent)

    def columns(layer, came, name):
        def kernel(*refs):
            column_kernel(layer, *refs)

        return call(
            kernel, plain, came, carried, shared, twiddle, table, back, turned, name=name
        )

    def rows(layer, came, name):
        def kernel(*refs):
            row_kernel(layer, *refs)

        return call(kernel, plain, came, shared, twiddle, table, back, turned, name=name)

    came = exchanged(columns(0, carried, "columns01"))
    came = exchanged(rows(1, came, "rows12"))
    came = exchanged(columns(2, came, "columns23"))

    slot = lax.axis_index("layer")
    picks = jnp.where(slot < send_counts[0], send_table[0, :, 0], -1).reshape(32, 1)
    pupil, result = call(
        last_kernel,
        (jax.ShapeDtypeStruct(launch.shape, BF), jax.ShapeDtypeStruct((32, 32), F32)),
        came, shared, twiddle, table, back, tables["twiddle_sub"], tables["inverse_sub"],
        jnp.asarray(spot_table()), templates.T, picks,
        scratch=[pltpu.VMEM((512, 256), BF)],
        name="rows3",
    )
    return (pupil, exchanged(result).reshape(1, 32, 1, 2, 16))


def solution(mesh):
    placed = (
        P(None, None, "strip", None),
        P("layer", "strip", None),
        P("layer"),
        P(),
        P("strip", None, "layer"),
        P("strip", None),
    )
    return jax.shard_map(
        per_device,
        mesh=mesh,
        in_specs=placed,
        out_specs=(P(None, None, "strip", None), P("strip", None, "layer", None, None)),
        check_vma=False,
    )
```

time: 1430 us -> 102 us (0.07)
  matrix products: 1030 us -> 0 us
  blocking collectives: 195 us -> 54.8 us
  local copies, waits for them, and re-layouts: 61.9 us -> 5.23 us
  waiting for transfers between devices: 57.9 us -> 17.9 us
  starting transfers between devices: 41.8 us -> 7.43 us
  other arithmetic: 17.3 us -> 2.32 us
    dot_general x66 -> x0, matrix products: 1030 us -> none  [the longest x8 130 us: layer_step(): jnp.einsum('acpj,jk->acpk', columns, cosine_table, preferred_element_type...]
    all_to_all x16 -> x4, blocking collectives: 195 us -> 54.8 us  [the longest x3 42.6 us: exchanged(): lax.all_to_all(block, 'strip', split_axis=0, concat_axis=0, tiled=True)]
    psum x1 -> x0, waiting for transfers between devices: 38.7 us -> none  [broadcast(): return lax.psum(jnp.where(mine, x, jnp.zeros_like(x)), axis)]
    ppermute x8 -> x0, starting transfers between devices: 32 us -> none  [passed_along(): lax.ppermute(value, axis, [(source, source + steps) for source in range(f...]
    another operation x76 -> x0, local copies, waits for them, and re-layouts: 23.5 us -> none
    ppermute x8 -> x0, waiting for transfers between devices: 19.2 us -> none  [passed_along(): lax.ppermute(value, axis, [(source, source + steps) for source in range(f...]
    all_to_all x1 -> x2, waiting for transfers between devices: 0.01 us -> 17.9 us  [exchanged(): lax.all_to_all(block, 'strip', split_axis=0, concat_axis=0, tiled=True)]
  transfers between devices with their start and end apart: 10 -> 2, of which waited for: 9 -> 2; matrix products, arithmetic and copies ran while one was open for 1% -> 0% of each run, Pallas kernels for 0% -> 0%
where the time goes in v1:
time: 102 us; the launch traced here: 101 us
  blocking collectives  54.8 us (54%)
  waiting for transfers between devices  17.9 us (18%)
  Pallas kernels  9.76 us (10%)
  starting transfers between devices  7.43 us (7%)
  local copies, waits for them, and re-layouts  5.23 us (5%)
  between operations  3.86 us (4%)
  other arithmetic  2.32 us (2%)
    all_to_all x3, blocking collectives, exchanged(): lax.all_to_all(block, 'strip', split_axis=0, concat_axis=0, tiled=True)  42.6 us
    all_to_all x2, waiting for transfers between devices, exchanged(): lax.all_to_all(block, 'strip', split_axis=0, concat_axis=0, tiled=True)  17.9 us
    all_to_all x1, blocking collectives, per_device(): lax.all_to_all(jnp.broadcast_to(mine[None], (4, 48, N)), 'layer', split_a...  12.1 us
    pallas_call x5, Pallas kernels, call(): pl.pallas_call(kernel, out_shape=shapes, scratch_shapes=list(scratch), co...  9.76 us
    all_to_all x2, starting transfers between devices, exchanged(): lax.all_to_all(block, 'strip', split_axis=0, concat_axis=0, tiled=True)  7.43 us
    unnamed x24, local copies, waits for them, and re-layouts  4.33 us
  transfers between devices with their start and end apart: 2, of which 2 were waited for; matrix products, arithmetic and copies ran while one was open for 0% of the time, Pallas kernels for 0%

profile of v1, /device:TPU:1, one launch (start us, length us, event | category | flops | bytes accessed | tf_op | source)
XLA Modules:
  0.0 101.3 jit_solution(8368695556448717950)
XLA Ops:
  0.6 0.0 copy-start.1
  0.6 0.0 copy-start
  3.8 0.9 convert_bitcast_fusion
  4.7 1.4 %select_convert_fusion = bf16[16,1024]{1,0:T(8,128)(2,1)S(1)} fusion(bf16[16]{0:T(256)(128)(2,1)S(1)} %compare_select_fusion, f32[]{:T(128)} %bitcast.3, f32[]{:T(128)} %bitcast.2, pred[16]{0:T(512)(128)(4,1)S(1)} %get-tuple-element.8, pred[16]{0:T(512)(128)(4,1)S(1)} %get-tuple-element.9), kind=kLoop, calls=%fused_computation.1 | loop fusion | flops 32768 | bytes 32840 | tf_op jit(solution)/shard_map/convert.1
  6.1 12.1 %all_to_all.34.shared.refs_2_.refs_1_ = bf16[4,48,1024]{2,1,0:T(8,128)(2,1)S(1)} all-to-all(bf16[4,48,1024]{2,1,0:T(8,128)(2,1)S(1)} %broadcast_in_dim.48), channel_id=1, replica_groups=mesh['layer'=4,'strip'=32] {'layer'}, dimensions={0} | all-to-all | bytes 786432 | tf_op jit(solution)/shard_map/all_to_all | solution.py:297
  18.2 0.9 copy-done.5
  19.2 0.7 copy-done.6
  19.9 1.0 rows0.1
  20.9 19.9 %all_to_all.35.refs_0_.refs_1_ = bf16[32,48,128]{2,1,0:T(8,128)(2,1)S(1)} all-to-all(bf16[32,48,128]{2,1,0:T(8,128)(2,1)S(1)} %rows0.1), channel_id=1, replica_groups=mesh['layer'=4,'strip'=32] {'strip'}, dimensions={0} | all-to-all | bytes 786432 | tf_op jit(solution)/shard_map/all_to_all | solution.py:282
  40.8 1.6 %columns01.1 = bf16[32,32,128]{2,1,0:T(8,128)(2,1)S(1)} custom-call(bf16[32,48,128]{2,1,0:T(8,128)(2,1)S(1)} %all_to_all.35.refs_0_.refs_1_, bf16[32,48,128]{2,1,0:T(8,128)(2,1)S(1)} %all_to_all.35.refs_0_.refs_1_, bf16[4,48,1024]{2,1,0:T(8,128)(2,1)S(1)} %all_to_all.34.shared.refs_2_.refs_1_, f32[2,4,256]{2,1,0:T(4,128)S(1)} %copy-done.7, ...), custom_call_target="tpu_custom_call" | custom-call | tf_op jit(solution)/shard_map/columns01/pallas_call | solution.py:272
  42.4 12.3 %all_to_all.36.refs_0_ = bf16[32,32,128]{2,1,0:T(8,128)(2,1)S(1)} all-to-all(bf16[32,32,128]{2,1,0:T(8,128)(2,1)S(1)} %columns01.1), channel_id=1, replica_groups=mesh['layer'=4,'strip'=32] {'strip'}, dimensions={0} | all-to-all | bytes 524288 | tf_op jit(solution)/shard_map/all_to_all | solution.py:282
  54.7 2.3 %rows12.1 = bf16[32,32,128]{2,1,0:T(8,128)(2,1)} custom-call(bf16[32,32,128]{2,1,0:T(8,128)(2,1)S(1)} %all_to_all.36.refs_0_, bf16[4,48,1024]{2,1,0:T(8,128)(2,1)S(1)} %all_to_all.34.shared.refs_2_.refs_1_, f32[2,4,256]{2,1,0:T(4,128)S(1)} %copy-done.7, bf16[512,512]{1,0:T(8,128)(2,1)S(1)} %copy-done.1, bf16[512,512]{1,0:T(8,128)(2,1)S(1)} %copy-done.2, ...), custom_call_target="tpu_custom_call" | custom-call | tf_op jit(solution)/shard_map/rows12/pallas_call | solution.py:272
  57.0 3.7 %all-to-all-start.3 = ((bf16[32,32,128]{2,1,0:T(8,128)(2,1)}), bf16[32,32,128]{2,1,0:T(8,128)(2,1)S(1)}, u32[]{:S(2)}, u32[]{:S(2)}) async-start(bf16[32,32,128]{2,1,0:T(8,128)(2,1)} %rows12.1), calls=%async_computation.3 | async-start | bytes 524288 | tf_op jit(solution)/shard_map/all_to_all | solution.py:282
  60.8 9.0 %all-to-all-done.3.refs_0_ = bf16[32,32,128]{2,1,0:T(8,128)(2,1)S(1)} async-done(((bf16[32,32,128]{2,1,0:T(8,128)(2,1)}), bf16[32,32,128]{2,1,0:T(8,128)(2,1)S(1)}, u32[]{:S(2)}, u32[]{:S(2)}) %all-to-all-start.3) | async-done | bytes 262176 | tf_op jit(solution)/shard_map/all_to_all | solution.py:282
  69.9 2.3 %columns23.1 = bf16[32,32,128]{2,1,0:T(8,128)(2,1)} custom-call(bf16[32,32,128]{2,1,0:T(8,128)(2,1)S(1)} %all-to-all-done.3.refs_0_, bf16[32,48,128]{2,1,0:T(8,128)(2,1)S(1)} %all_to_all.35.refs_0_.refs_1_, bf16[4,48,1024]{2,1,0:T(8,128)(2,1)S(1)} %all_to_all.34.shared.refs_2_.refs_1_, f32[2,4,256]{2,1,0:T(4,128)S(1)} %copy-done.7, ...), custom_call_target="tpu_custom_call" | custom-call | tf_op jit(solution)/shard_map/columns23/pallas_call | solution.py:272
  72.1 3.7 %all-to-all-start.4 = ((bf16[32,32,128]{2,1,0:T(8,128)(2,1)}), bf16[32,32,128]{2,1,0:T(8,128)(2,1)S(1)}, u32[]{:S(2)}, u32[]{:S(2)}) async-start(bf16[32,32,128]{2,1,0:T(8,128)(2,1)} %columns23.1), calls=%async_computation.4 | async-start | bytes 524288 | tf_op jit(solution)/shard_map/all_to_all | solution.py:282
  75.9 0.1 copy.22
  76.0 0.1 copy.21
  76.1 8.9 %all-to-all-done.4.came = bf16[32,32,128]{2,1,0:T(8,128)(2,1)S(1)} async-done(((bf16[32,32,128]{2,1,0:T(8,128)(2,1)}), bf16[32,32,128]{2,1,0:T(8,128)(2,1)S(1)}, u32[]{:S(2)}, u32[]{:S(2)}) %all-to-all-start.4) | async-done | bytes 262176 | tf_op jit(solution)/shard_map/all_to_all | solution.py:282
  84.9 1.6 %copy-done.3 = bf16[2048,512]{1,0:T(8,128)(2,1)S(1)} copy-done((bf16[2048,512]{1,0:T(8,128)(2,1)S(1)}, bf16[2048,512]{1,0:T(8,128)(2,1)}, u32[]{:S(2)}) %copy-start.3) | copy-done | bytes 2097176
  86.5 1.0 %copy-done.4 = bf16[512,512]{1,0:T(8,128)(2,1)S(1)} copy-done((bf16[512,512]{1,0:T(8,128)(2,1)S(1)}, bf16[512,512]{1,0:T(8,128)(2,1)}, u32[]{:S(2)}) %copy-start.4) | copy-done | bytes 524312
  87.6 2.6 %rows3.1 = (bf16[2,2,32,1024]{3,2,1,0:T(8,128)(2,1)}, f32[32,32]{1,0:T(8,128)S(1)}) custom-call(bf16[32,32,128]{2,1,0:T(8,128)(2,1)S(1)} %all-to-all-done.4.came, bf16[4,48,1024]{2,1,0:T(8,128)(2,1)S(1)} %all_to_all.34.shared.refs_2_.refs_1_, f32[2,4,256]{2,1,0:T(4,128)S(1)} %copy-done.7, bf16[512,512]{1,0:T(8,128)(2,1)S(1)} %copy-done.1, ...), custom_call_target="tpu_custom_call" | custom-call | tf_op jit(solution)/shard_map/rows3/pallas_call | solution.py:272
  90.2 10.4 %all_to_all.37 = f32[32,1,32]{2,1,0:T(1,128)S(1)} all-to-all(f32[32,1,32]{2,1,0:T(1,128)S(1)} %bitcast.17), channel_id=1, replica_groups=mesh['layer'=4,'strip'=32] {'strip'}, dimensions={0} | all-to-all | bytes 8192 | tf_op jit(solution)/shard_map/all_to_all | solution.py:282
  100.6 0.7 copy.24
  (24 shorter events, 0.1 us)
Async XLA Ops:
  0.6 17.6 %copy-start.1 = (bf16[512,512]{1,0:T(8,128)(2,1)S(1)}, bf16[512,512]{1,0:T(8,128)(2,1)}, u32[]{:S(2)}) copy-start(bf16[512,512]{1,0:T(8,128)(2,1)} %constant.30.clone.table.refs_4_.refs_3_) | copy-start | bytes 1572868
  0.6 17.6 %copy-start = (bf16[4,256,512]{2,1,0:T(8,128)(2,1)S(1)}, bf16[4,256,512]{2,1,0:T(8,128)(2,1)}, u32[]{:S(2)}) copy-start(bf16[4,256,512]{2,1,0:T(8,128)(2,1)} %constant.32.clone.turned.refs_6_.refs_5_) | copy-start | bytes 3145732
  6.1 34.7 %copy-start.2 = (bf16[512,512]{1,0:T(8,128)(2,1)S(1)}, bf16[512,512]{1,0:T(8,128)(2,1)}, u32[]{:S(2)}) copy-start(bf16[512,512]{1,0:T(8,128)(2,1)} %constant.31.clone.refs_5_.refs_4_.back) | copy-start | bytes 1572868
  18.2 1.0 copy-start.5
  19.2 0.7 copy-start.6
  19.9 20.9 %copy-start.7 = (f32[2,4,256]{2,1,0:T(4,128)S(1)}, f32[2,4,256]{2,1,0:T(4,128)}, u32[]{:S(2)}) copy-start(f32[2,4,256]{2,1,0:T(4,128)} %constant.33.clone.twiddle.refs_3_.refs_2_) | copy-start | bytes 24580
  57.0 12.8 %all-to-all-start.3 = ((bf16[32,32,128]{2,1,0:T(8,128)(2,1)}), bf16[32,32,128]{2,1,0:T(8,128)(2,1)S(1)}, u32[]{:S(2)}, u32[]{:S(2)}) async-start(bf16[32,32,128]{2,1,0:T(8,128)(2,1)} %rows12.1), calls=%async_computation.3 | async-start | bytes 524288 | tf_op jit(solution)/shard_map/all_to_all | solution.py:282
  60.8 15.1 %copy-start.11 = (s32[1,32]{1,0:T(1,128)S(1)}, s32[1,32]{1,0:T(1,128)}, u32[]{:S(2)}) copy-start(s32[1,32]{1,0:T(1,128)} %param.18) | copy-start | bytes 388
  60.8 15.1 %copy-start.10 = (s32[1,32,1]{1,2,0:T(1,128)S(1)}, s32[1,32,1]{1,2,0:T(1,128)}, u32[]{:S(2)}) copy-start(s32[1,32,1]{1,2,0:T(1,128)} %param.17) | copy-start | bytes 388
  60.8 24.2 %copy-start.8 = (bf16[1024,16]{0,1:T(8,128)(2,1)S(1)}, bf16[1024,16]{0,1:T(8,128)(2,1)}, u32[]{:S(2)}) copy-start(bf16[1024,16]{0,1:T(8,128)(2,1)} %param.16) | copy-start | bytes 98308
  60.8 24.1 %copy-start.9 = (f32[2,4,256]{2,1,0:T(4,128)S(1)}, f32[2,4,256]{2,1,0:T(4,128)}, u32[]{:S(2)}) copy-start(f32[2,4,256]{2,1,0:T(4,128)} %constant.35.clone.twiddle_sub) | copy-start | bytes 24580
  72.1 12.8 %all-to-all-start.4 = ((bf16[32,32,128]{2,1,0:T(8,128)(2,1)}), bf16[32,32,128]{2,1,0:T(8,128)(2,1)S(1)}, u32[]{:S(2)}, u32[]{:S(2)}) async-start(bf16[32,32,128]{2,1,0:T(8,128)(2,1)} %columns23.1), calls=%async_computation.4 | async-start | bytes 524288 | tf_op jit(solution)/shard_map/all_to_all | solution.py:282
  84.9 1.6 %copy-start.3 = (bf16[2048,512]{1,0:T(8,128)(2,1)S(1)}, bf16[2048,512]{1,0:T(8,128)(2,1)}, u32[]{:S(2)}) copy-start(bf16[2048,512]{1,0:T(8,128)(2,1)} %constant.36.clone.spots) | copy-start | bytes 6291460
  86.5 1.0 %copy-start.4 = (bf16[512,512]{1,0:T(8,128)(2,1)S(1)}, bf16[512,512]{1,0:T(8,128)(2,1)}, u32[]{:S(2)}) copy-start(bf16[512,512]{1,0:T(8,128)(2,1)} %constant.34.clone.back_sub) | copy-start | bytes 1572868

commit v2 on v1

--- a/solution.py
+++ b/solution.py
@@ -27,8 +27,6 @@
     forward = np.block([[cos, -sin], [sin, cos]])
     inverse = np.block([[cos, sin], [-sin, cos]])
     k1 = np.arange(4)
-    tw = 2.0 * np.pi * (k1[:, None] * n[None, :]) / N
-    twiddle = np.stack([np.cos(tw), np.sin(tw)])
     index = (n[None, :, None] * (4 * n[None, None, :] + k1[:, None, None])) % N
     full = 2.0 * np.pi * index / N
     turned = np.concatenate([np.cos(full), np.sin(full)], axis=2) / 16.0
@@ -38,9 +36,7 @@
         "forward": bf16(forward),
         "inverse": bf16(inverse),
         "turned": bf16(turned),
-        "twiddle": twiddle.astype(np.float32),
         "inverse_sub": bf16(inverse[:, both]),
-        "twiddle_sub": twiddle[:, :, order].astype(np.float32),
     }
 
 
@@ -63,6 +59,16 @@
     for a in (-1.0 / 3628800.0, 1.0 / 40320.0, -1.0 / 720.0, 1.0 / 24.0, -0.5, 1.0):
         c = c * z + a
     return 1.0 - 2.0 * s * s, 2.0 * s * c
+
+
+def twiddles(sub=False):
+    k1 = lax.broadcasted_iota(jnp.int32, (4, Q), 0)
+    n2 = lax.broadcasted_iota(jnp.int32, (4, Q), 1)
+    if sub:
+        n2 = (n2 % SUB) * SUB + n2 // SUB
+    turns = (k1 * n2).astype(F32) * (1.0 / N)
+    turns = jnp.where(turns > 0.5, turns - 1.0, turns)
+    return sincos(turns * (2.0 * math.pi))
 
 
 def spectral(shared, layer):
@@ -119,7 +125,7 @@
     rows = []
     for k1, (r, m) in enumerate(outs):
         if k1:
-            c, s = twiddle[0, k1 : k1 + 1, :], twiddle[1, k1 : k1 + 1, :]
+            c, s = twiddle[0][k1 : k1 + 1, :], twiddle[1][k1 : k1 + 1, :]
             r, m = r * c + m * s, m * c - r * s
         rows.append(jnp.concatenate([r, m], axis=1).astype(BF))
     z = jnp.dot(jnp.concatenate(rows, axis=0), table[...], preferred_element_type=F32)
@@ -138,7 +144,7 @@
     for k1 in range(4):
         r, m = y[64 * k1 : 64 * k1 + 64, :Q], y[64 * k1 : 64 * k1 + 64, Q:]
         if k1:
-            c, s = twiddle[0, k1 : k1 + 1, :], twiddle[1, k1 : k1 + 1, :]
+            c, s = twiddle[0][k1 : k1 + 1, :], twiddle[1][k1 : k1 + 1, :]
             r, m = r * c - m * s, m * c + r * s
         outs.append((r, m))
     (r0, i0), (r1, i1), (r2, i2), (r3, i3) = outs
@@ -180,7 +186,40 @@
     return out_re, out_im
 
 
-def first_kernel(launch, shared, twiddle, table, turned, out):
+def payload_kernel(
+    distance, far_screens, launch, far_targets, far_counts, far_table, far_turned, far_back,
+    shared, held, picks, table, turned, back,
+    screens, targets, counts, sems,
+):
+    copies = [
+        pltpu.make_async_copy(source, target, sems.at[i])
+        for i, (source, target) in enumerate([
+            (far_screens, screens), (far_targets, targets), (far_counts, counts),
+            (launch, held), (far_table, table), (far_turned, turned), (far_back, back),
+        ])
+    ]
+    for copy in copies:
+        copy.start()
+    for copy in copies[:3]:
+        copy.wait()
+    phase = screens[0].astype(BF)
+    d = jnp.full((16, N), distance[0], F32)
+    high = d.astype(BF).astype(F32)
+    middle = (d - high).astype(BF).astype(F32)
+    low = (d - high) - middle
+    row = lax.broadcasted_iota(jnp.int32, (16, N), 0)
+    tail = jnp.where(row == 0, high, jnp.where(row == 1, middle, jnp.where(row == 2, low, 0.0)))
+    tail = tail.astype(BF)
+    for group in range(4):
+        shared[group, 0:32, :] = phase
+        shared[group, 32:48, :] = tail
+    picks[...] = jnp.where(lax.axis_index("layer") < counts[...], targets[...], -1)
+    for copy in copies[3:]:
+        copy.wait()
+
+
+def first_kernel(launch, shared, table, turned, out):
+    twiddle = twiddles()
     re = quarters(jnp.concatenate([launch[0, 0], launch[1, 0]], axis=0).astype(F32))
     im = quarters(jnp.concatenate([launch[0, 1], launch[1, 1]], axis=0).astype(F32))
     re, im = through_screen(re, im, shared[0, 0:32, :].astype(F32))
@@ -200,7 +239,8 @@
     return quarters(re), quarters(im)
 
 
-def column_kernel(layer, came, carried, shared, twiddle, table, back, turned, out):
+def column_kernel(layer, came, carried, shared, table, back, turned, out):
+    twiddle = twiddles()
     groups = gathered(carried, 32, 16)
     which = layer // 2
     phase = jnp.concatenate([groups[which], groups[2 + which]], axis=0)
@@ -212,7 +252,8 @@
     inverse_turned(spectrum, turned, out)
 
 
-def row_kernel(layer, came, shared, twiddle, table, back, turned, out):
+def row_kernel(layer, came, shared, table, back, turned, out):
+    twiddle = twiddles()
     re, im = halves(gathered(came, 0, 32))
     spectrum = forward(re, im, spectral(shared, layer), twiddle, table)
     re, im = inverse(spectrum, twiddle, back)
@@ -222,10 +263,12 @@
 
 
 def last_kernel(
-    came, shared, twiddle, table, back, twiddle_sub, back_sub, spots, templates, picks,
-    pupil, result, cells,
+    came, shared, table, back, back_sub, spots, templates, picks,
+    far_pupil, result,
+    cells, pupil, sem,
 ):
     re, im = halves(gathered(came, 0, 32))
+    twiddle = twiddles()
     spectrum = forward(re, im, spectral(shared, 3), twiddle, table)
     re, im = inverse(spectrum, twiddle, back)
     for n in range(4):
@@ -233,7 +276,9 @@
             rows = slice(32 * field, 32 * field + 32)
             pupil[field, 0, :, Q * n : Q * n + Q] = re[n][rows].astype(BF)
             pupil[field, 1, :, Q * n : Q * n + Q] = im[n][rows].astype(BF)
-    for part, x in enumerate(inverse(spectrum, twiddle_sub, back_sub)):
+    written = pltpu.make_async_copy(pupil, far_pupil, sem)
+    written.start()
+    for part, x in enumerate(inverse(spectrum, twiddles(True), back_sub)):
         for field in range(2):
             for upper in range(2):
                 parts = [
@@ -256,79 +301,103 @@
         total += jnp.dot(
             templates[:, start : start + step], intensity, preferred_element_type=F32
         )
-    lane = lax.broadcasted_iota(jnp.int32, (32, 128), 1)
-    chosen = jnp.where(lane == picks[...], 1.0, 0.0).astype(F32)
+    chosen = jnp.where(lax.broadcasted_iota(jnp.int32, (128, 32), 0) == picks[...], 1.0, 0.0)
     for field in range(2):
         result[:, 16 * field : 16 * field + 16] = lax.dot_general(
-            chosen,
+            chosen.astype(F32),
             total[:, 128 * field : 128 * field + 128],
-            (((1,), (1,)), ((), ())),
+            (((0,), (1,)), ((), ())),
             precision=lax.Precision.HIGHEST,
             preferred_element_type=F32,
         )
-
-
-def call(kernel, shapes, *operands, scratch=(), name=None):
+    written.wait()
+
+
+VMEM = pl.BlockSpec(memory_space=pltpu.VMEM)
+SMEM = pl.BlockSpec(memory_space=pltpu.SMEM)
+FAR = pl.BlockSpec(memory_space=pltpu.HBM)
+
+
+def call(kernel, shapes, *operands, name=None, **specs):
     return pl.pallas_call(
         kernel,
         out_shape=shapes,
-        scratch_shapes=list(scratch),
-        compiler_params=pltpu.CompilerParams(vmem_limit_bytes=48 * 1024 * 1024),
+        compiler_params=pltpu.CompilerParams(vmem_limit_bytes=24 * 1024 * 1024),
         name=name,
+        **specs,
     )(*operands)
 
 
-def exchanged(block):
-    return lax.all_to_all(block, "strip", split_axis=0, concat_axis=0, tiled=True)
+def exchanged(block, axis="strip"):
+    return lax.all_to_all(block, axis, split_axis=0, concat_axis=0, tiled=True)
 
 
 def per_device(launch, screens, distance, templates, send_table, send_counts):
     tables = {name: jnp.asarray(value) for name, value in angle_tables().items()}
-    twiddle, table = tables["twiddle"], tables["forward"]
-    back, turned = tables["inverse"], tables["turned"]
-
-    d = distance.reshape(1, 1)
-    high = lax.reduce_precision(d, 8, 7)
-    middle = lax.reduce_precision(d - high, 8, 7)
-    low = (d - high) - middle
-    row = lax.broadcasted_iota(jnp.int32, (16, N), 0)
-    tail = jnp.where(row == 0, high, jnp.where(row == 1, middle, jnp.where(row == 2, low, 0.0)))
-    mine = jnp.concatenate([screens[0], tail], axis=0).astype(BF)
-    shared = lax.all_to_all(
-        jnp.broadcast_to(mine[None], (4, 48, N)), "layer", split_axis=0, concat_axis=0, tiled=True
+    table, back, turned = tables["forward"], tables["inverse"], tables["turned"]
+
+    payload, held, picks, table, turned, back = call(
+        payload_kernel,
+        (
+            jax.ShapeDtypeStruct((4, 48, N), BF),
+            jax.ShapeDtypeStruct(launch.shape, BF),
+            jax.ShapeDtypeStruct((1, 32), jnp.int32),
+            jax.ShapeDtypeStruct(table.shape, BF),
+            jax.ShapeDtypeStruct(turned.shape, BF),
+            jax.ShapeDtypeStruct(back.shape, BF),
+        ),
+        distance,
+        *[
+            pltpu.with_memory_space_constraint(x, pltpu.HBM)
+            for x in (
+                screens, launch, send_table.reshape(1, 32), send_counts, table, turned, back
+            )
+        ],
+        in_specs=[SMEM] + [FAR] * 7,
+        out_specs=(VMEM,) * 6,
+        scratch_shapes=[
+            pltpu.VMEM(screens.shape, F32),
+            pltpu.VMEM((1, 32), jnp.int32),
+            pltpu.VMEM((1, 32), jnp.int32),
+            pltpu.SemaphoreType.DMA((7,)),
+        ],
+        name="payload",
     )
+    shared = exchanged(payload, "layer")
 
     wide = jax.ShapeDtypeStruct((32, 48, 128), BF)
     plain = jax.ShapeDtypeStruct((32, 32, 128), BF)
-    sent = call(first_kernel, wide, launch, shared, twiddle, table, turned, name="rows0")
+    sent = call(first_kernel, wide, held, shared, table, turned, name="rows0")
     carried = exchanged(sent)
 
     def columns(layer, came, name):
         def kernel(*refs):
             column_kernel(layer, *refs)
 
-        return call(
-            kernel, plain, came, carried, shared, twiddle, table, back, turned, name=name
-        )
+        return call(kernel, plain, came, carried, shared, table, back, turned, name=name)
 
     def rows(layer, came, name):
         def kernel(*refs):
             row_kernel(layer, *refs)
 
-        return call(kernel, plain, came, shared, twiddle, table, back, turned, name=name)
+        return call(kernel, plain, came, shared, table, back, turned, name=name)
 
     came = exchanged(columns(0, carried, "columns01"))
     came = exchanged(rows(1, came, "rows12"))
     came = exchanged(columns(2, came, "columns23"))
 
-    slot = lax.axis_index("layer")
-    picks = jnp.where(slot < send_counts[0], send_table[0, :, 0], -1).reshape(32, 1)
+    spots = jnp.asarray(spot_table())
     pupil, result = call(
         last_kernel,
         (jax.ShapeDtypeStruct(launch.shape, BF), jax.ShapeDtypeStruct((32, 32), F32)),
-        came, shared, twiddle, table, back, tables["twiddle_sub"], tables["inverse_sub"],
-        jnp.asarray(spot_table()), templates.T, picks,
-        scratch=[pltpu.VMEM((512, 256), BF)],
+        came, shared, table, back, tables["inverse_sub"], spots, templates.T, picks,
+        in_specs=[VMEM] * 8,
+        out_specs=(FAR, VMEM),
+        scratch_shapes=[
+            pltpu.VMEM((512, 256), BF),
+            pltpu.VMEM(launch.shape, BF),
+            pltpu.SemaphoreType.DMA,
+        ],
         name="rows3",
     )
     return (pupil, exchanged(result).reshape(1, 32, 1, 2, 16))

time: 102 us -> 92.1 us (0.903)
  blocking collectives: 54.8 us -> 79.5 us
  waiting for transfers between devices: 17.9 us -> 0 us
  starting transfers between devices: 7.43 us -> 0 us
  local copies, waits for them, and re-layouts: 5.23 us -> 0.69 us
  between operations: 3.86 us -> 1.33 us
  other arithmetic: 2.32 us -> 0 us
    all_to_all x4 -> x6, blocking collectives: 54.8 us -> 79.5 us  [exchanged(): return lax.all_to_all(block, axis, split_axis=0, concat_axis=0, tiled=True)]
    all_to_all x2 -> x0, waiting for transfers between devices: 17.9 us -> none  [exchanged(): lax.all_to_all(block, 'strip', split_axis=0, concat_axis=0, tiled=True)]
    all_to_all x2 -> x0, starting transfers between devices: 7.43 us -> none  [exchanged(): lax.all_to_all(block, 'strip', split_axis=0, concat_axis=0, tiled=True)]
    unnamed x24 -> x6, local copies, waits for them, and re-layouts: 4.33 us -> 0.01 us
    another operation x1 -> x0, other arithmetic: 1.37 us -> none
    pallas_call x5 -> x6, Pallas kernels: 9.76 us -> 10.2 us  [call(): pl.pallas_call(kernel, out_shape=shapes, compiler_params=pltpu.CompilerPa...]
  transfers between devices with their start and end apart: 2 -> 0, of which waited for: 2 -> 0; matrix products, arithmetic and copies ran while one was open for 0% -> 0% of each run, Pallas kernels for 0% -> 0%
where the time goes in v2:
time: 92.1 us; the launch traced here: 91.7 us
  blocking collectives  79.5 us (86%)
  Pallas kernels  10.2 us (11%)
  between operations  1.33 us (1%)
    all_to_all x6, blocking collectives, exchanged(): return lax.all_to_all(block, axis, split_axis=0, concat_axis=0, tiled=True)  79.5 us
    pallas_call x6, Pallas kernels, call(): pl.pallas_call(kernel, out_shape=shapes, compiler_params=pltpu.CompilerPa...  10.2 us

profile of v2, /device:TPU:1, one launch (start us, length us, event | category | flops | bytes accessed | tf_op | source)
XLA Modules:
  0.0 91.7 jit_solution(748094116061437048)
XLA Ops:
  1.3 1.8 %payload.1 = (bf16[4,48,1024]{2,1,0:T(8,128)(2,1)S(1)}, bf16[2,2,32,1024]{3,2,1,0:T(8,128)(2,1)S(1)}, s32[1,32]{1,0:T(1,128)S(1)}, bf16[512,512]{1,0:T(8,128)(2,...) custom-call(f32[1]{0:T(128)S(6)} %copy.17.distance, f32[1,32,1024]{2,1,0:T(8,128)} %far_screens.1, ...), custom_call_target="tpu_custom_call" | custom-call | tf_op jit(solution)/shard_map/payload/pallas_call | solution.py:322
  3.0 12.0 %all_to_all.34.shared.refs_2_.refs_1_ = bf16[4,48,1024]{2,1,0:T(8,128)(2,1)S(1)} all-to-all(bf16[4,48,1024]{2,1,0:T(8,128)(2,1)S(1)} %get-tuple-element.11), channel_id=1, replica_groups=mesh['layer'=4,'strip'=32] {'layer'}, dimensions={0} | all-to-all | bytes 786432 | tf_op jit(solution)/shard_map/all_to_all | solution.py:332
  15.0 1.0 %rows0.1 = bf16[32,48,128]{2,1,0:T(8,128)(2,1)S(1)} custom-call(bf16[2,2,32,1024]{3,2,1,0:T(8,128)(2,1)S(1)} %get-tuple-element.10.launch, bf16[4,48,1024]{2,1,0:T(8,128)(2,1)S(1)} %all_to_all.34.shared.refs_2_.refs_1_, bf16[512,512]{1,0:T(8,128)(2,1)S(1)} %get-tuple-element.12.table.refs_3_.refs_2_, ...), custom_call_target="tpu_custom_call" | custom-call | tf_op jit(solution)/shard_map/rows0/pallas_call | solution.py:322
  16.1 19.9 %all_to_all.35.refs_0_.refs_1_ = bf16[32,48,128]{2,1,0:T(8,128)(2,1)S(1)} all-to-all(bf16[32,48,128]{2,1,0:T(8,128)(2,1)S(1)} %rows0.1), channel_id=1, replica_groups=mesh['layer'=4,'strip'=32] {'strip'}, dimensions={0} | all-to-all | bytes 786432 | tf_op jit(solution)/shard_map/all_to_all | solution.py:332
  36.0 1.6 %columns01.1 = bf16[32,32,128]{2,1,0:T(8,128)(2,1)S(1)} custom-call(bf16[32,48,128]{2,1,0:T(8,128)(2,1)S(1)} %all_to_all.35.refs_0_.refs_1_, bf16[32,48,128]{2,1,0:T(8,128)(2,1)S(1)} %all_to_all.35.refs_0_.refs_1_, bf16[4,48,1024]{2,1,0:T(8,128)(2,1)S(1)} %all_to_all.34.shared.refs_2_.refs_1_, bf16[512,512]{1,0:T(8,128)(2,1)S(1)} %get-tuple-element.12.table.refs_3_.refs_2_, ...), custom_call_target="tpu_custom_call" | custom-call | tf_op jit(solution)/shard_map/columns01/pallas_call | solution.py:322
  37.5 12.3 %all_to_all.36.refs_0_ = bf16[32,32,128]{2,1,0:T(8,128)(2,1)S(1)} all-to-all(bf16[32,32,128]{2,1,0:T(8,128)(2,1)S(1)} %columns01.1), channel_id=1, replica_groups=mesh['layer'=4,'strip'=32] {'strip'}, dimensions={0} | all-to-all | bytes 524288 | tf_op jit(solution)/shard_map/all_to_all | solution.py:332
  49.9 1.6 %rows12.1 = bf16[32,32,128]{2,1,0:T(8,128)(2,1)S(1)} custom-call(bf16[32,32,128]{2,1,0:T(8,128)(2,1)S(1)} %all_to_all.36.refs_0_, bf16[4,48,1024]{2,1,0:T(8,128)(2,1)S(1)} %all_to_all.34.shared.refs_2_.refs_1_, bf16[512,512]{1,0:T(8,128)(2,1)S(1)} %get-tuple-element.12.table.refs_3_.refs_2_, bf16[512,512]{1,0:T(8,128)(2,1)S(1)} %get-tuple-element.14.refs_4_.refs_3_.back, ...), custom_call_target="tpu_custom_call" | custom-call | tf_op jit(solution)/shard_map/rows12/pallas_call | solution.py:322
  51.5 12.5 %all_to_all.37.refs_0_ = bf16[32,32,128]{2,1,0:T(8,128)(2,1)S(1)} all-to-all(bf16[32,32,128]{2,1,0:T(8,128)(2,1)S(1)} %rows12.1), channel_id=1, replica_groups=mesh['layer'=4,'strip'=32] {'strip'}, dimensions={0} | all-to-all | bytes 524288 | tf_op jit(solution)/shard_map/all_to_all | solution.py:332
  63.9 0.0 copy-start
  63.9 0.0 copy-start.1
  64.0 0.0 copy-start.2
  64.0 1.6 %columns23.1 = bf16[32,32,128]{2,1,0:T(8,128)(2,1)S(1)} custom-call(bf16[32,32,128]{2,1,0:T(8,128)(2,1)S(1)} %all_to_all.37.refs_0_, bf16[32,48,128]{2,1,0:T(8,128)(2,1)S(1)} %all_to_all.35.refs_0_.refs_1_, bf16[4,48,1024]{2,1,0:T(8,128)(2,1)S(1)} %all_to_all.34.shared.refs_2_.refs_1_, bf16[512,512]{1,0:T(8,128)(2,1)S(1)} %get-tuple-element.12.table.refs_3_.refs_2_, ...), custom_call_target="tpu_custom_call" | custom-call | tf_op jit(solution)/shard_map/columns23/pallas_call | solution.py:322
  65.5 12.5 %all_to_all.38.came = bf16[32,32,128]{2,1,0:T(8,128)(2,1)S(1)} all-to-all(bf16[32,32,128]{2,1,0:T(8,128)(2,1)S(1)} %columns23.1), channel_id=1, replica_groups=mesh['layer'=4,'strip'=32] {'strip'}, dimensions={0} | all-to-all | bytes 524288 | tf_op jit(solution)/shard_map/all_to_all | solution.py:332
  78.0 0.0 copy-done
  78.0 0.0 copy-done.1
  78.0 0.0 copy-done.2
  78.0 2.6 %rows3.1 = (bf16[2,2,32,1024]{3,2,1,0:T(8,128)(2,1)}, f32[32,32]{1,0:T(8,128)S(1)}) custom-call(bf16[32,32,128]{2,1,0:T(8,128)(2,1)S(1)} %all_to_all.38.came, bf16[4,48,1024]{2,1,0:T(8,128)(2,1)S(1)} %all_to_all.34.shared.refs_2_.refs_1_, bf16[512,512]{1,0:T(8,128)(2,1)S(1)} %get-tuple-element.12.table.refs_3_.refs_2_, ...), custom_call_target="tpu_custom_call" | custom-call | tf_op jit(solution)/shard_map/rows3/pallas_call | solution.py:322
  80.6 10.4 %all_to_all.39 = f32[32,1,32]{2,1,0:T(1,128)S(1)} all-to-all(f32[32,1,32]{2,1,0:T(1,128)S(1)} %bitcast.7), channel_id=1, replica_groups=mesh['layer'=4,'strip'=32] {'strip'}, dimensions={0} | all-to-all | bytes 8192 | tf_op jit(solution)/shard_map/all_to_all | solution.py:332
  91.1 0.7 copy.16
Async XLA Ops:
  63.9 14.0 %copy-start = (bf16[2048,512]{1,0:T(8,128)(2,1)S(1)}, bf16[2048,512]{1,0:T(8,128)(2,1)}, u32[]{:S(2)}) copy-start(bf16[2048,512]{1,0:T(8,128)(2,1)} %constant.14.clone.spots) | copy-start | bytes 6291460
  63.9 14.1 %copy-start.1 = (bf16[512,512]{1,0:T(8,128)(2,1)S(1)}, bf16[512,512]{1,0:T(8,128)(2,1)}, u32[]{:S(2)}) copy-start(bf16[512,512]{1,0:T(8,128)(2,1)} %constant.13.clone.back_sub) | copy-start | bytes 1572868
  64.0 14.1 %copy-start.2 = (bf16[1024,16]{0,1:T(8,128)(2,1)S(1)}, bf16[1024,16]{0,1:T(8,128)(2,1)}, u32[]{:S(2)}) copy-start(bf16[1024,16]{0,1:T(8,128)(2,1)} %param.14) | copy-start | bytes 98308

commit v3 on v2

--- a/solution.py
+++ b/solution.py
@@ -72,8 +72,8 @@
 
 
 def spectral(shared, layer):
-    tail = shared[layer, 32:48, :].astype(F32)
-    d = (tail[0:1] + tail[1:2]) + tail[2:3]
+    tail = shared[layer, 0:16, N : N + 128].astype(F32)
+    d = jnp.concatenate([(tail[0:1] + tail[1:2]) + tail[2:3]] * (N // 128), axis=1)
     place = lax.broadcasted_iota(jnp.int32, (1, N), 1)
     k = 4 * (place % Q) + place // Q
     m = jnp.where(k < N // 2, k, k - N).astype(F32)
@@ -99,12 +99,20 @@
     return parts
 
 
-def gathered(block, first, rows):
+def gathered(block, base, first):
     columns = []
-    for start in range(0, 32, 4):
-        parts = [block[start + t, first : first + rows, :].astype(F32) for t in range(4)]
+    for start in range(base, base + 32, 4):
+        parts = [block[start + t, first : first + 16, :].astype(F32) for t in range(4)]
         columns.append(granules(parts, 32))
     return [jnp.concatenate([c[g] for c in columns], axis=1) for g in range(4)]
+
+
+def field_of(block, base=0):
+    groups = gathered(block, base, 0)
+    return (
+        jnp.concatenate([groups[0], groups[2]], axis=0),
+        jnp.concatenate([groups[1], groups[3]], axis=0),
+    )
 
 
 def quarters(x):
@@ -130,8 +138,9 @@
         rows.append(jnp.concatenate([r, m], axis=1).astype(BF))
     z = jnp.dot(jnp.concatenate(rows, axis=0), table[...], preferred_element_type=F32)
     spectrum = []
+    size = re[0].shape[0]
     for k1 in range(4):
-        zr, zi = z[64 * k1 : 64 * k1 + 64, :Q], z[64 * k1 : 64 * k1 + 64, Q:]
+        zr, zi = z[size * k1 : size * k1 + size, :Q], z[size * k1 : size * k1 + size, Q:]
         hr, hi = h[0][:, Q * k1 : Q * k1 + Q], h[1][:, Q * k1 : Q * k1 + Q]
         spectrum.append(((zr * hr - zi * hi).astype(BF), (zr * hi + zi * hr).astype(BF)))
     return spectrum
@@ -141,8 +150,9 @@
     stacked = jnp.concatenate([jnp.concatenate(s, axis=1) for s in spectrum], axis=0)
     y = jnp.dot(stacked, table[...], preferred_element_type=F32)
     outs = []
+    size = spectrum[0][0].shape[0]
     for k1 in range(4):
-        r, m = y[64 * k1 : 64 * k1 + 64, :Q], y[64 * k1 : 64 * k1 + 64, Q:]
+        r, m = y[size * k1 : size * k1 + size, :Q], y[size * k1 : size * k1 + size, Q:]
         if k1:
             c, s = twiddle[0][k1 : k1 + 1, :], twiddle[1][k1 : k1 + 1, :]
             r, m = r * c - m * s, m * c + r * s
@@ -159,30 +169,33 @@
     ys = []
     for k1 in range(4):
         r, m = spectrum[k1]
-        rows = jnp.concatenate(
-            [jnp.concatenate([r, -m], axis=1), jnp.concatenate([m, r], axis=1)], axis=0
-        )
+        pair = [jnp.concatenate([r, -m], axis=1), jnp.concatenate([m, r], axis=1)]
         ys.append(
             lax.dot_general(
-                turned[k1], rows, (((1,), (1,)), ((), ())), preferred_element_type=F32
+                turned[k1],
+                jnp.concatenate(pair + pair, axis=0),
+                (((1,), (1,)), ((), ())),
+                preferred_element_type=F32,
             )
         )
     a, b, c, d = ys[0] + ys[2], ys[0] - ys[2], ys[1] + ys[3], ys[1] - ys[3]
     lane = lax.broadcasted_iota(jnp.int32, d.shape, 1)
-    swapped = pltpu.roll(d, 64, 1)
-    d = jnp.where(lane < 64, -swapped, swapped)
+    swapped = pltpu.roll(d, 32, 1)
+    d = jnp.where((lane // 32) % 2 == 0, -swapped, swapped)
+    low = lax.broadcasted_iota(jnp.int32, (8, 16, 128), 2) < 64
     for n1, x in enumerate((a + c, b + d, a - c, b - d)):
-        out[8 * n1 : 8 * n1 + 8, 0:32, :] = x.astype(BF).reshape(8, 32, 128)
+        x = x.reshape(8, 2, 16, 128)
+        x = jnp.where(low, x[:, 0], x[:, 1]).astype(BF)
+        for base in range(0, out.shape[0], 32):
+            out[base + 8 * n1 : base + 8 * n1 + 8, 0:16, :] = x
 
 
 def through_screen(re, im, phase):
     cos, sin = sincos(phase)
     out_re, out_im = [], []
-    for n in range(4):
-        c, s = cos[:, Q * n : Q * n + Q], sin[:, Q * n : Q * n + Q]
-        c, s = jnp.concatenate([c, c], axis=0), jnp.concatenate([s, s], axis=0)
-        out_re.append(re[n] * c - im[n] * s)
-        out_im.append(re[n] * s + im[n] * c)
+    for r, m, c, s in zip(re, im, quarters(cos), quarters(sin)):
+        out_re.append(r * c - m * s)
+        out_im.append(r * s + m * c)
     return out_re, out_im
 
 
@@ -191,75 +204,70 @@
     shared, held, picks, table, turned, back,
     screens, targets, counts, sems,
 ):
+    group = lax.axis_index("layer")
     copies = [
         pltpu.make_async_copy(source, target, sems.at[i])
         for i, (source, target) in enumerate([
             (far_screens, screens), (far_targets, targets), (far_counts, counts),
-            (launch, held), (far_table, table), (far_turned, turned), (far_back, back),
+            (launch.at[group % 2], held), (far_table, table), (far_turned, turned),
+            (far_back, back),
         ])
     ]
     for copy in copies:
         copy.start()
+    d = jnp.full((32, 128), distance[0], F32)
+    high = d.astype(BF).astype(F32)
+    middle = (d - high).astype(BF).astype(F32)
+    low = (d - high) - middle
+    row = lax.broadcasted_iota(jnp.int32, (32, 128), 0)
+    tail = jnp.where(row == 0, high, jnp.where(row == 1, middle, jnp.where(row == 2, low, 0.0)))
+    tail = tail.astype(BF)
     for copy in copies[:3]:
         copy.wait()
     phase = screens[0].astype(BF)
-    d = jnp.full((16, N), distance[0], F32)
-    high = d.astype(BF).astype(F32)
-    middle = (d - high).astype(BF).astype(F32)
-    low = (d - high) - middle
-    row = lax.broadcasted_iota(jnp.int32, (16, N), 0)
-    tail = jnp.where(row == 0, high, jnp.where(row == 1, middle, jnp.where(row == 2, low, 0.0)))
-    tail = tail.astype(BF)
-    for group in range(4):
-        shared[group, 0:32, :] = phase
-        shared[group, 32:48, :] = tail
-    picks[...] = jnp.where(lax.axis_index("layer") < counts[...], targets[...], -1)
+    for other in range(4):
+        shared[other, :, 0:N] = phase
+        shared[other, :, N : N + 128] = tail
+    picks[...] = jnp.where(group < counts[...], targets[...], -1)
     for copy in copies[3:]:
         copy.wait()
 
 
-def first_kernel(launch, shared, table, turned, out):
+def first_kernel(held, shared, table, turned, out):
     twiddle = twiddles()
-    re = quarters(jnp.concatenate([launch[0, 0], launch[1, 0]], axis=0).astype(F32))
-    im = quarters(jnp.concatenate([launch[0, 1], launch[1, 1]], axis=0).astype(F32))
-    re, im = through_screen(re, im, shared[0, 0:32, :].astype(F32))
+    re, im = quarters(held[0].astype(F32)), quarters(held[1].astype(F32))
+    re, im = through_screen(re, im, shared[0, :, 0:N].astype(F32))
     spectrum = forward(re, im, spectral(shared, 0), twiddle, table)
     inverse_turned(spectrum, turned, out)
-    both = jnp.concatenate([shared[1, 0:32, :], shared[3, 0:32, :]], axis=0).astype(F32)
+    both = jnp.concatenate([shared[1, :, 0:N], shared[3, :, 0:N]], axis=0).astype(F32)
     for block in range(8):
         piece = both[:, 128 * block : 128 * block + 128].T.reshape(4, 2, 16, 64)
-        out[4 * block : 4 * block + 4, 32:48, :] = jnp.concatenate(
+        out[4 * block : 4 * block + 4, 16:32, :] = jnp.concatenate(
             [piece[:, 0], piece[:, 1]], axis=2
         ).astype(BF)
 
 
-def halves(groups):
-    re = jnp.concatenate([groups[0], groups[1]], axis=0)
-    im = jnp.concatenate([groups[2], groups[3]], axis=0)
-    return quarters(re), quarters(im)
-
-
-def column_kernel(layer, came, carried, shared, table, back, turned, out):
+def middle(layer, came, phase, shared, table, back, turned, out):
     twiddle = twiddles()
-    groups = gathered(carried, 32, 16)
-    which = layer // 2
-    phase = jnp.concatenate([groups[which], groups[2 + which]], axis=0)
-    re, im = halves(gathered(came, 0, 32))
-    spectrum = forward(re, im, spectral(shared, layer), twiddle, table)
+    re, im = field_of(came)
+    spectrum = forward(
+        quarters(re), quarters(im), spectral(shared, layer), twiddle, table
+    )
     re, im = inverse(spectrum, twiddle, back)
     re, im = through_screen(re, im, phase)
     spectrum = forward(re, im, spectral(shared, layer + 1), twiddle, table)
     inverse_turned(spectrum, turned, out)
 
 
-def row_kernel(layer, came, shared, table, back, turned, out):
-    twiddle = twiddles()
-    re, im = halves(gathered(came, 0, 32))
-    spectrum = forward(re, im, spectral(shared, layer), twiddle, table)
-    re, im = inverse(spectrum, twiddle, back)
-    re, im = through_screen(re, im, shared[layer + 1, 0:32, :].astype(F32))
-    spectrum = forward(re, im, spectral(shared, layer + 1), twiddle, table)
-    inverse_turned(spectrum, turned, out)
+def column_kernel(layer, came, carried, shared, *rest):
+    groups = gathered(carried, 0, 16)
+    which = layer // 2
+    phase = jnp.concatenate([groups[which], groups[2 + which]], axis=0)
+    middle(layer, came, phase, shared, *rest)
+
+
+def row_kernel(layer, came, shared, *rest):
+    middle(layer, came, shared[layer + 1, :, 0:N].astype(F32), shared, *rest)
 
 
 def last_kernel(
@@ -267,7 +275,8 @@
     far_pupil, result,
     cells, pupil, sem,
 ):
-    re, im = halves(gathered(came, 0, 32))
+    fields = [field_of(came, 0), field_of(came, 32)]
+    re, im = [quarters(jnp.concatenate(x, axis=0)) for x in zip(*fields)]
     twiddle = twiddles()
     spectrum = forward(re, im, spectral(shared, 3), twiddle, table)
     re, im = inverse(spectrum, twiddle, back)
@@ -328,8 +337,10 @@
     )(*operands)
 
 
-def exchanged(block, axis="strip"):
-    return lax.all_to_all(block, axis, split_axis=0, concat_axis=0, tiled=True)
+def exchanged(block, axis="strip", groups=None):
+    return lax.all_to_all(
+        block, axis, split_axis=0, concat_axis=0, tiled=True, axis_index_groups=groups
+    )
 
 
 def per_device(launch, screens, distance, templates, send_table, send_counts):
@@ -339,8 +350,8 @@
     payload, held, picks, table, turned, back = call(
         payload_kernel,
         (
-            jax.ShapeDtypeStruct((4, 48, N), BF),
-            jax.ShapeDtypeStruct(launch.shape, BF),
+            jax.ShapeDtypeStruct((4, 32, N + 128), BF),
+            jax.ShapeDtypeStruct(launch.shape[1:], BF),
             jax.ShapeDtypeStruct((1, 32), jnp.int32),
             jax.ShapeDtypeStruct(table.shape, BF),
             jax.ShapeDtypeStruct(turned.shape, BF),
@@ -365,16 +376,18 @@
     )
     shared = exchanged(payload, "layer")
 
-    wide = jax.ShapeDtypeStruct((32, 48, 128), BF)
-    plain = jax.ShapeDtypeStruct((32, 32, 128), BF)
+    wide = jax.ShapeDtypeStruct((32, 32, 128), BF)
+    plain = jax.ShapeDtypeStruct((32, 16, 128), BF)
+    twice = jax.ShapeDtypeStruct((64, 16, 128), BF)
+    pairs = [[32 * group + strip for group in pair for strip in range(32)] for pair in ((0, 1), (2, 3))]
     sent = call(first_kernel, wide, held, shared, table, turned, name="rows0")
     carried = exchanged(sent)
 
-    def columns(layer, came, name):
+    def columns(layer, came, shape, name):
         def kernel(*refs):
             column_kernel(layer, *refs)
 
-        return call(kernel, plain, came, carried, shared, table, back, turned, name=name)
+        return call(kernel, shape, came, carried, shared, table, back, turned, name=name)
 
     def rows(layer, came, name):
         def kernel(*refs):
@@ -382,9 +395,9 @@
 
         return call(kernel, plain, came, shared, table, back, turned, name=name)
 
-    came = exchanged(columns(0, carried, "columns01"))
+    came = exchanged(columns(0, carried, plain, "columns01"))
     came = exchanged(rows(1, came, "rows12"))
-    came = exchanged(columns(2, came, "columns23"))
+    came = exchanged(columns(2, came, twice, "columns23"), ("layer", "strip"), pairs)
 
     spots = jnp.asarray(spot_table())
     pupil, result = call(

time: 92.1 us -> 88.2 us (0.958)
  blocking collectives: 79.5 us -> 76.4 us
    all_to_all x6, blocking collectives: 79.5 us -> 76.4 us  [exchanged(): lax.all_to_all(block, axis, split_axis=0, concat_axis=0, tiled=True, axis...]
where the time goes in v3:
time: 88.2 us; the launch traced here: 87.8 us
  blocking collectives  76.4 us (87%)
  Pallas kernels  9.37 us (11%)
  between operations  1.35 us (2%)
    all_to_all x6, blocking collectives, exchanged(): lax.all_to_all(block, axis, split_axis=0, concat_axis=0, tiled=True, axis...  76.4 us
    pallas_call x6, Pallas kernels, call(): pl.pallas_call(kernel, out_shape=shapes, compiler_params=pltpu.CompilerPa...  9.37 us

profile of v3, /device:TPU:1, one launch (start us, length us, event | category | flops | bytes accessed | tf_op | source)
XLA Modules:
  0.0 87.8 jit_solution(1913783408465737970)
XLA Ops:
  1.3 1.8 %payload.1 = (bf16[4,32,1152]{2,1,0:T(8,128)(2,1)S(1)}, bf16[2,32,1024]{2,1,0:T(8,128)(2,1)S(1)}, s32[1,32]{1,0:T(1,128)S(1)}, bf16[512,512]{1,0:T(8,128)(2,1)S(...) custom-call(f32[1]{0:T(128)S(6)} %copy.17.distance, f32[1,32,1024]{2,1,0:T(8,128)} %far_screens.1, ...), custom_call_target="tpu_custom_call" | custom-call | tf_op jit(solution)/shard_map/payload/pallas_call | solution.py:331
  3.0 10.6 %all_to_all.34.shared.refs_2_.refs_1_ = bf16[4,32,1152]{2,1,0:T(8,128)(2,1)S(1)} all-to-all(bf16[4,32,1152]{2,1,0:T(8,128)(2,1)S(1)} %get-tuple-element.11), channel_id=1, replica_groups=mesh['layer'=4,'strip'=32] {'layer'}, dimensions={0} | all-to-all | bytes 589824 | tf_op jit(solution)/shard_map/all_to_all | solution.py:341
  13.7 0.9 %rows0.1 = bf16[32,32,128]{2,1,0:T(8,128)(2,1)S(1)} custom-call(bf16[2,32,1024]{2,1,0:T(8,128)(2,1)S(1)} %get-tuple-element.10.held, bf16[4,32,1152]{2,1,0:T(8,128)(2,1)S(1)} %all_to_all.34.shared.refs_2_.refs_1_, bf16[512,512]{1,0:T(8,128)(2,1)S(1)} %get-tuple-element.12.table.refs_3_.refs_2_, bf16[4,256,512]{2,1,0:T(8,128)(2,1)S(1)} %get-tuple-element.13.turned.refs_5_.refs_4_), custom_call_target="tpu_custom_call" | custom-call | tf_op jit(solution)/shard_map/rows0/pallas_call | solution.py:331
  14.6 18.9 %all_to_all.35.refs_0_.refs_1_ = bf16[32,32,128]{2,1,0:T(8,128)(2,1)S(1)} all-to-all(bf16[32,32,128]{2,1,0:T(8,128)(2,1)S(1)} %rows0.1), channel_id=1, replica_groups=mesh['layer'=4,'strip'=32] {'strip'}, dimensions={0} | all-to-all | bytes 524288 | tf_op jit(solution)/shard_map/all_to_all | solution.py:341
  33.5 1.3 %columns01.1 = bf16[32,16,128]{2,1,0:T(8,128)(2,1)S(1)} custom-call(bf16[32,32,128]{2,1,0:T(8,128)(2,1)S(1)} %all_to_all.35.refs_0_.refs_1_, bf16[32,32,128]{2,1,0:T(8,128)(2,1)S(1)} %all_to_all.35.refs_0_.refs_1_, bf16[4,32,1152]{2,1,0:T(8,128)(2,1)S(1)} %all_to_all.34.shared.refs_2_.refs_1_, bf16[512,512]{1,0:T(8,128)(2,1)S(1)} %get-tuple-element.12.table.refs_3_.refs_2_, ...), custom_call_target="tpu_custom_call" | custom-call | tf_op jit(solution)/shard_map/columns01/pallas_call | solution.py:331
  34.8 11.2 %all_to_all.36.refs_0_ = bf16[32,16,128]{2,1,0:T(8,128)(2,1)S(1)} all-to-all(bf16[32,16,128]{2,1,0:T(8,128)(2,1)S(1)} %columns01.1), channel_id=1, replica_groups=mesh['layer'=4,'strip'=32] {'strip'}, dimensions={0} | all-to-all | bytes 262144 | tf_op jit(solution)/shard_map/all_to_all | solution.py:341
  46.0 1.4 %rows12.1 = bf16[32,16,128]{2,1,0:T(8,128)(2,1)S(1)} custom-call(bf16[32,16,128]{2,1,0:T(8,128)(2,1)S(1)} %all_to_all.36.refs_0_, bf16[4,32,1152]{2,1,0:T(8,128)(2,1)S(1)} %all_to_all.34.shared.refs_2_.refs_1_, bf16[512,512]{1,0:T(8,128)(2,1)S(1)} %get-tuple-element.12.table.refs_3_.refs_2_, bf16[512,512]{1,0:T(8,128)(2,1)S(1)} %get-tuple-element.14.refs_4_.refs_3_.back, ...), custom_call_target="tpu_custom_call" | custom-call | tf_op jit(solution)/shard_map/rows12/pallas_call | solution.py:331
  47.4 0.0 copy-start
  47.4 0.0 copy-start.1
  47.4 0.0 copy-start.2
  47.4 11.4 %all_to_all.37.refs_0_ = bf16[32,16,128]{2,1,0:T(8,128)(2,1)S(1)} all-to-all(bf16[32,16,128]{2,1,0:T(8,128)(2,1)S(1)} %rows12.1), channel_id=1, replica_groups=mesh['layer'=4,'strip'=32] {'strip'}, dimensions={0} | all-to-all | bytes 262144 | tf_op jit(solution)/shard_map/all_to_all | solution.py:341
  58.8 1.3 %columns23.1 = bf16[64,16,128]{2,1,0:T(8,128)(2,1)S(1)} custom-call(bf16[32,16,128]{2,1,0:T(8,128)(2,1)S(1)} %all_to_all.37.refs_0_, bf16[32,32,128]{2,1,0:T(8,128)(2,1)S(1)} %all_to_all.35.refs_0_.refs_1_, bf16[4,32,1152]{2,1,0:T(8,128)(2,1)S(1)} %all_to_all.34.shared.refs_2_.refs_1_, bf16[512,512]{1,0:T(8,128)(2,1)S(1)} %get-tuple-element.12.table.refs_3_.refs_2_, ...), custom_call_target="tpu_custom_call" | custom-call | tf_op jit(solution)/shard_map/columns23/pallas_call | solution.py:331
  60.2 13.4 %all_to_all.38.came = bf16[64,16,128]{2,1,0:T(8,128)(2,1)S(1)} all-to-all(bf16[64,16,128]{2,1,0:T(8,128)(2,1)S(1)} %columns23.1), channel_id=1, replica_groups={{0,1,2,3,4,5,6,7,8,9,10,11,12,13,14,15,16,17,18,19,20,21,22,23,24,25,26..., dimensions={0} | all-to-all | bytes 524288 | tf_op jit(solution)/shard_map/all_to_all | solution.py:341
  73.6 0.0 copy-done
  73.6 0.0 copy-done.1
  73.6 0.0 copy-done.2
  73.6 2.6 %rows3.1 = (bf16[2,2,32,1024]{3,2,1,0:T(8,128)(2,1)}, f32[32,32]{1,0:T(8,128)S(1)}) custom-call(bf16[64,16,128]{2,1,0:T(8,128)(2,1)S(1)} %all_to_all.38.came, bf16[4,32,1152]{2,1,0:T(8,128)(2,1)S(1)} %all_to_all.34.shared.refs_2_.refs_1_, bf16[512,512]{1,0:T(8,128)(2,1)S(1)} %get-tuple-element.12.table.refs_3_.refs_2_, ...), custom_call_target="tpu_custom_call" | custom-call | tf_op jit(solution)/shard_map/rows3/pallas_call | solution.py:331
  76.3 10.9 %all_to_all.39 = f32[32,1,32]{2,1,0:T(1,128)S(1)} all-to-all(f32[32,1,32]{2,1,0:T(1,128)S(1)} %bitcast.7), channel_id=1, replica_groups=mesh['layer'=4,'strip'=32] {'strip'}, dimensions={0} | all-to-all | bytes 8192 | tf_op jit(solution)/shard_map/all_to_all | solution.py:341
  87.1 0.7 copy.16
Async XLA Ops:
  47.4 26.2 %copy-start = (bf16[2048,512]{1,0:T(8,128)(2,1)S(1)}, bf16[2048,512]{1,0:T(8,128)(2,1)}, u32[]{:S(2)}) copy-start(bf16[2048,512]{1,0:T(8,128)(2,1)} %constant.14.clone.spots) | copy-start | bytes 6291460
  47.4 26.2 %copy-start.1 = (bf16[512,512]{1,0:T(8,128)(2,1)S(1)}, bf16[512,512]{1,0:T(8,128)(2,1)}, u32[]{:S(2)}) copy-start(bf16[512,512]{1,0:T(8,128)(2,1)} %constant.13.clone.back_sub) | copy-start | bytes 1572868
  47.4 26.2 %copy-start.2 = (bf16[1024,16]{0,1:T(8,128)(2,1)S(1)}, bf16[1024,16]{0,1:T(8,128)(2,1)}, u32[]{:S(2)}) copy-start(bf16[1024,16]{0,1:T(8,128)(2,1)} %param.14) | copy-start | bytes 98308

commit v4 on v3

--- a/solution.py
+++ b/solution.py
@@ -20,24 +20,23 @@
     return np.asarray(table, np.float32).astype(jnp.bfloat16)
 
 
+ORDERS = {
+    "plain": lambda at: at,
+    "send": lambda at: (at % 128) // 16 * 32 + at // 128 * 16 + at % 16,
+    "sub": lambda at: at % SUB * SUB + at // SUB,
+}
+
+
 def angle_tables():
     n = np.arange(Q)
     turn = 2.0 * np.pi * ((n[:, None] * n[None, :]) % Q) / Q
     cos, sin = np.cos(turn) / 16.0, np.sin(turn) / 16.0
     forward = np.block([[cos, -sin], [sin, cos]])
     inverse = np.block([[cos, sin], [-sin, cos]])
-    k1 = np.arange(4)
-    index = (n[None, :, None] * (4 * n[None, None, :] + k1[:, None, None])) % N
-    full = 2.0 * np.pi * index / N
-    turned = np.concatenate([np.cos(full), np.sin(full)], axis=2) / 16.0
-    order = (np.arange(SUB)[None, :] * SUB + np.arange(SUB)[:, None]).reshape(-1)
-    both = np.concatenate([order, Q + order])
-    return {
-        "forward": bf16(forward),
-        "inverse": bf16(inverse),
-        "turned": bf16(turned),
-        "inverse_sub": bf16(inverse[:, both]),
-    }
+    tables = {"forward": bf16(forward)}
+    for name, order in ORDERS.items():
+        tables[name] = bf16(inverse[:, np.concatenate([order(n), Q + order(n)])])
+    return tables
 
 
 def spot_table():
@@ -61,26 +60,33 @@
     return 1.0 - 2.0 * s * s, 2.0 * s * c
 
 
-def twiddles(sub=False):
+def twiddles(out):
     k1 = lax.broadcasted_iota(jnp.int32, (4, Q), 0)
-    n2 = lax.broadcasted_iota(jnp.int32, (4, Q), 1)
-    if sub:
-        n2 = (n2 % SUB) * SUB + n2 // SUB
-    turns = (k1 * n2).astype(F32) * (1.0 / N)
-    turns = jnp.where(turns > 0.5, turns - 1.0, turns)
-    return sincos(turns * (2.0 * math.pi))
-
-
-def spectral(shared, layer):
-    tail = shared[layer, 0:16, N : N + 128].astype(F32)
-    d = jnp.concatenate([(tail[0:1] + tail[1:2]) + tail[2:3]] * (N // 128), axis=1)
-    place = lax.broadcasted_iota(jnp.int32, (1, N), 1)
+    at = lax.broadcasted_iota(jnp.int32, (4, Q), 1)
+    for i, order in enumerate(ORDERS.values()):
+        turns = (k1 * order(at)).astype(F32) * (1.0 / N)
+        turns = jnp.where(turns > 0.5, turns - 1.0, turns)
+        out[8 * i : 8 * i + 4, :], out[8 * i + 4 : 8 * i + 8, :] = sincos(turns * (2.0 * math.pi))
+
+
+def spectra(shared, out):
+    d = []
+    for layer in range(4):
+        tail = shared[layer, 0:16, N : N + 128].astype(F32)
+        d.append((tail[0:1] + tail[1:2]) + tail[2:3])
+    d = jnp.concatenate([jnp.concatenate(d, axis=0)] * (N // 128), axis=1)
+    place = lax.broadcasted_iota(jnp.int32, (4, N), 1)
     k = 4 * (place % Q) + place // Q
     m = jnp.where(k < N // 2, k, k - N).astype(F32)
     turns = d * (m * m * (0.5 / (N * N)))
     frac = turns - jnp.floor(turns + 0.5)
     cos, sin = sincos(frac * (2.0 * math.pi))
-    return 0.25 * cos, -0.25 * sin
+    out[0:4, :], out[4:8, :] = 0.25 * cos, -0.25 * sin
+
+
+def twisted(twiddle, order, k1):
+    row = 8 * list(ORDERS).index(order) + k1
+    return twiddle[row : row + 1, :], twiddle[row + 4 : row + 5, :]
 
 
 def granules(parts, width):
@@ -119,7 +125,7 @@
     return [x[:, Q * n : Q * n + Q] for n in range(4)]
 
 
-def forward(re, im, h, twiddle, table):
+def forward(re, im, layer, spectrum_rows, twiddle, table):
     ar, ai = re[0] + re[2], im[0] + im[2]
     br, bi = re[0] - re[2], im[0] - im[2]
     cr, ci = re[1] + re[3], im[1] + im[3]
@@ -133,7 +139,7 @@
     rows = []
     for k1, (r, m) in enumerate(outs):
         if k1:
-            c, s = twiddle[0][k1 : k1 + 1, :], twiddle[1][k1 : k1 + 1, :]
+            c, s = twisted(twiddle, "plain", k1)
             r, m = r * c + m * s, m * c - r * s
         rows.append(jnp.concatenate([r, m], axis=1).astype(BF))
     z = jnp.dot(jnp.concatenate(rows, axis=0), table[...], preferred_element_type=F32)
@@ -141,12 +147,13 @@
     size = re[0].shape[0]
     for k1 in range(4):
         zr, zi = z[size * k1 : size * k1 + size, :Q], z[size * k1 : size * k1 + size, Q:]
-        hr, hi = h[0][:, Q * k1 : Q * k1 + Q], h[1][:, Q * k1 : Q * k1 + Q]
+        hr = spectrum_rows[layer : layer + 1, Q * k1 : Q * k1 + Q]
+        hi = spectrum_rows[layer + 4 : layer + 5, Q * k1 : Q * k1 + Q]
         spectrum.append(((zr * hr - zi * hi).astype(BF), (zr * hi + zi * hr).astype(BF)))
     return spectrum
 
 
-def inverse(spectrum, twiddle, table):
+def inverse(spectrum, order, twiddle, table):
     stacked = jnp.concatenate([jnp.concatenate(s, axis=1) for s in spectrum], axis=0)
     y = jnp.dot(stacked, table[...], preferred_element_type=F32)
     outs = []
@@ -154,7 +161,7 @@
     for k1 in range(4):
         r, m = y[size * k1 : size * k1 + size, :Q], y[size * k1 : size * k1 + size, Q:]
         if k1:
-            c, s = twiddle[0][k1 : k1 + 1, :], twiddle[1][k1 : k1 + 1, :]
+            c, s = twisted(twiddle, order, k1)
             r, m = r * c - m * s, m * c + r * s
         outs.append((r, m))
     (r0, i0), (r1, i1), (r2, i2), (r3, i3) = outs
@@ -165,27 +172,10 @@
     return re, im
 
 
-def inverse_turned(spectrum, turned, out):
-    ys = []
-    for k1 in range(4):
-        r, m = spectrum[k1]
-        pair = [jnp.concatenate([r, -m], axis=1), jnp.concatenate([m, r], axis=1)]
-        ys.append(
-            lax.dot_general(
-                turned[k1],
-                jnp.concatenate(pair + pair, axis=0),
-                (((1,), (1,)), ((), ())),
-                preferred_element_type=F32,
-            )
-        )
-    a, b, c, d = ys[0] + ys[2], ys[0] - ys[2], ys[1] + ys[3], ys[1] - ys[3]
-    lane = lax.broadcasted_iota(jnp.int32, d.shape, 1)
-    swapped = pltpu.roll(d, 32, 1)
-    d = jnp.where((lane // 32) % 2 == 0, -swapped, swapped)
-    low = lax.broadcasted_iota(jnp.int32, (8, 16, 128), 2) < 64
-    for n1, x in enumerate((a + c, b + d, a - c, b - d)):
-        x = x.reshape(8, 2, 16, 128)
-        x = jnp.where(low, x[:, 0], x[:, 1]).astype(BF)
+def sent(spectrum, twiddle, table, out):
+    for n1, (r, m) in enumerate(zip(*inverse(spectrum, "send", twiddle, table))):
+        x = jnp.concatenate([r[:, :128], m[:, :128], r[:, 128:], m[:, 128:]], axis=0)
+        x = x.T.astype(BF).reshape(8, 16, 128)
         for base in range(0, out.shape[0], 32):
             out[base + 8 * n1 : base + 8 * n1 + 8, 0:16, :] = x
 
@@ -200,8 +190,8 @@
 
 
 def payload_kernel(
-    distance, far_screens, launch, far_targets, far_counts, far_table, far_turned, far_back,
-    shared, held, picks, table, turned, back,
+    distance, far_screens, launch, far_targets, far_counts, far_table, far_send, far_back,
+    shared, held, picks, table, send, back, twiddle,
     screens, targets, counts, sems,
 ):
     group = lax.axis_index("layer")
@@ -209,7 +199,7 @@
         pltpu.make_async_copy(source, target, sems.at[i])
         for i, (source, target) in enumerate([
             (far_screens, screens), (far_targets, targets), (far_counts, counts),
-            (launch.at[group % 2], held), (far_table, table), (far_turned, turned),
+            (launch.at[group % 2], held), (far_table, table), (far_send, send),
             (far_back, back),
         ])
     ]
@@ -222,6 +212,7 @@
     row = lax.broadcasted_iota(jnp.int32, (32, 128), 0)
     tail = jnp.where(row == 0, high, jnp.where(row == 1, middle, jnp.where(row == 2, low, 0.0)))
     tail = tail.astype(BF)
+    twiddles(twiddle)
     for copy in copies[:3]:
         copy.wait()
     phase = screens[0].astype(BF)
@@ -233,12 +224,11 @@
         copy.wait()
 
 
-def first_kernel(held, shared, table, turned, out):
-    twiddle = twiddles()
+def first_kernel(held, shared, twiddle, table, send, out, h):
+    spectra(shared, h)
     re, im = quarters(held[0].astype(F32)), quarters(held[1].astype(F32))
     re, im = through_screen(re, im, shared[0, :, 0:N].astype(F32))
-    spectrum = forward(re, im, spectral(shared, 0), twiddle, table)
-    inverse_turned(spectrum, turned, out)
+    sent(forward(re, im, 0, h, twiddle, table), twiddle, send, out)
     both = jnp.concatenate([shared[1, :, 0:N], shared[3, :, 0:N]], axis=0).astype(F32)
     for block in range(8):
         piece = both[:, 128 * block : 128 * block + 128].T.reshape(4, 2, 16, 64)
@@ -247,39 +237,34 @@
         ).astype(BF)
 
 
-def middle(layer, came, phase, shared, table, back, turned, out):
-    twiddle = twiddles()
+def middle(layer, came, phase, h, twiddle, table, back, send, out):
     re, im = field_of(came)
-    spectrum = forward(
-        quarters(re), quarters(im), spectral(shared, layer), twiddle, table
-    )
-    re, im = inverse(spectrum, twiddle, back)
+    spectrum = forward(quarters(re), quarters(im), layer, h, twiddle, table)
+    re, im = inverse(spectrum, "plain", twiddle, back)
     re, im = through_screen(re, im, phase)
-    spectrum = forward(re, im, spectral(shared, layer + 1), twiddle, table)
-    inverse_turned(spectrum, turned, out)
-
-
-def column_kernel(layer, came, carried, shared, *rest):
+    sent(forward(re, im, layer + 1, h, twiddle, table), twiddle, send, out)
+
+
+def column_kernel(layer, came, carried, *rest):
     groups = gathered(carried, 0, 16)
     which = layer // 2
     phase = jnp.concatenate([groups[which], groups[2 + which]], axis=0)
-    middle(layer, came, phase, shared, *rest)
+    middle(layer, came, phase, *rest)
 
 
 def row_kernel(layer, came, shared, *rest):
-    middle(layer, came, shared[layer + 1, :, 0:N].astype(F32), shared, *rest)
+    middle(layer, came, shared[layer + 1, :, 0:N].astype(F32), *rest)
 
 
 def last_kernel(
-    came, shared, table, back, back_sub, spots, templates, picks,
+    came, h, twiddle, table, back, back_sub, spots, templates, picks,
     far_pupil, result,
     cells, pupil, sem,
 ):
     fields = [field_of(came, 0), field_of(came, 32)]
     re, im = [quarters(jnp.concatenate(x, axis=0)) for x in zip(*fields)]
-    twiddle = twiddles()
-    spectrum = forward(re, im, spectral(shared, 3), twiddle, table)
-    re, im = inverse(spectrum, twiddle, back)
+    spectrum = forward(re, im, 3, h, twiddle, table)
+    re, im = inverse(spectrum, "plain", twiddle, back)
     for n in range(4):
         for field in range(2):
             rows = slice(32 * field, 32 * field + 32)
@@ -287,7 +272,7 @@
             pupil[field, 1, :, Q * n : Q * n + Q] = im[n][rows].astype(BF)
     written = pltpu.make_async_copy(pupil, far_pupil, sem)
     written.start()
-    for part, x in enumerate(inverse(spectrum, twiddles(True), back_sub)):
+    for part, x in enumerate(inverse(spectrum, "sub", twiddle, back_sub)):
         for field in range(2):
             for upper in range(2):
                 parts = [
@@ -345,27 +330,28 @@
 
 def per_device(launch, screens, distance, templates, send_table, send_counts):
     tables = {name: jnp.asarray(value) for name, value in angle_tables().items()}
-    table, back, turned = tables["forward"], tables["inverse"], tables["turned"]
-
-    payload, held, picks, table, turned, back = call(
+    table, back, send = tables["forward"], tables["plain"], tables["send"]
+
+    payload, held, picks, table, send, back, twiddle = call(
         payload_kernel,
         (
             jax.ShapeDtypeStruct((4, 32, N + 128), BF),
             jax.ShapeDtypeStruct(launch.shape[1:], BF),
             jax.ShapeDtypeStruct((1, 32), jnp.int32),
             jax.ShapeDtypeStruct(table.shape, BF),
-            jax.ShapeDtypeStruct(turned.shape, BF),
+            jax.ShapeDtypeStruct(send.shape, BF),
             jax.ShapeDtypeStruct(back.shape, BF),
+            jax.ShapeDtypeStruct((24, Q), F32),
         ),
         distance,
         *[
             pltpu.with_memory_space_constraint(x, pltpu.HBM)
             for x in (
-                screens, launch, send_table.reshape(1, 32), send_counts, table, turned, back
+                screens, launch, send_table.reshape(1, 32), send_counts, table, send, back
             )
         ],
         in_specs=[SMEM] + [FAR] * 7,
-        out_specs=(VMEM,) * 6,
+        out_specs=(VMEM,) * 7,
         scratch_shapes=[
             pltpu.VMEM(screens.shape, F32),
             pltpu.VMEM((1, 32), jnp.int32),
@@ -380,20 +366,23 @@
     plain = jax.ShapeDtypeStruct((32, 16, 128), BF)
     twice = jax.ShapeDtypeStruct((64, 16, 128), BF)
     pairs = [[32 * group + strip for group in pair for strip in range(32)] for pair in ((0, 1), (2, 3))]
-    sent = call(first_kernel, wide, held, shared, table, turned, name="rows0")
-    carried = exchanged(sent)
+    leaving, h = call(
+        first_kernel, (wide, jax.ShapeDtypeStruct((8, N), F32)),
+        held, shared, twiddle, table, send, name="rows0",
+    )
+    carried = exchanged(leaving)
 
     def columns(layer, came, shape, name):
         def kernel(*refs):
             column_kernel(layer, *refs)
 
-        return call(kernel, shape, came, carried, shared, table, back, turned, name=name)
+        return call(kernel, shape, came, carried, h, twiddle, table, back, send, name=name)
 
     def rows(layer, came, name):
         def kernel(*refs):
             row_kernel(layer, *refs)
 
-        return call(kernel, plain, came, shared, table, back, turned, name=name)
+        return call(kernel, plain, came, shared, h, twiddle, table, back, send, name=name)
 
     came = exchanged(columns(0, carried, plain, "columns01"))
     came = exchanged(rows(1, came, "rows12"))
@@ -403,8 +392,8 @@
     pupil, result = call(
         last_kernel,
         (jax.ShapeDtypeStruct(launch.shape, BF), jax.ShapeDtypeStruct((32, 32), F32)),
-        came, shared, table, back, tables["inverse_sub"], spots, templates.T, picks,
-        in_specs=[VMEM] * 8,
+        came, h, twiddle, table, back, tables["sub"], spots, templates.T, picks,
+        in_specs=[VMEM] * 9,
         out_specs=(FAR, VMEM),
         scratch_shapes=[
             pltpu.VMEM((512, 256), BF),

time: 88.2 us -> 87 us (0.986)
  Pallas kernels: 9.37 us -> 8.42 us
    pallas_call x6, Pallas kernels: 9.37 us -> 8.42 us  [call(): pl.pallas_call(kernel, out_shape=shapes, compiler_params=pltpu.CompilerPa...]
where the time goes in v4:
time: 87 us; the launch traced here: 86.7 us
  blocking collectives  76.2 us (88%)
  Pallas kernels  8.42 us (10%)
  between operations  1.32 us (2%)
    all_to_all x6, blocking collectives, exchanged(): lax.all_to_all(block, axis, split_axis=0, concat_axis=0, tiled=True, axis...  76.2 us
    pallas_call x6, Pallas kernels, call(): pl.pallas_call(kernel, out_shape=shapes, compiler_params=pltpu.CompilerPa...  8.42 us

profile of v4, /device:TPU:1, one launch (start us, length us, event | category | flops | bytes accessed | tf_op | source)
XLA Modules:
  0.0 86.7 jit_solution(18421742933775884768)
XLA Ops:
  1.3 1.6 %payload.1 = (bf16[4,32,1152]{2,1,0:T(8,128)(2,1)S(1)}, bf16[2,32,1024]{2,1,0:T(8,128)(2,1)S(1)}, s32[1,32]{1,0:T(1,128)S(1)}, bf16[512,512]{1,0:T(8,128)(2,1)S(...) custom-call(f32[1]{0:T(128)S(6)} %copy.17.distance, ...), custom_call_target="tpu_custom_call" | custom-call | tf_op jit(solution)/shard_map/payload/pallas_call | solution.py:316
  2.9 10.6 %all_to_all.34.shared.refs_1_ = bf16[4,32,1152]{2,1,0:T(8,128)(2,1)S(1)} all-to-all(bf16[4,32,1152]{2,1,0:T(8,128)(2,1)S(1)} %get-tuple-element.14), channel_id=1, replica_groups=mesh['layer'=4,'strip'=32] {'layer'}, dimensions={0} | all-to-all | bytes 589824 | tf_op jit(solution)/shard_map/all_to_all | solution.py:326
  13.5 0.8 rows0.1
  14.3 18.9 %all_to_all.35.refs_0_.refs_1_ = bf16[32,32,128]{2,1,0:T(8,128)(2,1)S(1)} all-to-all(bf16[32,32,128]{2,1,0:T(8,128)(2,1)S(1)} %get-tuple-element.18), channel_id=1, replica_groups=mesh['layer'=4,'strip'=32] {'strip'}, dimensions={0} | all-to-all | bytes 524288 | tf_op jit(solution)/shard_map/all_to_all | solution.py:326
  33.1 1.1 %columns01.1 = bf16[32,16,128]{2,1,0:T(8,128)(2,1)S(1)} custom-call(bf16[32,32,128]{2,1,0:T(8,128)(2,1)S(1)} %all_to_all.35.refs_0_.refs_1_, bf16[32,32,128]{2,1,0:T(8,128)(2,1)S(1)} %all_to_all.35.refs_0_.refs_1_, f32[8,1024]{1,0:T(8,128)S(1)} %get-tuple-element.19.refs_2_.h, f32[24,256]{1,0:T(8,128)S(1)} %get-tuple-element.15.twiddle.refs_3_, ...), custom_call_target="tpu_custom_call" | custom-call | tf_op jit(solution)/shard_map/columns01/pallas_call | solution.py:316
  34.3 11.2 %all_to_all.36.refs_0_ = bf16[32,16,128]{2,1,0:T(8,128)(2,1)S(1)} all-to-all(bf16[32,16,128]{2,1,0:T(8,128)(2,1)S(1)} %columns01.1), channel_id=1, replica_groups=mesh['layer'=4,'strip'=32] {'strip'}, dimensions={0} | all-to-all | bytes 262144 | tf_op jit(solution)/shard_map/all_to_all | solution.py:326
  45.4 0.0 copy-start
  45.4 0.0 copy-start.1
  45.4 0.0 copy-start.2
  45.4 1.2 %rows12.1 = bf16[32,16,128]{2,1,0:T(8,128)(2,1)S(1)} custom-call(bf16[32,16,128]{2,1,0:T(8,128)(2,1)S(1)} %all_to_all.36.refs_0_, bf16[4,32,1152]{2,1,0:T(8,128)(2,1)S(1)} %all_to_all.34.shared.refs_1_, f32[8,1024]{1,0:T(8,128)S(1)} %get-tuple-element.19.refs_2_.h, f32[24,256]{1,0:T(8,128)S(1)} %get-tuple-element.15.twiddle.refs_3_, ...), custom_call_target="tpu_custom_call" | custom-call | tf_op jit(solution)/shard_map/rows12/pallas_call | solution.py:316
  46.6 11.3 %all_to_all.37.refs_0_ = bf16[32,16,128]{2,1,0:T(8,128)(2,1)S(1)} all-to-all(bf16[32,16,128]{2,1,0:T(8,128)(2,1)S(1)} %rows12.1), channel_id=1, replica_groups=mesh['layer'=4,'strip'=32] {'strip'}, dimensions={0} | all-to-all | bytes 262144 | tf_op jit(solution)/shard_map/all_to_all | solution.py:326
  57.9 1.1 %columns23.1 = bf16[64,16,128]{2,1,0:T(8,128)(2,1)S(1)} custom-call(bf16[32,16,128]{2,1,0:T(8,128)(2,1)S(1)} %all_to_all.37.refs_0_, bf16[32,32,128]{2,1,0:T(8,128)(2,1)S(1)} %all_to_all.35.refs_0_.refs_1_, f32[8,1024]{1,0:T(8,128)S(1)} %get-tuple-element.19.refs_2_.h, f32[24,256]{1,0:T(8,128)S(1)} %get-tuple-element.15.twiddle.refs_3_, ...), custom_call_target="tpu_custom_call" | custom-call | tf_op jit(solution)/shard_map/columns23/pallas_call | solution.py:316
  59.0 13.4 %all_to_all.38.came = bf16[64,16,128]{2,1,0:T(8,128)(2,1)S(1)} all-to-all(bf16[64,16,128]{2,1,0:T(8,128)(2,1)S(1)} %columns23.1), channel_id=1, replica_groups={{0,1,2,3,4,5,6,7,8,9,10,11,12,13,14,15,16,17,18,19,20,21,22,23,24,25,26..., dimensions={0} | all-to-all | bytes 524288 | tf_op jit(solution)/shard_map/all_to_all | solution.py:326
  72.5 0.0 copy-done
  72.5 0.0 copy-done.1
  72.5 0.0 copy-done.2
  72.5 2.6 %rows3.1 = (bf16[2,2,32,1024]{3,2,1,0:T(8,128)(2,1)}, f32[32,32]{1,0:T(8,128)S(1)}) custom-call(bf16[64,16,128]{2,1,0:T(8,128)(2,1)S(1)} %all_to_all.38.came, f32[8,1024]{1,0:T(8,128)S(1)} %get-tuple-element.19.refs_2_.h, f32[24,256]{1,0:T(8,128)S(1)} %get-tuple-element.15.twiddle.refs_3_, bf16[512,512]{1,0:T(8,128)(2,1)S(1)} %get-tuple-element.16.table.refs_4_, ...), custom_call_target="tpu_custom_call" | custom-call | tf_op jit(solution)/shard_map/rows3/pallas_call | solution.py:316
  75.1 10.9 %all_to_all.39 = f32[32,1,32]{2,1,0:T(1,128)S(1)} all-to-all(f32[32,1,32]{2,1,0:T(1,128)S(1)} %bitcast.7), channel_id=1, replica_groups=mesh['layer'=4,'strip'=32] {'strip'}, dimensions={0} | all-to-all | bytes 8192 | tf_op jit(solution)/shard_map/all_to_all | solution.py:326
  86.0 0.7 copy.16
Async XLA Ops:
  45.4 27.1 %copy-start = (bf16[2048,512]{1,0:T(8,128)(2,1)S(1)}, bf16[2048,512]{1,0:T(8,128)(2,1)}, u32[]{:S(2)}) copy-start(bf16[2048,512]{1,0:T(8,128)(2,1)} %constant.14.clone.spots) | copy-start | bytes 6291460
  45.4 27.1 %copy-start.1 = (bf16[512,512]{1,0:T(8,128)(2,1)S(1)}, bf16[512,512]{1,0:T(8,128)(2,1)}, u32[]{:S(2)}) copy-start(bf16[512,512]{1,0:T(8,128)(2,1)} %constant.13.clone.back_sub) | copy-start | bytes 1572868
  45.4 27.1 %copy-start.2 = (bf16[1024,16]{0,1:T(8,128)(2,1)S(1)}, bf16[1024,16]{0,1:T(8,128)(2,1)}, u32[]{:S(2)}) copy-start(bf16[1024,16]{0,1:T(8,128)(2,1)} %param.14) | copy-start | bytes 98308

commit v5 on v4

--- a/solution.py
+++ b/solution.py
@@ -44,7 +44,7 @@
     wave = (np.cos(turn) - 1j * np.sin(turn)) / math.sqrt(SUB)
     kron = wave[:, None, None, :] * wave[None, :, :, None]
     kron = kron.reshape(SPOT * SPOT, SUB * SUB)
-    return bf16(np.block([[kron.real, -kron.imag], [kron.imag, kron.real]]))
+    return bf16(np.block([[kron.real, -kron.imag], [kron.imag, kron.real]]).T)
 
 
 def sincos(x):
@@ -108,9 +108,9 @@
 def gathered(block, base, first):
     columns = []
     for start in range(base, base + 32, 4):
-        parts = [block[start + t, first : first + 16, :].astype(F32) for t in range(4)]
+        parts = [block[start + t, first : first + 16, :] for t in range(4)]
         columns.append(granules(parts, 32))
-    return [jnp.concatenate([c[g] for c in columns], axis=1) for g in range(4)]
+    return [jnp.concatenate([c[g] for c in columns], axis=1).astype(F32) for g in range(4)]
 
 
 def field_of(block, base=0):
@@ -190,8 +190,8 @@
 
 
 def payload_kernel(
-    distance, far_screens, launch, far_targets, far_counts, far_table, far_send, far_back,
-    shared, held, picks, table, send, back, twiddle,
+    distance, far_screens, launch, far_targets, far_counts, far_table,
+    shared, held, picks, table, twiddle,
     screens, targets, counts, sems,
 ):
     group = lax.axis_index("layer")
@@ -199,8 +199,7 @@
         pltpu.make_async_copy(source, target, sems.at[i])
         for i, (source, target) in enumerate([
             (far_screens, screens), (far_targets, targets), (far_counts, counts),
-            (launch.at[group % 2], held), (far_table, table), (far_send, send),
-            (far_back, back),
+            (launch.at[group % 2], held), (far_table, table),
         ])
     ]
     for copy in copies:
@@ -224,11 +223,15 @@
         copy.wait()
 
 
-def first_kernel(held, shared, twiddle, table, send, out, h):
+def first_kernel(held, shared, twiddle, table, far_send, out, h, send, sem):
+    copy = pltpu.make_async_copy(far_send, send, sem)
+    copy.start()
     spectra(shared, h)
     re, im = quarters(held[0].astype(F32)), quarters(held[1].astype(F32))
     re, im = through_screen(re, im, shared[0, :, 0:N].astype(F32))
-    sent(forward(re, im, 0, h, twiddle, table), twiddle, send, out)
+    spectrum = forward(re, im, 0, h, twiddle, table)
+    copy.wait()
+    sent(spectrum, twiddle, send, out)
     both = jnp.concatenate([shared[1, :, 0:N], shared[3, :, 0:N]], axis=0).astype(F32)
     for block in range(8):
         piece = both[:, 128 * block : 128 * block + 128].T.reshape(4, 2, 16, 64)
@@ -264,6 +267,18 @@
     fields = [field_of(came, 0), field_of(came, 32)]
     re, im = [quarters(jnp.concatenate(x, axis=0)) for x in zip(*fields)]
     spectrum = forward(re, im, 3, h, twiddle, table)
+    for part, x in enumerate(inverse(spectrum, "sub", twiddle, back_sub)):
+        for field in range(2):
+            for upper in range(2):
+                parts = [
+                    x[n1][32 * field + 16 * a : 32 * field + 16 * a + 16,
+                          128 * upper : 128 * upper + 128].astype(BF)
+                    for a in range(2)
+                    for n1 in range(4)
+                ]
+                for k, piece in enumerate(granules(parts, 16)):
+                    row = part * 256 + (upper * 8 + k) * 16
+                    cells[row : row + 16, 128 * field : 128 * field + 128] = piece
     re, im = inverse(spectrum, "plain", twiddle, back)
     for n in range(4):
         for field in range(2):
@@ -272,38 +287,24 @@
             pupil[field, 1, :, Q * n : Q * n + Q] = im[n][rows].astype(BF)
     written = pltpu.make_async_copy(pupil, far_pupil, sem)
     written.start()
-    for part, x in enumerate(inverse(spectrum, "sub", twiddle, back_sub)):
-        for field in range(2):
-            for upper in range(2):
-                parts = [
-                    x[n1][32 * field + 16 * a : 32 * field + 16 * a + 16,
-                          128 * upper : 128 * upper + 128]
-                    for a in range(2)
-                    for n1 in range(4)
-                ]
-                for k, piece in enumerate(granules(parts, 16)):
-                    row = part * 256 + (upper * 8 + k) * 16
-                    cells[row : row + 16, 128 * field : 128 * field + 128] = piece.astype(BF)
-    total = jnp.zeros((16, 256), F32)
-    step = 256
-    for start in range(0, 1024, step):
-        sre = jnp.dot(spots[start : start + step, :], cells[...], preferred_element_type=F32)
-        sim = jnp.dot(
-            spots[1024 + start : 1024 + start + step, :], cells[...], preferred_element_type=F32
-        )
-        intensity = (sre * sre + sim * sim).astype(BF)
-        total += jnp.dot(
-            templates[:, start : start + step], intensity, preferred_element_type=F32
-        )
-    chosen = jnp.where(lax.broadcasted_iota(jnp.int32, (128, 32), 0) == picks[...], 1.0, 0.0)
+    place = lax.broadcasted_iota(jnp.int32, (128, 32), 0)
+    chosen = jnp.where(place == picks[...], 1.0, 0.0).astype(F32).T.astype(BF)
+    slots = [
+        lax.dot_general(
+            chosen,
+            cells[:, 128 * field : 128 * field + 128],
+            (((1,), (1,)), ((), ())),
+            preferred_element_type=F32,
+        ).astype(BF)
+        for field in range(2)
+    ]
+    spot = jnp.dot(jnp.concatenate(slots, axis=0), spots[...], preferred_element_type=F32)
+    intensity = (spot[:, :1024] * spot[:, :1024] + spot[:, 1024:] * spot[:, 1024:]).astype(BF)
+    total = lax.dot_general(
+        intensity, templates[...], (((1,), (1,)), ((), ())), preferred_element_type=F32
+    )
     for field in range(2):
-        result[:, 16 * field : 16 * field + 16] = lax.dot_general(
-            chosen.astype(F32),
-            total[:, 128 * field : 128 * field + 128],
-            (((0,), (1,)), ((), ())),
-            precision=lax.Precision.HIGHEST,
-            preferred_element_type=F32,
-        )
+        result[:, 16 * field : 16 * field + 16] = total[32 * field : 32 * field + 32]
     written.wait()
 
 
@@ -332,31 +333,29 @@
     tables = {name: jnp.asarray(value) for name, value in angle_tables().items()}
     table, back, send = tables["forward"], tables["plain"], tables["send"]
 
-    payload, held, picks, table, send, back, twiddle = call(
+    payload, held, picks, table, twiddle = call(
         payload_kernel,
         (
             jax.ShapeDtypeStruct((4, 32, N + 128), BF),
             jax.ShapeDtypeStruct(launch.shape[1:], BF),
             jax.ShapeDtypeStruct((1, 32), jnp.int32),
             jax.ShapeDtypeStruct(table.shape, BF),
-            jax.ShapeDtypeStruct(send.shape, BF),
-            jax.ShapeDtypeStruct(back.shape, BF),
             jax.ShapeDtypeStruct((24, Q), F32),
         ),
         distance,
         *[
             pltpu.with_memory_space_constraint(x, pltpu.HBM)
             for x in (
-                screens, launch, send_table.reshape(1, 32), send_counts, table, send, back
+                screens, launch, send_table.reshape(1, 32), send_counts, table
             )
         ],
-        in_specs=[SMEM] + [FAR] * 7,
-        out_specs=(VMEM,) * 7,
+        in_specs=[SMEM] + [FAR] * 5,
+        out_specs=(VMEM,) * 5,
         scratch_shapes=[
             pltpu.VMEM(screens.shape, F32),
             pltpu.VMEM((1, 32), jnp.int32),
             pltpu.VMEM((1, 32), jnp.int32),
-            pltpu.SemaphoreType.DMA((7,)),
+            pltpu.SemaphoreType.DMA((5,)),
         ],
         name="payload",
     )
@@ -366,9 +365,14 @@
     plain = jax.ShapeDtypeStruct((32, 16, 128), BF)
     twice = jax.ShapeDtypeStruct((64, 16, 128), BF)
     pairs = [[32 * group + strip for group in pair for strip in range(32)] for pair in ((0, 1), (2, 3))]
-    leaving, h = call(
-        first_kernel, (wide, jax.ShapeDtypeStruct((8, N), F32)),
-        held, shared, twiddle, table, send, name="rows0",
+    leaving, h, send = call(
+        first_kernel,
+        (wide, jax.ShapeDtypeStruct((8, N), F32), jax.ShapeDtypeStruct(send.shape, BF)),
+        held, shared, twiddle, table, pltpu.with_memory_space_constraint(send, pltpu.HBM),
+        in_specs=[VMEM] * 4 + [FAR],
+        out_specs=(VMEM,) * 3,
+        scratch_shapes=[pltpu.SemaphoreType.DMA],
+        name="rows0",
     )
     carried = exchanged(leaving)
 

time: 87 us -> 86.9 us (level)
  no operation moved by 1% of the time
where the time goes in v5:
time: 86.9 us; the launch traced here: 86.4 us
  blocking collectives  76.3 us (88%)
  Pallas kernels  8.09 us (9%)
  between operations  1.4 us (2%)
    all_to_all x6, blocking collectives, exchanged(): lax.all_to_all(block, axis, split_axis=0, concat_axis=0, tiled=True, axis...  76.3 us
    pallas_call x6, Pallas kernels, call(): pl.pallas_call(kernel, out_shape=shapes, compiler_params=pltpu.CompilerPa...  8.09 us

profile of v5, /device:TPU:1, one launch (start us, length us, event | category | flops | bytes accessed | tf_op | source)
XLA Modules:
  0.0 86.4 jit_solution(14497718620242290684)
XLA Ops:
  0.6 0.0 copy-start
  1.3 1.3 %payload.1 = (bf16[4,32,1152]{2,1,0:T(8,128)(2,1)S(1)}, bf16[2,32,1024]{2,1,0:T(8,128)(2,1)S(1)}, s32[1,32]{1,0:T(1,128)S(1)}, bf16[512,512]{1,0:T(8,128)(2,1)S(1)}, f32[24,256]{1,0:T(8,128)S(1)}) custom-call(f32[1]{0:T(128)S(6)} %copy.17.distance, f32[1,32,1024]{2,1,0:T(8,128)} %far_screens.1, bf16[2,2,32,1024]{3,2,1,0:T(8,128)(2,1)} %launch.1, ...), custom_call_target="tpu_custom_call" | custom-call | tf_op jit(solution)/shard_map/payload/pallas_call | solution.py:317
  2.6 10.6 %all_to_all.34.shared.refs_1_ = bf16[4,32,1152]{2,1,0:T(8,128)(2,1)S(1)} all-to-all(bf16[4,32,1152]{2,1,0:T(8,128)(2,1)S(1)} %get-tuple-element.13), channel_id=1, replica_groups=mesh['layer'=4,'strip'=32] {'layer'}, dimensions={0} | all-to-all | bytes 589824 | tf_op jit(solution)/shard_map/all_to_all | solution.py:327
  13.2 1.5 %rows0.1 = (bf16[32,32,128]{2,1,0:T(8,128)(2,1)S(1)}, f32[8,1024]{1,0:T(8,128)S(1)}, bf16[512,512]{1,0:T(8,128)(2,1)S(1)}) custom-call(bf16[2,32,1024]{2,1,0:T(8,128)(2,1)S(1)} %get-tuple-element.12.held, bf16[4,32,1152]{2,1,0:T(8,128)(2,1)S(1)} %all_to_all.34.shared.refs_1_, f32[24,256]{1,0:T(8,128)S(1)} %get-tuple-element.14.twiddle.refs_3_, ...), custom_call_target="tpu_custom_call" | custom-call | tf_op jit(solution)/shard_map/rows0/pallas_call | solution.py:317
  14.8 18.9 %all_to_all.35.refs_0_.refs_1_ = bf16[32,32,128]{2,1,0:T(8,128)(2,1)S(1)} all-to-all(bf16[32,32,128]{2,1,0:T(8,128)(2,1)S(1)} %get-tuple-element.16), channel_id=1, replica_groups=mesh['layer'=4,'strip'=32] {'strip'}, dimensions={0} | all-to-all | bytes 524288 | tf_op jit(solution)/shard_map/all_to_all | solution.py:327
  33.6 0.0 copy-done
  33.6 1.1 %columns01.1 = bf16[32,16,128]{2,1,0:T(8,128)(2,1)S(1)} custom-call(bf16[32,32,128]{2,1,0:T(8,128)(2,1)S(1)} %all_to_all.35.refs_0_.refs_1_, bf16[32,32,128]{2,1,0:T(8,128)(2,1)S(1)} %all_to_all.35.refs_0_.refs_1_, f32[8,1024]{1,0:T(8,128)S(1)} %get-tuple-element.17.refs_2_.h, f32[24,256]{1,0:T(8,128)S(1)} %get-tuple-element.14.twiddle.refs_3_, ...), custom_call_target="tpu_custom_call" | custom-call | tf_op jit(solution)/shard_map/columns01/pallas_call | solution.py:317
  34.7 11.2 %all_to_all.36.refs_0_ = bf16[32,16,128]{2,1,0:T(8,128)(2,1)S(1)} all-to-all(bf16[32,16,128]{2,1,0:T(8,128)(2,1)S(1)} %columns01.1), channel_id=1, replica_groups=mesh['layer'=4,'strip'=32] {'strip'}, dimensions={0} | all-to-all | bytes 262144 | tf_op jit(solution)/shard_map/all_to_all | solution.py:327
  45.9 0.0 copy-start.1
  45.9 0.0 copy-start.2
  45.9 0.0 copy-start.3
  45.9 1.2 %rows12.1 = bf16[32,16,128]{2,1,0:T(8,128)(2,1)S(1)} custom-call(bf16[32,16,128]{2,1,0:T(8,128)(2,1)S(1)} %all_to_all.36.refs_0_, bf16[4,32,1152]{2,1,0:T(8,128)(2,1)S(1)} %all_to_all.34.shared.refs_1_, f32[8,1024]{1,0:T(8,128)S(1)} %get-tuple-element.17.refs_2_.h, f32[24,256]{1,0:T(8,128)S(1)} %get-tuple-element.14.twiddle.refs_3_, ...), custom_call_target="tpu_custom_call" | custom-call | tf_op jit(solution)/shard_map/rows12/pallas_call | solution.py:317
  47.1 11.3 %all_to_all.37.refs_0_ = bf16[32,16,128]{2,1,0:T(8,128)(2,1)S(1)} all-to-all(bf16[32,16,128]{2,1,0:T(8,128)(2,1)S(1)} %rows12.1), channel_id=1, replica_groups=mesh['layer'=4,'strip'=32] {'strip'}, dimensions={0} | all-to-all | bytes 262144 | tf_op jit(solution)/shard_map/all_to_all | solution.py:327
  58.4 1.1 %columns23.1 = bf16[64,16,128]{2,1,0:T(8,128)(2,1)S(1)} custom-call(bf16[32,16,128]{2,1,0:T(8,128)(2,1)S(1)} %all_to_all.37.refs_0_, bf16[32,32,128]{2,1,0:T(8,128)(2,1)S(1)} %all_to_all.35.refs_0_.refs_1_, f32[8,1024]{1,0:T(8,128)S(1)} %get-tuple-element.17.refs_2_.h, f32[24,256]{1,0:T(8,128)S(1)} %get-tuple-element.14.twiddle.refs_3_, ...), custom_call_target="tpu_custom_call" | custom-call | tf_op jit(solution)/shard_map/columns23/pallas_call | solution.py:317
  59.6 13.4 %all_to_all.38.came = bf16[64,16,128]{2,1,0:T(8,128)(2,1)S(1)} all-to-all(bf16[64,16,128]{2,1,0:T(8,128)(2,1)S(1)} %columns23.1), channel_id=1, replica_groups={{0,1,2,3,4,5,6,7,8,9,10,11,12,13,14,15,16,17,18,19,20,21,22,23,24,25,26..., dimensions={0} | all-to-all | bytes 524288 | tf_op jit(solution)/shard_map/all_to_all | solution.py:327
  73.0 0.0 copy-done.1
  73.0 0.0 copy-done.2
  73.0 0.0 copy-done.3
  73.0 1.9 %rows3.1 = (bf16[2,2,32,1024]{3,2,1,0:T(8,128)(2,1)}, f32[32,32]{1,0:T(8,128)S(1)}) custom-call(bf16[64,16,128]{2,1,0:T(8,128)(2,1)S(1)} %all_to_all.38.came, f32[8,1024]{1,0:T(8,128)S(1)} %get-tuple-element.17.refs_2_.h, f32[24,256]{1,0:T(8,128)S(1)} %get-tuple-element.14.twiddle.refs_3_, bf16[512,512]{1,0:T(8,128)(2,1)S(1)} %get-tuple-element.15.table.refs_4_, ...), custom_call_target="tpu_custom_call" | custom-call | tf_op jit(solution)/shard_map/rows3/pallas_call | solution.py:317
  74.9 10.9 %all_to_all.39 = f32[32,1,32]{2,1,0:T(1,128)S(1)} all-to-all(f32[32,1,32]{2,1,0:T(1,128)S(1)} %bitcast.7), channel_id=1, replica_groups=mesh['layer'=4,'strip'=32] {'strip'}, dimensions={0} | all-to-all | bytes 8192 | tf_op jit(solution)/shard_map/all_to_all | solution.py:327
  85.8 0.7 copy.16
Async XLA Ops:
  0.6 33.0 %copy-start = (bf16[512,512]{1,0:T(8,128)(2,1)S(1)}, bf16[512,512]{1,0:T(8,128)(2,1)}, u32[]{:S(2)}) copy-start(bf16[512,512]{1,0:T(8,128)(2,1)} %constant.11.clone.refs_5_.back) | copy-start | bytes 1572868
  45.9 27.1 %copy-start.1 = (bf16[512,2048]{1,0:T(8,128)(2,1)S(1)}, bf16[512,2048]{1,0:T(8,128)(2,1)}, u32[]{:S(2)}) copy-start(bf16[512,2048]{1,0:T(8,128)(2,1)} %constant.14.clone.spots) | copy-start | bytes 6291460
  45.9 27.1 %copy-start.2 = (bf16[512,512]{1,0:T(8,128)(2,1)S(1)}, bf16[512,512]{1,0:T(8,128)(2,1)}, u32[]{:S(2)}) copy-start(bf16[512,512]{1,0:T(8,128)(2,1)} %constant.13.clone.back_sub) | copy-start | bytes 1572868
  45.9 27.1 %copy-start.3 = (bf16[1024,16]{0,1:T(8,128)(2,1)S(1)}, bf16[1024,16]{0,1:T(8,128)(2,1)}, u32[]{:S(2)}) copy-start(bf16[1024,16]{0,1:T(8,128)(2,1)} %param.14) | copy-start | bytes 98308

commit v6 on v5

--- a/solution.py
+++ b/solution.py
@@ -50,14 +50,15 @@
 def sincos(x):
     y = 0.5 * x
     z = y * y
-    s = -1.0 / 39916800.0
-    for c in (1.0 / 362880.0, -1.0 / 5040.0, 1.0 / 120.0, -1.0 / 6.0, 1.0):
-        s = s * z + c
+    s = 2.6048728614114225e-06
+    for a in (-0.0001980891975108534, 0.008333048783242702, -0.16666658222675323, 1.0):
+        s = s * z + a
     s = s * y
-    c = 1.0 / 479001600.0
-    for a in (-1.0 / 3628800.0, 1.0 / 40320.0, -1.0 / 720.0, 1.0 / 24.0, -0.5, 1.0):
+    c = 2.3149976186687127e-05
+    for a in (-0.0013853529235348105, 0.04166356101632118, -0.4999990463256836, 0.9999999403953552):
         c = c * z + a
-    return 1.0 - 2.0 * s * s, 2.0 * s * c
+    t = s + s
+    return 1.0 - t * s, t * c
 
 
 def twiddles(out):
@@ -172,10 +173,10 @@
     return re, im
 
 
-def sent(spectrum, twiddle, table, out):
+def sent(spectrum, twiddle, table, out, turned=F32):
     for n1, (r, m) in enumerate(zip(*inverse(spectrum, "send", twiddle, table))):
         x = jnp.concatenate([r[:, :128], m[:, :128], r[:, 128:], m[:, 128:]], axis=0)
-        x = x.T.astype(BF).reshape(8, 16, 128)
+        x = x.astype(turned).T.astype(BF).reshape(8, 16, 128)
         for base in range(0, out.shape[0], 32):
             out[base + 8 * n1 : base + 8 * n1 + 8, 0:16, :] = x
 
@@ -190,8 +191,8 @@
 
 
 def payload_kernel(
-    distance, far_screens, launch, far_targets, far_counts, far_table,
-    shared, held, picks, table, twiddle,
+    distance, far_screens, launch, far_targets, far_counts, far_table, far_send,
+    shared, held, picks, table, send, twiddle,
     screens, targets, counts, sems,
 ):
     group = lax.axis_index("layer")
@@ -199,7 +200,7 @@
         pltpu.make_async_copy(source, target, sems.at[i])
         for i, (source, target) in enumerate([
             (far_screens, screens), (far_targets, targets), (far_counts, counts),
-            (launch.at[group % 2], held), (far_table, table),
+            (launch.at[group % 2], held), (far_table, table), (far_send, send),
         ])
     ]
     for copy in copies:
@@ -223,15 +224,11 @@
         copy.wait()
 
 
-def first_kernel(held, shared, twiddle, table, far_send, out, h, send, sem):
-    copy = pltpu.make_async_copy(far_send, send, sem)
-    copy.start()
+def first_kernel(held, shared, twiddle, table, send, out, h):
     spectra(shared, h)
     re, im = quarters(held[0].astype(F32)), quarters(held[1].astype(F32))
     re, im = through_screen(re, im, shared[0, :, 0:N].astype(F32))
-    spectrum = forward(re, im, 0, h, twiddle, table)
-    copy.wait()
-    sent(spectrum, twiddle, send, out)
+    sent(forward(re, im, 0, h, twiddle, table), twiddle, send, out)
     both = jnp.concatenate([shared[1, :, 0:N], shared[3, :, 0:N]], axis=0).astype(F32)
     for block in range(8):
         piece = both[:, 128 * block : 128 * block + 128].T.reshape(4, 2, 16, 64)
@@ -245,7 +242,7 @@
     spectrum = forward(quarters(re), quarters(im), layer, h, twiddle, table)
     re, im = inverse(spectrum, "plain", twiddle, back)
     re, im = through_screen(re, im, phase)
-    sent(forward(re, im, layer + 1, h, twiddle, table), twiddle, send, out)
+    sent(forward(re, im, layer + 1, h, twiddle, table), twiddle, send, out, BF)
 
 
 def column_kernel(layer, came, carried, *rest):
@@ -333,29 +330,30 @@
     tables = {name: jnp.asarray(value) for name, value in angle_tables().items()}
     table, back, send = tables["forward"], tables["plain"], tables["send"]
 
-    payload, held, picks, table, twiddle = call(
+    payload, held, picks, table, send, twiddle = call(
         payload_kernel,
         (
             jax.ShapeDtypeStruct((4, 32, N + 128), BF),
             jax.ShapeDtypeStruct(launch.shape[1:], BF),
             jax.ShapeDtypeStruct((1, 32), jnp.int32),
             jax.ShapeDtypeStruct(table.shape, BF),
+            jax.ShapeDtypeStruct(send.shape, BF),
             jax.ShapeDtypeStruct((24, Q), F32),
         ),
         distance,
         *[
             pltpu.with_memory_space_constraint(x, pltpu.HBM)
             for x in (
-                screens, launch, send_table.reshape(1, 32), send_counts, table
+                screens, launch, send_table.reshape(1, 32), send_counts, table, send
             )
         ],
-        in_specs=[SMEM] + [FAR] * 5,
-        out_specs=(VMEM,) * 5,
+        in_specs=[SMEM] + [FAR] * 6,
+        out_specs=(VMEM,) * 6,
         scratch_shapes=[
             pltpu.VMEM(screens.shape, F32),
             pltpu.VMEM((1, 32), jnp.int32),
             pltpu.VMEM((1, 32), jnp.int32),
-            pltpu.SemaphoreType.DMA((5,)),
+            pltpu.SemaphoreType.DMA((6,)),
         ],
         name="payload",
     )
@@ -365,14 +363,9 @@
     plain = jax.ShapeDtypeStruct((32, 16, 128), BF)
     twice = jax.ShapeDtypeStruct((64, 16, 128), BF)
     pairs = [[32 * group + strip for group in pair for strip in range(32)] for pair in ((0, 1), (2, 3))]
-    leaving, h, send = call(
-        first_kernel,
-        (wide, jax.ShapeDtypeStruct((8, N), F32), jax.ShapeDtypeStruct(send.shape, BF)),
-        held, shared, twiddle, table, pltpu.with_memory_space_constraint(send, pltpu.HBM),
-        in_specs=[VMEM] * 4 + [FAR],
-        out_specs=(VMEM,) * 3,
-        scratch_shapes=[pltpu.SemaphoreType.DMA],
-        name="rows0",
+    leaving, h = call(
+        first_kernel, (wide, jax.ShapeDtypeStruct((8, N), F32)),
+        held, shared, twiddle, table, send, name="rows0",
     )
     carried = exchanged(leaving)
 

time: 86.9 us -> 86.1 us (level)
  no operation moved by 1% of the time
where the time goes in v6:
time: 86.1 us; the launch traced here: 85.7 us
  blocking collectives  76.2 us (89%)
  Pallas kernels  7.42 us (9%)
  between operations  1.39 us (2%)
    all_to_all x6, blocking collectives, exchanged(): lax.all_to_all(block, axis, split_axis=0, concat_axis=0, tiled=True, axis...  76.2 us
    pallas_call x6, Pallas kernels, call(): pl.pallas_call(kernel, out_shape=shapes, compiler_params=pltpu.CompilerPa...  7.42 us

profile of v6, /device:TPU:1, one launch (start us, length us, event | category | flops | bytes accessed | tf_op | source)
XLA Modules:
  0.0 85.7 jit_solution(3745880242050929900)
XLA Ops:
  0.6 0.0 copy-start
  1.3 1.4 %payload.1 = (bf16[4,32,1152]{2,1,0:T(8,128)(2,1)S(1)}, bf16[2,32,1024]{2,1,0:T(8,128)(2,1)S(1)}, s32[1,32]{1,0:T(1,128)S(1)}, bf16[512,512]{1,0:T(8,128)(2,1)S(...) custom-call(f32[1]{0:T(128)S(6)} %copy.17.distance, f32[1,32,1024]{2,1,0:T(8,128)} %far_screens.1, ...), custom_call_target="tpu_custom_call" | custom-call | tf_op jit(solution)/shard_map/payload/pallas_call | solution.py:314
  2.8 10.6 %all_to_all.34.shared.refs_1_ = bf16[4,32,1152]{2,1,0:T(8,128)(2,1)S(1)} all-to-all(bf16[4,32,1152]{2,1,0:T(8,128)(2,1)S(1)} %get-tuple-element.13), channel_id=1, replica_groups=mesh['layer'=4,'strip'=32] {'layer'}, dimensions={0} | all-to-all | bytes 589824 | tf_op jit(solution)/shard_map/all_to_all | solution.py:324
  13.4 0.7 rows0.1
  14.1 18.9 %all_to_all.35.refs_0_.refs_1_ = bf16[32,32,128]{2,1,0:T(8,128)(2,1)S(1)} all-to-all(bf16[32,32,128]{2,1,0:T(8,128)(2,1)S(1)} %get-tuple-element.17), channel_id=1, replica_groups=mesh['layer'=4,'strip'=32] {'strip'}, dimensions={0} | all-to-all | bytes 524288 | tf_op jit(solution)/shard_map/all_to_all | solution.py:324
  33.0 0.0 copy-done
  33.0 1.1 %columns01.1 = bf16[32,16,128]{2,1,0:T(8,128)(2,1)S(1)} custom-call(bf16[32,32,128]{2,1,0:T(8,128)(2,1)S(1)} %all_to_all.35.refs_0_.refs_1_, bf16[32,32,128]{2,1,0:T(8,128)(2,1)S(1)} %all_to_all.35.refs_0_.refs_1_, f32[8,1024]{1,0:T(8,128)S(1)} %get-tuple-element.18.refs_2_.h, f32[24,256]{1,0:T(8,128)S(1)} %get-tuple-element.14.twiddle.refs_3_, ...), custom_call_target="tpu_custom_call" | custom-call | tf_op jit(solution)/shard_map/columns01/pallas_call | solution.py:314
  34.1 11.2 %all_to_all.36.refs_0_ = bf16[32,16,128]{2,1,0:T(8,128)(2,1)S(1)} all-to-all(bf16[32,16,128]{2,1,0:T(8,128)(2,1)S(1)} %columns01.1), channel_id=1, replica_groups=mesh['layer'=4,'strip'=32] {'strip'}, dimensions={0} | all-to-all | bytes 262144 | tf_op jit(solution)/shard_map/all_to_all | solution.py:324
  45.3 0.0 copy-start.1
  45.3 0.0 copy-start.2
  45.3 0.0 copy-start.3
  45.3 1.2 %rows12.1 = bf16[32,16,128]{2,1,0:T(8,128)(2,1)S(1)} custom-call(bf16[32,16,128]{2,1,0:T(8,128)(2,1)S(1)} %all_to_all.36.refs_0_, bf16[4,32,1152]{2,1,0:T(8,128)(2,1)S(1)} %all_to_all.34.shared.refs_1_, f32[8,1024]{1,0:T(8,128)S(1)} %get-tuple-element.18.refs_2_.h, f32[24,256]{1,0:T(8,128)S(1)} %get-tuple-element.14.twiddle.refs_3_, ...), custom_call_target="tpu_custom_call" | custom-call | tf_op jit(solution)/shard_map/rows12/pallas_call | solution.py:314
  46.5 11.3 %all_to_all.37.refs_0_ = bf16[32,16,128]{2,1,0:T(8,128)(2,1)S(1)} all-to-all(bf16[32,16,128]{2,1,0:T(8,128)(2,1)S(1)} %rows12.1), channel_id=1, replica_groups=mesh['layer'=4,'strip'=32] {'strip'}, dimensions={0} | all-to-all | bytes 262144 | tf_op jit(solution)/shard_map/all_to_all | solution.py:324
  57.7 1.1 %columns23.1 = bf16[64,16,128]{2,1,0:T(8,128)(2,1)S(1)} custom-call(bf16[32,16,128]{2,1,0:T(8,128)(2,1)S(1)} %all_to_all.37.refs_0_, bf16[32,32,128]{2,1,0:T(8,128)(2,1)S(1)} %all_to_all.35.refs_0_.refs_1_, f32[8,1024]{1,0:T(8,128)S(1)} %get-tuple-element.18.refs_2_.h, f32[24,256]{1,0:T(8,128)S(1)} %get-tuple-element.14.twiddle.refs_3_, ...), custom_call_target="tpu_custom_call" | custom-call | tf_op jit(solution)/shard_map/columns23/pallas_call | solution.py:314
  58.9 13.4 %all_to_all.38.came = bf16[64,16,128]{2,1,0:T(8,128)(2,1)S(1)} all-to-all(bf16[64,16,128]{2,1,0:T(8,128)(2,1)S(1)} %columns23.1), channel_id=1, replica_groups={{0,1,2,3,4,5,6,7,8,9,10,11,12,13,14,15,16,17,18,19,20,21,22,23,24,25,26..., dimensions={0} | all-to-all | bytes 524288 | tf_op jit(solution)/shard_map/all_to_all | solution.py:324
  72.3 0.0 copy-done.1
  72.3 0.0 copy-done.2
  72.3 0.0 copy-done.3
  72.3 1.9 %rows3.1 = (bf16[2,2,32,1024]{3,2,1,0:T(8,128)(2,1)}, f32[32,32]{1,0:T(8,128)S(1)}) custom-call(bf16[64,16,128]{2,1,0:T(8,128)(2,1)S(1)} %all_to_all.38.came, f32[8,1024]{1,0:T(8,128)S(1)} %get-tuple-element.18.refs_2_.h, f32[24,256]{1,0:T(8,128)S(1)} %get-tuple-element.14.twiddle.refs_3_, bf16[512,512]{1,0:T(8,128)(2,1)S(1)} %get-tuple-element.15.table.refs_4_, ...), custom_call_target="tpu_custom_call" | custom-call | tf_op jit(solution)/shard_map/rows3/pallas_call | solution.py:314
  74.2 10.9 %all_to_all.39 = f32[32,1,32]{2,1,0:T(1,128)S(1)} all-to-all(f32[32,1,32]{2,1,0:T(1,128)S(1)} %bitcast.7), channel_id=1, replica_groups=mesh['layer'=4,'strip'=32] {'strip'}, dimensions={0} | all-to-all | bytes 8192 | tf_op jit(solution)/shard_map/all_to_all | solution.py:324
  85.1 0.7 copy.16
Async XLA Ops:
  0.6 32.4 %copy-start = (bf16[512,512]{1,0:T(8,128)(2,1)S(1)}, bf16[512,512]{1,0:T(8,128)(2,1)}, u32[]{:S(2)}) copy-start(bf16[512,512]{1,0:T(8,128)(2,1)} %constant.11.clone.refs_5_.back) | copy-start | bytes 1572868
  45.3 27.0 %copy-start.1 = (bf16[512,2048]{1,0:T(8,128)(2,1)S(1)}, bf16[512,2048]{1,0:T(8,128)(2,1)}, u32[]{:S(2)}) copy-start(bf16[512,2048]{1,0:T(8,128)(2,1)} %constant.14.clone.spots) | copy-start | bytes 6291460
  45.3 27.0 %copy-start.2 = (bf16[512,512]{1,0:T(8,128)(2,1)S(1)}, bf16[512,512]{1,0:T(8,128)(2,1)}, u32[]{:S(2)}) copy-start(bf16[512,512]{1,0:T(8,128)(2,1)} %constant.13.clone.back_sub) | copy-start | bytes 1572868
  45.3 27.0 %copy-start.3 = (bf16[1024,16]{0,1:T(8,128)(2,1)S(1)}, bf16[1024,16]{0,1:T(8,128)(2,1)}, u32[]{:S(2)}) copy-start(bf16[1024,16]{0,1:T(8,128)(2,1)} %param.14) | copy-start | bytes 98308

commit v7 on v6

--- a/solution.py
+++ b/solution.py
@@ -192,7 +192,7 @@
 
 def payload_kernel(
     distance, far_screens, launch, far_targets, far_counts, far_table, far_send,
-    shared, held, picks, table, send, twiddle,
+    shared, held, table, send, twiddle,
     screens, targets, counts, sems,
 ):
     group = lax.axis_index("layer")
@@ -210,16 +210,19 @@
     middle = (d - high).astype(BF).astype(F32)
     low = (d - high) - middle
     row = lax.broadcasted_iota(jnp.int32, (32, 128), 0)
-    tail = jnp.where(row == 0, high, jnp.where(row == 1, middle, jnp.where(row == 2, low, 0.0)))
-    tail = tail.astype(BF)
     twiddles(twiddle)
     for copy in copies[:3]:
         copy.wait()
+    picks = jnp.where(group < counts[...], targets[...], -1).astype(F32)
+    picks = jnp.concatenate([picks, jnp.full((1, 96), -1.0, F32)], axis=1)
+    tail = jnp.zeros((32, 128), F32)
+    for i, value in enumerate((high, middle, low, picks)):
+        tail = jnp.where(row == i, value, tail)
+    tail = tail.astype(BF)
     phase = screens[0].astype(BF)
     for other in range(4):
         shared[other, :, 0:N] = phase
         shared[other, :, N : N + 128] = tail
-    picks[...] = jnp.where(group < counts[...], targets[...], -1)
     for copy in copies[3:]:
         copy.wait()
 
@@ -257,52 +260,52 @@
 
 
 def last_kernel(
-    came, h, twiddle, table, back, back_sub, spots, templates, picks,
-    far_pupil, result,
-    cells, pupil, sem,
+    came, shared, h, twiddle, table, back, back_sub, spots, templates, mine, result, cells
 ):
-    fields = [field_of(came, 0), field_of(came, 32)]
-    re, im = [quarters(jnp.concatenate(x, axis=0)) for x in zip(*fields)]
-    spectrum = forward(re, im, 3, h, twiddle, table)
+    re, im = field_of(came)
+    spectrum = forward(quarters(re), quarters(im), 3, h, twiddle, table)
     for part, x in enumerate(inverse(spectrum, "sub", twiddle, back_sub)):
-        for field in range(2):
-            for upper in range(2):
-                parts = [
-                    x[n1][32 * field + 16 * a : 32 * field + 16 * a + 16,
-                          128 * upper : 128 * upper + 128].astype(BF)
-                    for a in range(2)
-                    for n1 in range(4)
-                ]
-                for k, piece in enumerate(granules(parts, 16)):
-                    row = part * 256 + (upper * 8 + k) * 16
-                    cells[row : row + 16, 128 * field : 128 * field + 128] = piece
-    re, im = inverse(spectrum, "plain", twiddle, back)
-    for n in range(4):
-        for field in range(2):
-            rows = slice(32 * field, 32 * field + 32)
-            pupil[field, 0, :, Q * n : Q * n + Q] = re[n][rows].astype(BF)
-            pupil[field, 1, :, Q * n : Q * n + Q] = im[n][rows].astype(BF)
-    written = pltpu.make_async_copy(pupil, far_pupil, sem)
-    written.start()
-    place = lax.broadcasted_iota(jnp.int32, (128, 32), 0)
-    chosen = jnp.where(place == picks[...], 1.0, 0.0).astype(F32).T.astype(BF)
-    slots = [
-        lax.dot_general(
-            chosen,
-            cells[:, 128 * field : 128 * field + 128],
-            (((1,), (1,)), ((), ())),
-            preferred_element_type=F32,
-        ).astype(BF)
-        for field in range(2)
+        for upper in range(2):
+            parts = [
+                x[n1][16 * a : 16 * a + 16, 128 * upper : 128 * upper + 128].astype(BF)
+                for a in range(2)
+                for n1 in range(4)
+            ]
+            for k, piece in enumerate(granules(parts, 16)):
+                row = part * 256 + (upper * 8 + k) * 16
+                cells[row : row + 16, :] = piece
+    for part, x in enumerate(inverse(spectrum, "plain", twiddle, back)):
+        for n in range(4):
+            mine[part, :, Q * n : Q * n + Q] = x[n].astype(BF)
+    first = lax.axis_index("layer") // 2 * 2
+    picks = [shared[first + i, 0:16, N : N + 128].astype(F32)[3:4, :32] for i in range(2)]
+    picks = jnp.concatenate(picks, axis=1)
+    place = lax.broadcasted_iota(jnp.int32, (128, 64), 0).astype(F32)
+    chosen = jnp.where(place == picks, 1.0, 0.0).astype(F32).T.astype(BF)
+    slots = lax.dot_general(
+        chosen, cells[...], (((1,), (1,)), ((), ())), preferred_element_type=F32
+    ).astype(BF)
+    spot = jnp.dot(slots, spots[...], preferred_element_type=F32)
+    intensity = (spot[:, :1024] * spot[:, :1024] + spot[:, 1024:] * spot[:, 1024:]).astype(BF)
+    result[...] = lax.dot_general(
+        intensity, templates[...], (((1,), (1,)), ((), ())), preferred_element_type=F32
+    )
+
+
+def outputs_kernel(mine, other, result, pupil, correlation, turned, sems):
+    own = lax.axis_index("layer") % 2
+    copies = [
+        pltpu.make_async_copy(mine, pupil.at[own], sems.at[0]),
+        pltpu.make_async_copy(other, pupil.at[1 - own], sems.at[1]),
     ]
-    spot = jnp.dot(jnp.concatenate(slots, axis=0), spots[...], preferred_element_type=F32)
-    intensity = (spot[:, :1024] * spot[:, :1024] + spot[:, 1024:] * spot[:, 1024:]).astype(BF)
-    total = lax.dot_general(
-        intensity, templates[...], (((1,), (1,)), ((), ())), preferred_element_type=F32
-    )
+    for copy in copies:
+        copy.start()
     for field in range(2):
-        result[:, 16 * field : 16 * field + 16] = total[32 * field : 32 * field + 32]
-    written.wait()
+        turned[field] = result[32 * field : 32 * field + 32, :].T
+    copies.append(pltpu.make_async_copy(turned, correlation, sems.at[2]))
+    copies[2].start()
+    for copy in copies:
+        copy.wait()
 
 
 VMEM = pl.BlockSpec(memory_space=pltpu.VMEM)
@@ -330,12 +333,11 @@
     tables = {name: jnp.asarray(value) for name, value in angle_tables().items()}
     table, back, send = tables["forward"], tables["plain"], tables["send"]
 
-    payload, held, picks, table, send, twiddle = call(
+    payload, held, table, send, twiddle = call(
         payload_kernel,
         (
             jax.ShapeDtypeStruct((4, 32, N + 128), BF),
             jax.ShapeDtypeStruct(launch.shape[1:], BF),
-            jax.ShapeDtypeStruct((1, 32), jnp.int32),
             jax.ShapeDtypeStruct(table.shape, BF),
             jax.ShapeDtypeStruct(send.shape, BF),
             jax.ShapeDtypeStruct((24, Q), F32),
@@ -348,7 +350,7 @@
             )
         ],
         in_specs=[SMEM] + [FAR] * 6,
-        out_specs=(VMEM,) * 6,
+        out_specs=(VMEM,) * 5,
         scratch_shapes=[
             pltpu.VMEM(screens.shape, F32),
             pltpu.VMEM((1, 32), jnp.int32),
@@ -361,7 +363,6 @@
 
     wide = jax.ShapeDtypeStruct((32, 32, 128), BF)
     plain = jax.ShapeDtypeStruct((32, 16, 128), BF)
-    twice = jax.ShapeDtypeStruct((64, 16, 128), BF)
     pairs = [[32 * group + strip for group in pair for strip in range(32)] for pair in ((0, 1), (2, 3))]
     leaving, h = call(
         first_kernel, (wide, jax.ShapeDtypeStruct((8, N), F32)),
@@ -369,11 +370,11 @@
     )
     carried = exchanged(leaving)
 
-    def columns(layer, came, shape, name):
+    def columns(layer, came, name):
         def kernel(*refs):
             column_kernel(layer, *refs)
 
-        return call(kernel, shape, came, carried, h, twiddle, table, back, send, name=name)
+        return call(kernel, plain, came, carried, h, twiddle, table, back, send, name=name)
 
     def rows(layer, came, name):
         def kernel(*refs):
@@ -381,25 +382,30 @@
 
         return call(kernel, plain, came, shared, h, twiddle, table, back, send, name=name)
 
-    came = exchanged(columns(0, carried, plain, "columns01"))
+    came = exchanged(columns(0, carried, "columns01"))
     came = exchanged(rows(1, came, "rows12"))
-    came = exchanged(columns(2, came, twice, "columns23"), ("layer", "strip"), pairs)
+    came = exchanged(columns(2, came, "columns23"))
 
     spots = jnp.asarray(spot_table())
-    pupil, result = call(
+    mine, result = call(
         last_kernel,
-        (jax.ShapeDtypeStruct(launch.shape, BF), jax.ShapeDtypeStruct((32, 32), F32)),
-        came, h, twiddle, table, back, tables["sub"], spots, templates.T, picks,
-        in_specs=[VMEM] * 9,
-        out_specs=(FAR, VMEM),
-        scratch_shapes=[
-            pltpu.VMEM((512, 256), BF),
-            pltpu.VMEM(launch.shape, BF),
-            pltpu.SemaphoreType.DMA,
-        ],
+        (jax.ShapeDtypeStruct(launch.shape[1:], BF), jax.ShapeDtypeStruct((64, 16), F32)),
+        came, shared, h, twiddle, table, back, tables["sub"], spots, templates.T,
+        scratch_shapes=[pltpu.VMEM((512, 128), BF)],
         name="rows3",
     )
-    return (pupil, exchanged(result).reshape(1, 32, 1, 2, 16))
+    other = lax.ppermute(mine, "layer", [(0, 1), (1, 0), (2, 3), (3, 2)])
+    result = exchanged(result, ("layer", "strip"), pairs)
+    pupil, correlation = call(
+        outputs_kernel,
+        (jax.ShapeDtypeStruct(launch.shape, BF), jax.ShapeDtypeStruct((2, 16, 32), F32)),
+        mine, other, result,
+        in_specs=[VMEM] * 3,
+        out_specs=(FAR, FAR),
+        scratch_shapes=[pltpu.VMEM((2, 16, 32), F32), pltpu.SemaphoreType.DMA((3,))],
+        name="outputs",
+    )
+    return (pupil, correlation.transpose(2, 0, 1)[None, :, None])
 
 
 def solution(mesh):

time: 86.1 us -> 86.1 us (level)
    pallas_call x6 -> x7, Pallas kernels: 7.42 us -> 7.81 us  [call(): pl.pallas_call(kernel, out_shape=shapes, compiler_params=pltpu.CompilerPa...]
  transfers between devices with their start and end apart: 0 -> 1, of which waited for: 0 -> 0; matrix products, arithmetic and copies ran while one was open for 0% -> 0% of each run, Pallas kernels for 0% -> 0%
where the time goes in v7:
time: 86.1 us; the launch traced here: 85.7 us
  blocking collectives  76.2 us (89%)
  Pallas kernels  7.81 us (9%)
  between operations  1.38 us (2%)
    all_to_all x6, blocking collectives, exchanged(): lax.all_to_all(block, axis, split_axis=0, concat_axis=0, tiled=True, axis...  76.2 us
    pallas_call x7, Pallas kernels, call(): pl.pallas_call(kernel, out_shape=shapes, compiler_params=pltpu.CompilerPa...  7.81 us
  transfers between devices with their start and end apart: 1, of which 0 were waited for; matrix products, arithmetic and copies ran while one was open for 0% of the time, Pallas kernels for 0%

profile of v7, /device:TPU:1, one launch (start us, length us, event | category | flops | bytes accessed | tf_op | source)
XLA Modules:
  0.0 85.7 jit_solution(13408647744360369719)
XLA Ops:
  0.6 0.0 copy-start
  1.3 1.4 %payload.1 = (bf16[4,32,1152]{2,1,0:T(8,128)(2,1)S(1)}, bf16[2,32,1024]{2,1,0:T(8,128)(2,1)S(1)}, bf16[512,512]{1,0:T(8,128)(2,1)S(1)}, bf16[512,512]{1,0:T(8,128)(2,1)S(1)}, f32[24,256]{1,0:T(8,128)S(1)}) custom-call(f32[1]{0:T(128)S(6)} %copy.14.distance, f32[1,32,1024]{2,1,0:T(8,128)} %far_screens.1, bf16[2,2,32,1024]{3,2,1,0:T(8,128)(2,1)} %launch.1, ...), custom_call_target="tpu_custom_call" | custom-call | tf_op jit(solution)/shard_map/payload/pallas_call | solution.py:317
  2.8 10.6 %all_to_all.36.shared.refs_1_ = bf16[4,32,1152]{2,1,0:T(8,128)(2,1)S(1)} all-to-all(bf16[4,32,1152]{2,1,0:T(8,128)(2,1)S(1)} %get-tuple-element.14), channel_id=1, replica_groups=mesh['layer'=4,'strip'=32] {'layer'}, dimensions={0} | all-to-all | bytes 589824 | tf_op jit(solution)/shard_map/all_to_all | solution.py:327
  13.4 0.7 rows0.1
  14.1 18.9 %all_to_all.37.refs_0_.refs_1_ = bf16[32,32,128]{2,1,0:T(8,128)(2,1)S(1)} all-to-all(bf16[32,32,128]{2,1,0:T(8,128)(2,1)S(1)} %get-tuple-element.18), channel_id=1, replica_groups=mesh['layer'=4,'strip'=32] {'strip'}, dimensions={0} | all-to-all | bytes 524288 | tf_op jit(solution)/shard_map/all_to_all | solution.py:327
  33.0 0.0 copy-done
  33.0 1.1 %columns01.1 = bf16[32,16,128]{2,1,0:T(8,128)(2,1)S(1)} custom-call(bf16[32,32,128]{2,1,0:T(8,128)(2,1)S(1)} %all_to_all.37.refs_0_.refs_1_, bf16[32,32,128]{2,1,0:T(8,128)(2,1)S(1)} %all_to_all.37.refs_0_.refs_1_, f32[8,1024]{1,0:T(8,128)S(1)} %get-tuple-element.19.refs_2_.h, f32[24,256]{1,0:T(8,128)S(1)} %get-tuple-element.15.twiddle.refs_3_, ...), custom_call_target="tpu_custom_call" | custom-call | tf_op jit(solution)/shard_map/columns01/pallas_call | solution.py:317
  34.1 11.2 %all_to_all.38.refs_0_ = bf16[32,16,128]{2,1,0:T(8,128)(2,1)S(1)} all-to-all(bf16[32,16,128]{2,1,0:T(8,128)(2,1)S(1)} %columns01.1), channel_id=1, replica_groups=mesh['layer'=4,'strip'=32] {'strip'}, dimensions={0} | all-to-all | bytes 262144 | tf_op jit(solution)/shard_map/all_to_all | solution.py:327
  45.3 0.0 copy-start.1
  45.3 0.0 copy-start.2
  45.3 0.0 copy-start.3
  45.3 1.1 %rows12.1 = bf16[32,16,128]{2,1,0:T(8,128)(2,1)S(1)} custom-call(bf16[32,16,128]{2,1,0:T(8,128)(2,1)S(1)} %all_to_all.38.refs_0_, bf16[4,32,1152]{2,1,0:T(8,128)(2,1)S(1)} %all_to_all.36.shared.refs_1_, f32[8,1024]{1,0:T(8,128)S(1)} %get-tuple-element.19.refs_2_.h, f32[24,256]{1,0:T(8,128)S(1)} %get-tuple-element.15.twiddle.refs_3_, ...), custom_call_target="tpu_custom_call" | custom-call | tf_op jit(solution)/shard_map/rows12/pallas_call | solution.py:317
  46.4 11.3 %all_to_all.39.refs_0_ = bf16[32,16,128]{2,1,0:T(8,128)(2,1)S(1)} all-to-all(bf16[32,16,128]{2,1,0:T(8,128)(2,1)S(1)} %rows12.1), channel_id=1, replica_groups=mesh['layer'=4,'strip'=32] {'strip'}, dimensions={0} | all-to-all | bytes 262144 | tf_op jit(solution)/shard_map/all_to_all | solution.py:327
  57.7 1.1 %columns23.1 = bf16[32,16,128]{2,1,0:T(8,128)(2,1)S(1)} custom-call(bf16[32,16,128]{2,1,0:T(8,128)(2,1)S(1)} %all_to_all.39.refs_0_, bf16[32,32,128]{2,1,0:T(8,128)(2,1)S(1)} %all_to_all.37.refs_0_.refs_1_, f32[8,1024]{1,0:T(8,128)S(1)} %get-tuple-element.19.refs_2_.h, f32[24,256]{1,0:T(8,128)S(1)} %get-tuple-element.15.twiddle.refs_3_, ...), custom_call_target="tpu_custom_call" | custom-call | tf_op jit(solution)/shard_map/columns23/pallas_call | solution.py:317
  58.8 11.3 %all_to_all.40.came = bf16[32,16,128]{2,1,0:T(8,128)(2,1)S(1)} all-to-all(bf16[32,16,128]{2,1,0:T(8,128)(2,1)S(1)} %columns23.1), channel_id=1, replica_groups=mesh['layer'=4,'strip'=32] {'strip'}, dimensions={0} | all-to-all | bytes 262144 | tf_op jit(solution)/shard_map/all_to_all | solution.py:327
  70.1 0.0 copy-done.1
  70.1 0.0 copy-done.2
  70.1 0.0 copy-done.3
  70.1 1.6 %rows3.1 = (bf16[2,32,1024]{2,1,0:T(8,128)(2,1)S(1)}, f32[64,16]{1,0:T(8,128)S(1)}) custom-call(bf16[32,16,128]{2,1,0:T(8,128)(2,1)S(1)} %all_to_all.40.came, bf16[4,32,1152]{2,1,0:T(8,128)(2,1)S(1)} %all_to_all.36.shared.refs_1_, f32[8,1024]{1,0:T(8,128)S(1)} %get-tuple-element.19.refs_2_.h, f32[24,256]{1,0:T(8,128)S(1)} %get-tuple-element.15.twiddle.refs_3_, ...), custom_call_target="tpu_custom_call" | custom-call | tf_op jit(solution)/shard_map/rows3/pallas_call | solution.py:317
  71.7 0.3 collective-permute-start
  72.0 13.0 %all_to_all.41 = f32[64,1,16]{2,1,0:T(1,128)S(1)} all-to-all(f32[64,1,16]{2,1,0:T(1,128)S(1)} %bitcast.11), channel_id=1, replica_groups={{0,1,2,3,4,5,6,7,8,9,10,11,12,13,14,15,16,17,18,19,20,21,22,23,24,25,26..., dimensions={0} | all-to-all | bytes 8192 | tf_op jit(solution)/shard_map/all_to_all | solution.py:327
  85.0 0.0 collective-permute-done.other
  85.0 0.7 outputs.1
Async XLA Ops:
  0.6 32.4 %copy-start = (bf16[512,512]{1,0:T(8,128)(2,1)S(1)}, bf16[512,512]{1,0:T(8,128)(2,1)}, u32[]{:S(2)}) copy-start(bf16[512,512]{1,0:T(8,128)(2,1)} %constant.11.clone.refs_5_.back) | copy-start | bytes 1572868
  45.3 24.8 %copy-start.1 = (bf16[512,2048]{1,0:T(8,128)(2,1)S(1)}, bf16[512,2048]{1,0:T(8,128)(2,1)}, u32[]{:S(2)}) copy-start(bf16[512,2048]{1,0:T(8,128)(2,1)} %constant.14.clone.spots) | copy-start | bytes 6291460
  45.3 24.8 %copy-start.2 = (bf16[512,512]{1,0:T(8,128)(2,1)S(1)}, bf16[512,512]{1,0:T(8,128)(2,1)}, u32[]{:S(2)}) copy-start(bf16[512,512]{1,0:T(8,128)(2,1)} %constant.13.clone.back_sub) | copy-start | bytes 1572868
  45.3 24.8 %copy-start.3 = (bf16[1024,16]{0,1:T(8,128)(2,1)S(1)}, bf16[1024,16]{0,1:T(8,128)(2,1)}, u32[]{:S(2)}) copy-start(bf16[1024,16]{0,1:T(8,128)(2,1)} %param.14) | copy-start | bytes 98308
  71.7 13.3 %collective-permute-start = (bf16[2,32,1024]{2,1,0:T(8,128)(2,1)S(1)}, bf16[2,32,1024]{2,1,0:T(8,128)(2,1)S(1)}, u32[]{:S(2)}, u32[]{:S(2)}) collective-permute-start(bf16[2,32,1024]{2,1,0:T(8,128)(2,1)S(1)} %get-tuple-element.20.mine), channel_id=1, source_target_pairs={{0,32},{32,0},{64,96},{96,64},{1,33},{33,1},{65,97},{97,65},{2,34}... | collective-permute-start | bytes 393224 | tf_op jit(solution)/shard_map/ppermute | solution.py:397

commit v8 on v6

--- a/solution.py
+++ b/solution.py
@@ -191,8 +191,8 @@
 
 
 def payload_kernel(
-    distance, far_screens, launch, far_targets, far_counts, far_table, far_send,
-    shared, held, picks, table, send, twiddle,
+    distance, far_screens, launch, far_targets, far_counts,
+    shared, held, picks, twiddle,
     screens, targets, counts, sems,
 ):
     group = lax.axis_index("layer")
@@ -200,7 +200,7 @@
         pltpu.make_async_copy(source, target, sems.at[i])
         for i, (source, target) in enumerate([
             (far_screens, screens), (far_targets, targets), (far_counts, counts),
-            (launch.at[group % 2], held), (far_table, table), (far_send, send),
+            (launch.at[group % 2], held),
         ])
     ]
     for copy in copies:
@@ -330,31 +330,30 @@
     tables = {name: jnp.asarray(value) for name, value in angle_tables().items()}
     table, back, send = tables["forward"], tables["plain"], tables["send"]
 
-    payload, held, picks, table, send, twiddle = call(
+    payload, held, picks, twiddle = call(
         payload_kernel,
         (
             jax.ShapeDtypeStruct((4, 32, N + 128), BF),
             jax.ShapeDtypeStruct(launch.shape[1:], BF),
             jax.ShapeDtypeStruct((1, 32), jnp.int32),
-            jax.ShapeDtypeStruct(table.shape, BF),
-            jax.ShapeDtypeStruct(send.shape, BF),
             jax.ShapeDtypeStruct((24, Q), F32),
         ),
         distance,
         *[
             pltpu.with_memory_space_constraint(x, pltpu.HBM)
             for x in (
-                screens, launch, send_table.reshape(1, 32), send_counts, table, send
+                screens, launch, send_table.reshape(1, 32), send_counts
             )
         ],
-        in_specs=[SMEM] + [FAR] * 6,
-        out_specs=(VMEM,) * 6,
+        in_specs=[SMEM] + [FAR] * 4,
+        out_specs=(VMEM,) * 4,
         scratch_shapes=[
             pltpu.VMEM(screens.shape, F32),
             pltpu.VMEM((1, 32), jnp.int32),
             pltpu.VMEM((1, 32), jnp.int32),
-            pltpu.SemaphoreType.DMA((6,)),
+            pltpu.SemaphoreType.DMA((4,)),
         ],
+        cost_estimate=pl.CostEstimate(flops=1500000000, bytes_accessed=4000000, transcendentals=0),
         name="payload",
     )
     shared = exchanged(payload, "layer")

time: 86.1 us -> 85.9 us (level)
  no operation moved by 1% of the time
where the time goes in v8:
time: 85.9 us; the launch traced here: 85.5 us
  blocking collectives  76.4 us (89%)
  Pallas kernels  7.11 us (8%)
  between operations  1.35 us (2%)
    all_to_all x6, blocking collectives, exchanged(): lax.all_to_all(block, axis, split_axis=0, concat_axis=0, tiled=True, axis...  76.4 us
    pallas_call x6, Pallas kernels, call(): pl.pallas_call(kernel, out_shape=shapes, compiler_params=pltpu.CompilerPa...  7.11 us

profile of v8, /device:TPU:1, one launch (start us, length us, event | category | flops | bytes accessed | tf_op | source)
XLA Modules:
  0.0 85.5 jit_solution(16632178317823636992)
XLA Ops:
  1.3 0.0 copy-start
  1.3 0.0 copy-start.2
  1.3 1.1 %payload.1 = (bf16[4,32,1152]{2,1,0:T(8,128)(2,1)S(1)}, bf16[2,32,1024]{2,1,0:T(8,128)(2,1)S(1)}, s32[1,32]{1,0:T(1,128)S(1)}, f32[24,256]{1,0:T(8,128)S(1)}) custom-call(f32[1]{0:T(128)S(6)} %copy.17.distance, f32[1,32,1024]{2,1,0:T(8,128)} %far_screens.1, bf16[2,2,32,1024]{3,2,1,0:T(8,128)(2,1)} %launch.1, s32[1,32]{1,0:T(1,128)} %bitcast.9, ...), custom_call_target="tpu_custom_call" | custom-call | flops 1500000000 | bytes 4000000 | tf_op jit(solution)/shard_map/payload/pallas_call | solution.py:314
  2.4 0.0 copy-start.1
  2.4 10.8 %all_to_all.34.shared.refs_1_ = bf16[4,32,1152]{2,1,0:T(8,128)(2,1)S(1)} all-to-all(bf16[4,32,1152]{2,1,0:T(8,128)(2,1)S(1)} %get-tuple-element.11), channel_id=1, replica_groups=mesh['layer'=4,'strip'=32] {'layer'}, dimensions={0} | all-to-all | bytes 589824 | tf_op jit(solution)/shard_map/all_to_all | solution.py:324
  13.2 0.0 copy-done
  13.2 0.0 copy-done.2
  13.2 0.7 rows0.1
  13.9 18.9 %all_to_all.35.refs_0_.refs_1_ = bf16[32,32,128]{2,1,0:T(8,128)(2,1)S(1)} all-to-all(bf16[32,32,128]{2,1,0:T(8,128)(2,1)S(1)} %get-tuple-element.13), channel_id=1, replica_groups=mesh['layer'=4,'strip'=32] {'strip'}, dimensions={0} | all-to-all | bytes 524288 | tf_op jit(solution)/shard_map/all_to_all | solution.py:324
  32.8 0.0 copy-done.1
  32.8 1.1 %columns01.1 = bf16[32,16,128]{2,1,0:T(8,128)(2,1)S(1)} custom-call(bf16[32,32,128]{2,1,0:T(8,128)(2,1)S(1)} %all_to_all.35.refs_0_.refs_1_, bf16[32,32,128]{2,1,0:T(8,128)(2,1)S(1)} %all_to_all.35.refs_0_.refs_1_, f32[8,1024]{1,0:T(8,128)S(1)} %get-tuple-element.14.refs_2_.h, f32[24,256]{1,0:T(8,128)S(1)} %get-tuple-element.12.twiddle.refs_3_, ...), custom_call_target="tpu_custom_call" | custom-call | tf_op jit(solution)/shard_map/columns01/pallas_call | solution.py:314
  33.9 11.2 %all_to_all.36.refs_0_ = bf16[32,16,128]{2,1,0:T(8,128)(2,1)S(1)} all-to-all(bf16[32,16,128]{2,1,0:T(8,128)(2,1)S(1)} %columns01.1), channel_id=1, replica_groups=mesh['layer'=4,'strip'=32] {'strip'}, dimensions={0} | all-to-all | bytes 262144 | tf_op jit(solution)/shard_map/all_to_all | solution.py:324
  45.1 0.0 copy-start.3
  45.1 0.0 copy-start.4
  45.1 1.1 %rows12.1 = bf16[32,16,128]{2,1,0:T(8,128)(2,1)S(1)} custom-call(bf16[32,16,128]{2,1,0:T(8,128)(2,1)S(1)} %all_to_all.36.refs_0_, bf16[4,32,1152]{2,1,0:T(8,128)(2,1)S(1)} %all_to_all.34.shared.refs_1_, f32[8,1024]{1,0:T(8,128)S(1)} %get-tuple-element.14.refs_2_.h, f32[24,256]{1,0:T(8,128)S(1)} %get-tuple-element.12.twiddle.refs_3_, ...), custom_call_target="tpu_custom_call" | custom-call | tf_op jit(solution)/shard_map/rows12/pallas_call | solution.py:314
  46.3 11.3 %all_to_all.37.refs_0_ = bf16[32,16,128]{2,1,0:T(8,128)(2,1)S(1)} all-to-all(bf16[32,16,128]{2,1,0:T(8,128)(2,1)S(1)} %rows12.1), channel_id=1, replica_groups=mesh['layer'=4,'strip'=32] {'strip'}, dimensions={0} | all-to-all | bytes 262144 | tf_op jit(solution)/shard_map/all_to_all | solution.py:324
  57.5 1.1 %columns23.1 = bf16[64,16,128]{2,1,0:T(8,128)(2,1)S(1)} custom-call(bf16[32,16,128]{2,1,0:T(8,128)(2,1)S(1)} %all_to_all.37.refs_0_, bf16[32,32,128]{2,1,0:T(8,128)(2,1)S(1)} %all_to_all.35.refs_0_.refs_1_, f32[8,1024]{1,0:T(8,128)S(1)} %get-tuple-element.14.refs_2_.h, f32[24,256]{1,0:T(8,128)S(1)} %get-tuple-element.12.twiddle.refs_3_, ...), custom_call_target="tpu_custom_call" | custom-call | tf_op jit(solution)/shard_map/columns23/pallas_call | solution.py:314
  58.7 13.4 %all_to_all.38.came = bf16[64,16,128]{2,1,0:T(8,128)(2,1)S(1)} all-to-all(bf16[64,16,128]{2,1,0:T(8,128)(2,1)S(1)} %columns23.1), channel_id=1, replica_groups={{0,1,2,3,4,5,6,7,8,9,10,11,12,13,14,15,16,17,18,19,20,21,22,23,24,25,26..., dimensions={0} | all-to-all | bytes 524288 | tf_op jit(solution)/shard_map/all_to_all | solution.py:324
  72.1 0.0 copy-done.3
  72.1 0.0 copy-done.4
  72.1 0.0 copy-done.5
  72.1 1.9 %rows3.1 = (bf16[2,2,32,1024]{3,2,1,0:T(8,128)(2,1)}, f32[32,32]{1,0:T(8,128)S(1)}) custom-call(bf16[64,16,128]{2,1,0:T(8,128)(2,1)S(1)} %all_to_all.38.came, f32[8,1024]{1,0:T(8,128)S(1)} %get-tuple-element.14.refs_2_.h, f32[24,256]{1,0:T(8,128)S(1)} %get-tuple-element.12.twiddle.refs_3_, bf16[512,512]{1,0:T(8,128)(2,1)S(1)} %copy-done, ...), custom_call_target="tpu_custom_call" | custom-call | tf_op jit(solution)/shard_map/rows3/pallas_call | solution.py:314
  74.0 10.9 %all_to_all.39 = f32[32,1,32]{2,1,0:T(1,128)S(1)} all-to-all(f32[32,1,32]{2,1,0:T(1,128)S(1)} %bitcast.7), channel_id=1, replica_groups=mesh['layer'=4,'strip'=32] {'strip'}, dimensions={0} | all-to-all | bytes 8192 | tf_op jit(solution)/shard_map/all_to_all | solution.py:324
  84.9 0.7 copy.16
  (1 shorter events, 0.0 us)
Async XLA Ops:
  1.3 11.9 %copy-start = (bf16[512,512]{1,0:T(8,128)(2,1)S(1)}, bf16[512,512]{1,0:T(8,128)(2,1)}, u32[]{:S(2)}) copy-start(bf16[512,512]{1,0:T(8,128)(2,1)} %constant.10.clone.table.refs_4_) | copy-start | bytes 1572868
  1.3 11.9 %copy-start.2 = (bf16[512,512]{1,0:T(8,128)(2,1)S(1)}, bf16[512,512]{1,0:T(8,128)(2,1)}, u32[]{:S(2)}) copy-start(bf16[512,512]{1,0:T(8,128)(2,1)} %constant.12.clone.send.refs_6_) | copy-start | bytes 1572868
  2.4 30.4 %copy-start.1 = (bf16[512,512]{1,0:T(8,128)(2,1)S(1)}, bf16[512,512]{1,0:T(8,128)(2,1)}, u32[]{:S(2)}) copy-start(bf16[512,512]{1,0:T(8,128)(2,1)} %constant.11.clone.refs_5_.back) | copy-start | bytes 1572868
  45.1 27.0 %copy-start.3 = (bf16[512,2048]{1,0:T(8,128)(2,1)S(1)}, bf16[512,2048]{1,0:T(8,128)(2,1)}, u32[]{:S(2)}) copy-start(bf16[512,2048]{1,0:T(8,128)(2,1)} %constant.14.clone.spots) | copy-start | bytes 6291460
  45.1 27.0 %copy-start.4 = (bf16[512,512]{1,0:T(8,128)(2,1)S(1)}, bf16[512,512]{1,0:T(8,128)(2,1)}, u32[]{:S(2)}) copy-start(bf16[512,512]{1,0:T(8,128)(2,1)} %constant.13.clone.back_sub) | copy-start | bytes 1572868
  45.1 27.0 %copy-start.5 = (bf16[1024,16]{0,1:T(8,128)(2,1)S(1)}, bf16[1024,16]{0,1:T(8,128)(2,1)}, u32[]{:S(2)}) copy-start(bf16[1024,16]{0,1:T(8,128)(2,1)} %param.14) | copy-start | bytes 98308

commit v9 on v8

--- a/solution.py
+++ b/solution.py
@@ -14,6 +14,7 @@
 SPOT = 2 * SUB
 BF = jnp.bfloat16
 F32 = jnp.float32
+CODE = 25.0
 
 
 def bf16(table):
@@ -59,6 +60,14 @@
         c = c * z + a
     t = s + s
     return 1.0 - t * s, t * c
+
+
+def coded(phase):
+    return jnp.exp(CODE * phase).astype(BF)
+
+
+def decoded(code):
+    return jnp.log(code.astype(F32)) * (1.0 / CODE)
 
 
 def twiddles(out):
@@ -215,7 +224,7 @@
     twiddles(twiddle)
     for copy in copies[:3]:
         copy.wait()
-    phase = screens[0].astype(BF)
+    phase = coded(screens[0])
     for other in range(4):
         shared[other, :, 0:N] = phase
         shared[other, :, N : N + 128] = tail
@@ -227,7 +236,7 @@
 def first_kernel(held, shared, twiddle, table, send, out, h):
     spectra(shared, h)
     re, im = quarters(held[0].astype(F32)), quarters(held[1].astype(F32))
-    re, im = through_screen(re, im, shared[0, :, 0:N].astype(F32))
+    re, im = through_screen(re, im, decoded(shared[0, :, 0:N]))
     sent(forward(re, im, 0, h, twiddle, table), twiddle, send, out)
     both = jnp.concatenate([shared[1, :, 0:N], shared[3, :, 0:N]], axis=0).astype(F32)
     for block in range(8):
@@ -248,12 +257,12 @@
 def column_kernel(layer, came, carried, *rest):
     groups = gathered(carried, 0, 16)
     which = layer // 2
-    phase = jnp.concatenate([groups[which], groups[2 + which]], axis=0)
+    phase = decoded(jnp.concatenate([groups[which], groups[2 + which]], axis=0))
     middle(layer, came, phase, *rest)
 
 
 def row_kernel(layer, came, shared, *rest):
-    middle(layer, came, shared[layer + 1, :, 0:N].astype(F32), *rest)
+    middle(layer, came, decoded(shared[layer + 1, :, 0:N]), *rest)
 
 
 def last_kernel(

time: 85.9 us -> 86 us (level)
  no operation moved by 1% of the time
where the time goes in v9:
time: 86 us; the launch traced here: 85.6 us
  blocking collectives  76.4 us (89%)
  Pallas kernels  7.17 us (8%)
  between operations  1.35 us (2%)
    all_to_all x6, blocking collectives, exchanged(): lax.all_to_all(block, axis, split_axis=0, concat_axis=0, tiled=True, axis...  76.4 us
    pallas_call x6, Pallas kernels, call(): pl.pallas_call(kernel, out_shape=shapes, compiler_params=pltpu.CompilerPa...  7.17 us

profile of v9, /device:TPU:1, one launch (start us, length us, event | category | flops | bytes accessed | tf_op | source)
XLA Modules:
  0.0 85.6 jit_solution(4285857076030241421)
XLA Ops:
  1.3 0.0 copy-start
  1.3 0.0 copy-start.2
  1.3 1.1 %payload.1 = (bf16[4,32,1152]{2,1,0:T(8,128)(2,1)S(1)}, bf16[2,32,1024]{2,1,0:T(8,128)(2,1)S(1)}, s32[1,32]{1,0:T(1,128)S(1)}, f32[24,256]{1,0:T(8,128)S(1)}) custom-call(f32[1]{0:T(128)S(6)} %copy.17.distance, f32[1,32,1024]{2,1,0:T(8,128)} %far_screens.1, bf16[2,2,32,1024]{3,2,1,0:T(8,128)(2,1)} %launch.1, s32[1,32]{1,0:T(1,128)} %bitcast.9, ...), custom_call_target="tpu_custom_call" | custom-call | flops 1500000000 | bytes 4000000 | tf_op jit(solution)/shard_map/payload/pallas_call | solution.py:323
  2.4 0.0 copy-start.1
  2.4 10.8 %all_to_all.34.shared.refs_1_ = bf16[4,32,1152]{2,1,0:T(8,128)(2,1)S(1)} all-to-all(bf16[4,32,1152]{2,1,0:T(8,128)(2,1)S(1)} %get-tuple-element.11), channel_id=1, replica_groups=mesh['layer'=4,'strip'=32] {'layer'}, dimensions={0} | all-to-all | bytes 589824 | tf_op jit(solution)/shard_map/all_to_all | solution.py:333
  13.2 0.0 copy-done
  13.2 0.0 copy-done.2
  13.2 0.8 rows0.1
  14.0 18.9 %all_to_all.35.refs_0_.refs_1_ = bf16[32,32,128]{2,1,0:T(8,128)(2,1)S(1)} all-to-all(bf16[32,32,128]{2,1,0:T(8,128)(2,1)S(1)} %get-tuple-element.13), channel_id=1, replica_groups=mesh['layer'=4,'strip'=32] {'strip'}, dimensions={0} | all-to-all | bytes 524288 | tf_op jit(solution)/shard_map/all_to_all | solution.py:333
  32.8 0.0 copy-done.1
  32.8 1.1 %columns01.1 = bf16[32,16,128]{2,1,0:T(8,128)(2,1)S(1)} custom-call(bf16[32,32,128]{2,1,0:T(8,128)(2,1)S(1)} %all_to_all.35.refs_0_.refs_1_, bf16[32,32,128]{2,1,0:T(8,128)(2,1)S(1)} %all_to_all.35.refs_0_.refs_1_, f32[8,1024]{1,0:T(8,128)S(1)} %get-tuple-element.14.refs_2_.h, f32[24,256]{1,0:T(8,128)S(1)} %get-tuple-element.12.twiddle.refs_3_, ...), custom_call_target="tpu_custom_call" | custom-call | tf_op jit(solution)/shard_map/columns01/pallas_call | solution.py:323
  33.9 11.2 %all_to_all.36.refs_0_ = bf16[32,16,128]{2,1,0:T(8,128)(2,1)S(1)} all-to-all(bf16[32,16,128]{2,1,0:T(8,128)(2,1)S(1)} %columns01.1), channel_id=1, replica_groups=mesh['layer'=4,'strip'=32] {'strip'}, dimensions={0} | all-to-all | bytes 262144 | tf_op jit(solution)/shard_map/all_to_all | solution.py:333
  45.1 0.0 copy-start.3
  45.1 0.0 copy-start.4
  45.1 1.2 %rows12.1 = bf16[32,16,128]{2,1,0:T(8,128)(2,1)S(1)} custom-call(bf16[32,16,128]{2,1,0:T(8,128)(2,1)S(1)} %all_to_all.36.refs_0_, bf16[4,32,1152]{2,1,0:T(8,128)(2,1)S(1)} %all_to_all.34.shared.refs_1_, f32[8,1024]{1,0:T(8,128)S(1)} %get-tuple-element.14.refs_2_.h, f32[24,256]{1,0:T(8,128)S(1)} %get-tuple-element.12.twiddle.refs_3_, ...), custom_call_target="tpu_custom_call" | custom-call | tf_op jit(solution)/shard_map/rows12/pallas_call | solution.py:323
  46.3 11.3 %all_to_all.37.refs_0_ = bf16[32,16,128]{2,1,0:T(8,128)(2,1)S(1)} all-to-all(bf16[32,16,128]{2,1,0:T(8,128)(2,1)S(1)} %rows12.1), channel_id=1, replica_groups=mesh['layer'=4,'strip'=32] {'strip'}, dimensions={0} | all-to-all | bytes 262144 | tf_op jit(solution)/shard_map/all_to_all | solution.py:333
  57.6 1.1 %columns23.1 = bf16[64,16,128]{2,1,0:T(8,128)(2,1)S(1)} custom-call(bf16[32,16,128]{2,1,0:T(8,128)(2,1)S(1)} %all_to_all.37.refs_0_, bf16[32,32,128]{2,1,0:T(8,128)(2,1)S(1)} %all_to_all.35.refs_0_.refs_1_, f32[8,1024]{1,0:T(8,128)S(1)} %get-tuple-element.14.refs_2_.h, f32[24,256]{1,0:T(8,128)S(1)} %get-tuple-element.12.twiddle.refs_3_, ...), custom_call_target="tpu_custom_call" | custom-call | tf_op jit(solution)/shard_map/columns23/pallas_call | solution.py:323
  58.7 13.4 %all_to_all.38.came = bf16[64,16,128]{2,1,0:T(8,128)(2,1)S(1)} all-to-all(bf16[64,16,128]{2,1,0:T(8,128)(2,1)S(1)} %columns23.1), channel_id=1, replica_groups={{0,1,2,3,4,5,6,7,8,9,10,11,12,13,14,15,16,17,18,19,20,21,22,23,24,25,26..., dimensions={0} | all-to-all | bytes 524288 | tf_op jit(solution)/shard_map/all_to_all | solution.py:333
  72.1 0.0 copy-done.3
  72.1 0.0 copy-done.4
  72.1 0.0 copy-done.5
  72.2 1.9 %rows3.1 = (bf16[2,2,32,1024]{3,2,1,0:T(8,128)(2,1)}, f32[32,32]{1,0:T(8,128)S(1)}) custom-call(bf16[64,16,128]{2,1,0:T(8,128)(2,1)S(1)} %all_to_all.38.came, f32[8,1024]{1,0:T(8,128)S(1)} %get-tuple-element.14.refs_2_.h, f32[24,256]{1,0:T(8,128)S(1)} %get-tuple-element.12.twiddle.refs_3_, bf16[512,512]{1,0:T(8,128)(2,1)S(1)} %copy-done, ...), custom_call_target="tpu_custom_call" | custom-call | tf_op jit(solution)/shard_map/rows3/pallas_call | solution.py:323
  74.0 10.9 %all_to_all.39 = f32[32,1,32]{2,1,0:T(1,128)S(1)} all-to-all(f32[32,1,32]{2,1,0:T(1,128)S(1)} %bitcast.7), channel_id=1, replica_groups=mesh['layer'=4,'strip'=32] {'strip'}, dimensions={0} | all-to-all | bytes 8192 | tf_op jit(solution)/shard_map/all_to_all | solution.py:333
  84.9 0.7 copy.16
  (1 shorter events, 0.0 us)
Async XLA Ops:
  1.3 11.9 %copy-start = (bf16[512,512]{1,0:T(8,128)(2,1)S(1)}, bf16[512,512]{1,0:T(8,128)(2,1)}, u32[]{:S(2)}) copy-start(bf16[512,512]{1,0:T(8,128)(2,1)} %constant.10.clone.table.refs_4_) | copy-start | bytes 1572868
  1.3 11.9 %copy-start.2 = (bf16[512,512]{1,0:T(8,128)(2,1)S(1)}, bf16[512,512]{1,0:T(8,128)(2,1)}, u32[]{:S(2)}) copy-start(bf16[512,512]{1,0:T(8,128)(2,1)} %constant.12.clone.send.refs_6_) | copy-start | bytes 1572868
  2.4 30.4 %copy-start.1 = (bf16[512,512]{1,0:T(8,128)(2,1)S(1)}, bf16[512,512]{1,0:T(8,128)(2,1)}, u32[]{:S(2)}) copy-start(bf16[512,512]{1,0:T(8,128)(2,1)} %constant.11.clone.refs_5_.back) | copy-start | bytes 1572868
  45.1 27.0 %copy-start.3 = (bf16[512,2048]{1,0:T(8,128)(2,1)S(1)}, bf16[512,2048]{1,0:T(8,128)(2,1)}, u32[]{:S(2)}) copy-start(bf16[512,2048]{1,0:T(8,128)(2,1)} %constant.14.clone.spots) | copy-start | bytes 6291460
  45.1 27.0 %copy-start.4 = (bf16[512,512]{1,0:T(8,128)(2,1)S(1)}, bf16[512,512]{1,0:T(8,128)(2,1)}, u32[]{:S(2)}) copy-start(bf16[512,512]{1,0:T(8,128)(2,1)} %constant.13.clone.back_sub) | copy-start | bytes 1572868
  45.1 27.0 %copy-start.5 = (bf16[1024,16]{0,1:T(8,128)(2,1)S(1)}, bf16[1024,16]{0,1:T(8,128)(2,1)}, u32[]{:S(2)}) copy-start(bf16[1024,16]{0,1:T(8,128)(2,1)} %param.14) | copy-start | bytes 98308

commit v10 on v7

--- a/solution.py
+++ b/solution.py
@@ -14,6 +14,7 @@
 SPOT = 2 * SUB
 BF = jnp.bfloat16
 F32 = jnp.float32
+CODE = 25.0
 
 
 def bf16(table):
@@ -59,6 +60,14 @@
         c = c * z + a
     t = s + s
     return 1.0 - t * s, t * c
+
+
+def coded(phase):
+    return jnp.exp(CODE * phase).astype(BF)
+
+
+def decoded(code):
+    return jnp.log(code.astype(F32)) * (1.0 / CODE)
 
 
 def twiddles(out):
@@ -191,8 +200,8 @@
 
 
 def payload_kernel(
-    distance, far_screens, launch, far_targets, far_counts, far_table, far_send,
-    shared, held, table, send, twiddle,
+    distance, far_screens, launch, far_targets, far_counts,
+    shared, held, twiddle,
     screens, targets, counts, sems,
 ):
     group = lax.axis_index("layer")
@@ -200,7 +209,7 @@
         pltpu.make_async_copy(source, target, sems.at[i])
         for i, (source, target) in enumerate([
             (far_screens, screens), (far_targets, targets), (far_counts, counts),
-            (launch.at[group % 2], held), (far_table, table), (far_send, send),
+            (launch.at[group % 2], held),
         ])
     ]
     for copy in copies:
@@ -219,7 +228,7 @@
     for i, value in enumerate((high, middle, low, picks)):
         tail = jnp.where(row == i, value, tail)
     tail = tail.astype(BF)
-    phase = screens[0].astype(BF)
+    phase = coded(screens[0])
     for other in range(4):
         shared[other, :, 0:N] = phase
         shared[other, :, N : N + 128] = tail
@@ -230,7 +239,7 @@
 def first_kernel(held, shared, twiddle, table, send, out, h):
     spectra(shared, h)
     re, im = quarters(held[0].astype(F32)), quarters(held[1].astype(F32))
-    re, im = through_screen(re, im, shared[0, :, 0:N].astype(F32))
+    re, im = through_screen(re, im, decoded(shared[0, :, 0:N]))
     sent(forward(re, im, 0, h, twiddle, table), twiddle, send, out)
     both = jnp.concatenate([shared[1, :, 0:N], shared[3, :, 0:N]], axis=0).astype(F32)
     for block in range(8):
@@ -251,12 +260,12 @@
 def column_kernel(layer, came, carried, *rest):
     groups = gathered(carried, 0, 16)
     which = layer // 2
-    phase = jnp.concatenate([groups[which], groups[2 + which]], axis=0)
+    phase = decoded(jnp.concatenate([groups[which], groups[2 + which]], axis=0))
     middle(layer, came, phase, *rest)
 
 
 def row_kernel(layer, came, shared, *rest):
-    middle(layer, came, shared[layer + 1, :, 0:N].astype(F32), *rest)
+    middle(layer, came, decoded(shared[layer + 1, :, 0:N]), *rest)
 
 
 def last_kernel(
@@ -333,30 +342,29 @@
     tables = {name: jnp.asarray(value) for name, value in angle_tables().items()}
     table, back, send = tables["forward"], tables["plain"], tables["send"]
 
-    payload, held, table, send, twiddle = call(
+    payload, held, twiddle = call(
         payload_kernel,
         (
             jax.ShapeDtypeStruct((4, 32, N + 128), BF),
             jax.ShapeDtypeStruct(launch.shape[1:], BF),
-            jax.ShapeDtypeStruct(table.shape, BF),
-            jax.ShapeDtypeStruct(send.shape, BF),
             jax.ShapeDtypeStruct((24, Q), F32),
         ),
         distance,
         *[
             pltpu.with_memory_space_constraint(x, pltpu.HBM)
             for x in (
-                screens, launch, send_table.reshape(1, 32), send_counts, table, send
+                screens, launch, send_table.reshape(1, 32), send_counts
             )
         ],
-        in_specs=[SMEM] + [FAR] * 6,
-        out_specs=(VMEM,) * 5,
+        in_specs=[SMEM] + [FAR] * 4,
+        out_specs=(VMEM,) * 3,
         scratch_shapes=[
             pltpu.VMEM(screens.shape, F32),
             pltpu.VMEM((1, 32), jnp.int32),
             pltpu.VMEM((1, 32), jnp.int32),
-            pltpu.SemaphoreType.DMA((6,)),
+            pltpu.SemaphoreType.DMA((4,)),
         ],
+        cost_estimate=pl.CostEstimate(flops=1500000000, bytes_accessed=4000000, transcendentals=0),
         name="payload",
     )
     shared = exchanged(payload, "layer")

time: 86.1 us -> 85.9 us (level)
  no operation moved by 1% of the time
where the time goes in v10:
time: 85.9 us; the launch traced here: 85.6 us
  blocking collectives  76.3 us (89%)
  Pallas kernels  7.55 us (9%)
  between operations  1.34 us (2%)
    all_to_all x6, blocking collectives, exchanged(): lax.all_to_all(block, axis, split_axis=0, concat_axis=0, tiled=True, axis...  76.3 us
    pallas_call x7, Pallas kernels, call(): pl.pallas_call(kernel, out_shape=shapes, compiler_params=pltpu.CompilerPa...  7.55 us
  transfers between devices with their start and end apart: 1, of which 0 were waited for; matrix products, arithmetic and copies ran while one was open for 0% of the time, Pallas kernels for 0%

profile of v10, /device:TPU:1, one launch (start us, length us, event | category | flops | bytes accessed | tf_op | source)
XLA Modules:
  0.0 85.6 jit_solution(3039897467146540149)
XLA Ops:
  1.3 0.0 copy-start
  1.3 0.0 copy-start.1
  1.3 1.1 %payload.1 = (bf16[4,32,1152]{2,1,0:T(8,128)(2,1)S(1)}, bf16[2,32,1024]{2,1,0:T(8,128)(2,1)S(1)}, f32[24,256]{1,0:T(8,128)S(1)}) custom-call(f32[1]{0:T(128)S(6)} %copy.14.distance, f32[1,32,1024]{2,1,0:T(8,128)} %far_screens.1, bf16[2,2,32,1024]{3,2,1,0:T(8,128)(2,1)} %launch.1, s32[1,32]{1,0:T(1,128)} %bitcast.13, s32[1,32]{1,0:T(1,128)} %far_counts.1), custom_call_target="tpu_custom_call" | custom-call | flops 1500000000 | bytes 4000000 | tf_op jit(solution)/shard_map/payload/pallas_call | solution.py:326
  2.4 0.0 copy-start.2
  2.4 10.8 %all_to_all.36.shared.refs_1_ = bf16[4,32,1152]{2,1,0:T(8,128)(2,1)S(1)} all-to-all(bf16[4,32,1152]{2,1,0:T(8,128)(2,1)S(1)} %get-tuple-element.12), channel_id=1, replica_groups=mesh['layer'=4,'strip'=32] {'layer'}, dimensions={0} | all-to-all | bytes 589824 | tf_op jit(solution)/shard_map/all_to_all | solution.py:336
  13.2 0.0 copy-done
  13.2 0.0 copy-done.1
  13.2 0.7 rows0.1
  13.9 18.9 %all_to_all.37.refs_0_.refs_1_ = bf16[32,32,128]{2,1,0:T(8,128)(2,1)S(1)} all-to-all(bf16[32,32,128]{2,1,0:T(8,128)(2,1)S(1)} %get-tuple-element.14), channel_id=1, replica_groups=mesh['layer'=4,'strip'=32] {'strip'}, dimensions={0} | all-to-all | bytes 524288 | tf_op jit(solution)/shard_map/all_to_all | solution.py:336
  32.8 0.0 copy-done.2
  32.8 1.1 %columns01.1 = bf16[32,16,128]{2,1,0:T(8,128)(2,1)S(1)} custom-call(bf16[32,32,128]{2,1,0:T(8,128)(2,1)S(1)} %all_to_all.37.refs_0_.refs_1_, bf16[32,32,128]{2,1,0:T(8,128)(2,1)S(1)} %all_to_all.37.refs_0_.refs_1_, f32[8,1024]{1,0:T(8,128)S(1)} %get-tuple-element.15.refs_2_.h, f32[24,256]{1,0:T(8,128)S(1)} %get-tuple-element.13.twiddle.refs_3_, ...), custom_call_target="tpu_custom_call" | custom-call | tf_op jit(solution)/shard_map/columns01/pallas_call | solution.py:326
  33.9 11.2 %all_to_all.38.refs_0_ = bf16[32,16,128]{2,1,0:T(8,128)(2,1)S(1)} all-to-all(bf16[32,16,128]{2,1,0:T(8,128)(2,1)S(1)} %columns01.1), channel_id=1, replica_groups=mesh['layer'=4,'strip'=32] {'strip'}, dimensions={0} | all-to-all | bytes 262144 | tf_op jit(solution)/shard_map/all_to_all | solution.py:336
  45.1 1.2 %rows12.1 = bf16[32,16,128]{2,1,0:T(8,128)(2,1)S(1)} custom-call(bf16[32,16,128]{2,1,0:T(8,128)(2,1)S(1)} %all_to_all.38.refs_0_, bf16[4,32,1152]{2,1,0:T(8,128)(2,1)S(1)} %all_to_all.36.shared.refs_1_, f32[8,1024]{1,0:T(8,128)S(1)} %get-tuple-element.15.refs_2_.h, f32[24,256]{1,0:T(8,128)S(1)} %get-tuple-element.13.twiddle.refs_3_, ...), custom_call_target="tpu_custom_call" | custom-call | tf_op jit(solution)/shard_map/rows12/pallas_call | solution.py:326
  46.2 11.3 %all_to_all.39.refs_0_ = bf16[32,16,128]{2,1,0:T(8,128)(2,1)S(1)} all-to-all(bf16[32,16,128]{2,1,0:T(8,128)(2,1)S(1)} %rows12.1), channel_id=1, replica_groups=mesh['layer'=4,'strip'=32] {'strip'}, dimensions={0} | all-to-all | bytes 262144 | tf_op jit(solution)/shard_map/all_to_all | solution.py:336
  57.5 1.1 %columns23.1 = bf16[32,16,128]{2,1,0:T(8,128)(2,1)S(1)} custom-call(bf16[32,16,128]{2,1,0:T(8,128)(2,1)S(1)} %all_to_all.39.refs_0_, bf16[32,32,128]{2,1,0:T(8,128)(2,1)S(1)} %all_to_all.37.refs_0_.refs_1_, f32[8,1024]{1,0:T(8,128)S(1)} %get-tuple-element.15.refs_2_.h, f32[24,256]{1,0:T(8,128)S(1)} %get-tuple-element.13.twiddle.refs_3_, ...), custom_call_target="tpu_custom_call" | custom-call | tf_op jit(solution)/shard_map/columns23/pallas_call | solution.py:326
  58.6 11.3 %all_to_all.40.came = bf16[32,16,128]{2,1,0:T(8,128)(2,1)S(1)} all-to-all(bf16[32,16,128]{2,1,0:T(8,128)(2,1)S(1)} %columns23.1), channel_id=1, replica_groups=mesh['layer'=4,'strip'=32] {'strip'}, dimensions={0} | all-to-all | bytes 262144 | tf_op jit(solution)/shard_map/all_to_all | solution.py:336
  69.9 0.0 copy-done.3
  69.9 0.0 copy-done.4
  69.9 0.0 copy-done.5
  69.9 1.6 %rows3.1 = (bf16[2,32,1024]{2,1,0:T(8,128)(2,1)S(1)}, f32[64,16]{1,0:T(8,128)S(1)}) custom-call(bf16[32,16,128]{2,1,0:T(8,128)(2,1)S(1)} %all_to_all.40.came, bf16[4,32,1152]{2,1,0:T(8,128)(2,1)S(1)} %all_to_all.36.shared.refs_1_, f32[8,1024]{1,0:T(8,128)S(1)} %get-tuple-element.15.refs_2_.h, f32[24,256]{1,0:T(8,128)S(1)} %get-tuple-element.13.twiddle.refs_3_, ...), custom_call_target="tpu_custom_call" | custom-call | tf_op jit(solution)/shard_map/rows3/pallas_call | solution.py:326
  71.5 0.3 collective-permute-start
  71.9 13.0 %all_to_all.41 = f32[64,1,16]{2,1,0:T(1,128)S(1)} all-to-all(f32[64,1,16]{2,1,0:T(1,128)S(1)} %bitcast.11), channel_id=1, replica_groups={{0,1,2,3,4,5,6,7,8,9,10,11,12,13,14,15,16,17,18,19,20,21,22,23,24,25,26..., dimensions={0} | all-to-all | bytes 8192 | tf_op jit(solution)/shard_map/all_to_all | solution.py:336
  84.8 0.0 collective-permute-done.other
  84.8 0.7 outputs.1
  (3 shorter events, 0.0 us)
Async XLA Ops:
  1.3 11.9 %copy-start = (bf16[512,512]{1,0:T(8,128)(2,1)S(1)}, bf16[512,512]{1,0:T(8,128)(2,1)}, u32[]{:S(2)}) copy-start(bf16[512,512]{1,0:T(8,128)(2,1)} %constant.10.clone.table.refs_4_) | copy-start | bytes 1572868
  1.3 11.9 %copy-start.1 = (bf16[512,512]{1,0:T(8,128)(2,1)S(1)}, bf16[512,512]{1,0:T(8,128)(2,1)}, u32[]{:S(2)}) copy-start(bf16[512,512]{1,0:T(8,128)(2,1)} %constant.12.clone.send.refs_6_) | copy-start | bytes 1572868
  2.4 30.4 %copy-start.2 = (bf16[512,512]{1,0:T(8,128)(2,1)S(1)}, bf16[512,512]{1,0:T(8,128)(2,1)}, u32[]{:S(2)}) copy-start(bf16[512,512]{1,0:T(8,128)(2,1)} %constant.11.clone.refs_5_.back) | copy-start | bytes 1572868
  45.1 24.8 %copy-start.3 = (bf16[512,2048]{1,0:T(8,128)(2,1)S(1)}, bf16[512,2048]{1,0:T(8,128)(2,1)}, u32[]{:S(2)}) copy-start(bf16[512,2048]{1,0:T(8,128)(2,1)} %constant.14.clone.spots) | copy-start | bytes 6291460
  45.1 24.8 %copy-start.4 = (bf16[512,512]{1,0:T(8,128)(2,1)S(1)}, bf16[512,512]{1,0:T(8,128)(2,1)}, u32[]{:S(2)}) copy-start(bf16[512,512]{1,0:T(8,128)(2,1)} %constant.13.clone.back_sub) | copy-start | bytes 1572868
  45.1 24.8 %copy-start.5 = (bf16[1024,16]{0,1:T(8,128)(2,1)S(1)}, bf16[1024,16]{0,1:T(8,128)(2,1)}, u32[]{:S(2)}) copy-start(bf16[1024,16]{0,1:T(8,128)(2,1)} %param.14) | copy-start | bytes 98308
  71.5 13.3 %collective-permute-start = (bf16[2,32,1024]{2,1,0:T(8,128)(2,1)S(1)}, bf16[2,32,1024]{2,1,0:T(8,128)(2,1)S(1)}, u32[]{:S(2)}, u32[]{:S(2)}) collective-permute-start(bf16[2,32,1024]{2,1,0:T(8,128)(2,1)S(1)} %get-tuple-element.16.mine), channel_id=1, source_target_pairs={{0,32},{32,0},{64,96},{96,64},{1,33},{33,1},{65,97},{97,65},{2,34}... | collective-permute-start | bytes 393224 | tf_op jit(solution)/shard_map/ppermute | solution.py:405

commit v11 on v9

--- a/solution.py
+++ b/solution.py
@@ -200,8 +200,8 @@
 
 
 def payload_kernel(
-    distance, far_screens, launch, far_targets, far_counts,
-    shared, held, picks, twiddle,
+    distance, far_screens, far_targets, far_counts,
+    shared, picks, twiddle,
     screens, targets, counts, sems,
 ):
     group = lax.axis_index("layer")
@@ -209,7 +209,6 @@
         pltpu.make_async_copy(source, target, sems.at[i])
         for i, (source, target) in enumerate([
             (far_screens, screens), (far_targets, targets), (far_counts, counts),
-            (launch.at[group % 2], held),
         ])
     ]
     for copy in copies:
@@ -222,20 +221,19 @@
     tail = jnp.where(row == 0, high, jnp.where(row == 1, middle, jnp.where(row == 2, low, 0.0)))
     tail = tail.astype(BF)
     twiddles(twiddle)
-    for copy in copies[:3]:
+    for copy in copies:
         copy.wait()
     phase = coded(screens[0])
     for other in range(4):
         shared[other, :, 0:N] = phase
         shared[other, :, N : N + 128] = tail
     picks[...] = jnp.where(group < counts[...], targets[...], -1)
-    for copy in copies[3:]:
-        copy.wait()
-
-
-def first_kernel(held, shared, twiddle, table, send, out, h):
+
+
+def first_kernel(launch, shared, twiddle, table, send, out, h):
     spectra(shared, h)
-    re, im = quarters(held[0].astype(F32)), quarters(held[1].astype(F32))
+    field = lax.axis_index("layer") % 2
+    re, im = quarters(launch[field, 0].astype(F32)), quarters(launch[field, 1].astype(F32))
     re, im = through_screen(re, im, decoded(shared[0, :, 0:N]))
     sent(forward(re, im, 0, h, twiddle, table), twiddle, send, out)
     both = jnp.concatenate([shared[1, :, 0:N], shared[3, :, 0:N]], axis=0).astype(F32)
@@ -339,11 +337,10 @@
     tables = {name: jnp.asarray(value) for name, value in angle_tables().items()}
     table, back, send = tables["forward"], tables["plain"], tables["send"]
 
-    payload, held, picks, twiddle = call(
+    payload, picks, twiddle = call(
         payload_kernel,
         (
             jax.ShapeDtypeStruct((4, 32, N + 128), BF),
-            jax.ShapeDtypeStruct(launch.shape[1:], BF),
             jax.ShapeDtypeStruct((1, 32), jnp.int32),
             jax.ShapeDtypeStruct((24, Q), F32),
         ),
@@ -351,16 +348,16 @@
         *[
             pltpu.with_memory_space_constraint(x, pltpu.HBM)
             for x in (
-                screens, launch, send_table.reshape(1, 32), send_counts
+                screens, send_table.reshape(1, 32), send_counts
             )
         ],
-        in_specs=[SMEM] + [FAR] * 4,
-        out_specs=(VMEM,) * 4,
+        in_specs=[SMEM] + [FAR] * 3,
+        out_specs=(VMEM,) * 3,
         scratch_shapes=[
             pltpu.VMEM(screens.shape, F32),
             pltpu.VMEM((1, 32), jnp.int32),
             pltpu.VMEM((1, 32), jnp.int32),
-            pltpu.SemaphoreType.DMA((4,)),
+            pltpu.SemaphoreType.DMA((3,)),
         ],
         cost_estimate=pl.CostEstimate(flops=1500000000, bytes_accessed=4000000, transcendentals=0),
         name="payload",
@@ -373,7 +370,7 @@
     pairs = [[32 * group + strip for group in pair for strip in range(32)] for pair in ((0, 1), (2, 3))]
     leaving, h = call(
         first_kernel, (wide, jax.ShapeDtypeStruct((8, N), F32)),
-        held, shared, twiddle, table, send, name="rows0",
+        launch, shared, twiddle, table, send, name="rows0",
     )
     carried = exchanged(leaving)
 

time: 86 us -> 85.9 us (level)
  no operation moved by 1% of the time
where the time goes in v11:
time: 85.9 us; the launch traced here: 85.5 us
  blocking collectives  76.4 us (89%)
  Pallas kernels  7.11 us (8%)
  between operations  1.36 us (2%)
    all_to_all x6, blocking collectives, exchanged(): lax.all_to_all(block, axis, split_axis=0, concat_axis=0, tiled=True, axis...  76.4 us
    pallas_call x6, Pallas kernels, call(): pl.pallas_call(kernel, out_shape=shapes, compiler_params=pltpu.CompilerPa...  7.11 us

profile of v11, /device:TPU:1, one launch (start us, length us, event | category | flops | bytes accessed | tf_op | source)
XLA Modules:
  0.0 85.5 jit_solution(18403698773954604578)
XLA Ops:
  1.3 0.0 copy-start
  1.3 0.0 copy-start.2
  1.3 0.0 copy-start.5
  1.3 1.1 %payload.1 = (bf16[4,32,1152]{2,1,0:T(8,128)(2,1)S(1)}, s32[1,32]{1,0:T(1,128)S(1)}, f32[24,256]{1,0:T(8,128)S(1)}) custom-call(f32[1]{0:T(128)S(6)} %copy.17.distance, f32[1,32,1024]{2,1,0:T(8,128)} %far_screens.1, s32[1,32]{1,0:T(1,128)} %bitcast.9, s32[1,32]{1,0:T(1,128)} %far_counts.1), custom_call_target="tpu_custom_call" | custom-call | flops 1500000000 | bytes 4000000 | tf_op jit(solution)/shard_map/payload/pallas_call | solution.py:321
  2.4 0.0 copy-start.1
  2.4 10.8 %all_to_all.34.shared.refs_1_ = bf16[4,32,1152]{2,1,0:T(8,128)(2,1)S(1)} all-to-all(bf16[4,32,1152]{2,1,0:T(8,128)(2,1)S(1)} %get-tuple-element.9), channel_id=1, replica_groups=mesh['layer'=4,'strip'=32] {'layer'}, dimensions={0} | all-to-all | bytes 589824 | tf_op jit(solution)/shard_map/all_to_all | solution.py:331
  13.2 0.0 copy-done
  13.2 0.0 copy-done.2
  13.2 0.0 copy-done.5
  13.2 0.8 rows0.1
  13.9 18.9 %all_to_all.35.refs_0_.refs_1_ = bf16[32,32,128]{2,1,0:T(8,128)(2,1)S(1)} all-to-all(bf16[32,32,128]{2,1,0:T(8,128)(2,1)S(1)} %get-tuple-element.11), channel_id=1, replica_groups=mesh['layer'=4,'strip'=32] {'strip'}, dimensions={0} | all-to-all | bytes 524288 | tf_op jit(solution)/shard_map/all_to_all | solution.py:331
  32.8 0.0 copy-done.1
  32.8 1.1 %columns01.1 = bf16[32,16,128]{2,1,0:T(8,128)(2,1)S(1)} custom-call(bf16[32,32,128]{2,1,0:T(8,128)(2,1)S(1)} %all_to_all.35.refs_0_.refs_1_, bf16[32,32,128]{2,1,0:T(8,128)(2,1)S(1)} %all_to_all.35.refs_0_.refs_1_, f32[8,1024]{1,0:T(8,128)S(1)} %get-tuple-element.12.refs_2_.h, f32[24,256]{1,0:T(8,128)S(1)} %get-tuple-element.10.twiddle.refs_3_, ...), custom_call_target="tpu_custom_call" | custom-call | tf_op jit(solution)/shard_map/columns01/pallas_call | solution.py:321
  33.9 11.2 %all_to_all.36.refs_0_ = bf16[32,16,128]{2,1,0:T(8,128)(2,1)S(1)} all-to-all(bf16[32,16,128]{2,1,0:T(8,128)(2,1)S(1)} %columns01.1), channel_id=1, replica_groups=mesh['layer'=4,'strip'=32] {'strip'}, dimensions={0} | all-to-all | bytes 262144 | tf_op jit(solution)/shard_map/all_to_all | solution.py:331
  45.1 1.2 %rows12.1 = bf16[32,16,128]{2,1,0:T(8,128)(2,1)S(1)} custom-call(bf16[32,16,128]{2,1,0:T(8,128)(2,1)S(1)} %all_to_all.36.refs_0_, bf16[4,32,1152]{2,1,0:T(8,128)(2,1)S(1)} %all_to_all.34.shared.refs_1_, f32[8,1024]{1,0:T(8,128)S(1)} %get-tuple-element.12.refs_2_.h, f32[24,256]{1,0:T(8,128)S(1)} %get-tuple-element.10.twiddle.refs_3_, ...), custom_call_target="tpu_custom_call" | custom-call | tf_op jit(solution)/shard_map/rows12/pallas_call | solution.py:321
  46.3 11.3 %all_to_all.37.refs_0_ = bf16[32,16,128]{2,1,0:T(8,128)(2,1)S(1)} all-to-all(bf16[32,16,128]{2,1,0:T(8,128)(2,1)S(1)} %rows12.1), channel_id=1, replica_groups=mesh['layer'=4,'strip'=32] {'strip'}, dimensions={0} | all-to-all | bytes 262144 | tf_op jit(solution)/shard_map/all_to_all | solution.py:331
  57.5 1.1 %columns23.1 = bf16[64,16,128]{2,1,0:T(8,128)(2,1)S(1)} custom-call(bf16[32,16,128]{2,1,0:T(8,128)(2,1)S(1)} %all_to_all.37.refs_0_, bf16[32,32,128]{2,1,0:T(8,128)(2,1)S(1)} %all_to_all.35.refs_0_.refs_1_, f32[8,1024]{1,0:T(8,128)S(1)} %get-tuple-element.12.refs_2_.h, f32[24,256]{1,0:T(8,128)S(1)} %get-tuple-element.10.twiddle.refs_3_, ...), custom_call_target="tpu_custom_call" | custom-call | tf_op jit(solution)/shard_map/columns23/pallas_call | solution.py:321
  58.7 13.4 %all_to_all.38.came = bf16[64,16,128]{2,1,0:T(8,128)(2,1)S(1)} all-to-all(bf16[64,16,128]{2,1,0:T(8,128)(2,1)S(1)} %columns23.1), channel_id=1, replica_groups={{0,1,2,3,4,5,6,7,8,9,10,11,12,13,14,15,16,17,18,19,20,21,22,23,24,25,26..., dimensions={0} | all-to-all | bytes 524288 | tf_op jit(solution)/shard_map/all_to_all | solution.py:331
  72.1 0.0 copy-done.3
  72.1 0.0 copy-done.4
  72.1 0.0 copy-done.6
  72.1 1.9 %rows3.1 = (bf16[2,2,32,1024]{3,2,1,0:T(8,128)(2,1)}, f32[32,32]{1,0:T(8,128)S(1)}) custom-call(bf16[64,16,128]{2,1,0:T(8,128)(2,1)S(1)} %all_to_all.38.came, f32[8,1024]{1,0:T(8,128)S(1)} %get-tuple-element.12.refs_2_.h, f32[24,256]{1,0:T(8,128)S(1)} %get-tuple-element.10.twiddle.refs_3_, bf16[512,512]{1,0:T(8,128)(2,1)S(1)} %copy-done, ...), custom_call_target="tpu_custom_call" | custom-call | tf_op jit(solution)/shard_map/rows3/pallas_call | solution.py:321
  74.0 10.9 %all_to_all.39 = f32[32,1,32]{2,1,0:T(1,128)S(1)} all-to-all(f32[32,1,32]{2,1,0:T(1,128)S(1)} %bitcast.7), channel_id=1, replica_groups=mesh['layer'=4,'strip'=32] {'strip'}, dimensions={0} | all-to-all | bytes 8192 | tf_op jit(solution)/shard_map/all_to_all | solution.py:331
  84.9 0.7 copy.16
  (3 shorter events, 0.0 us)
Async XLA Ops:
  1.3 11.9 %copy-start = (bf16[512,512]{1,0:T(8,128)(2,1)S(1)}, bf16[512,512]{1,0:T(8,128)(2,1)}, u32[]{:S(2)}) copy-start(bf16[512,512]{1,0:T(8,128)(2,1)} %constant.10.clone.table.refs_4_) | copy-start | bytes 1572868
  1.3 11.9 %copy-start.2 = (bf16[512,512]{1,0:T(8,128)(2,1)S(1)}, bf16[512,512]{1,0:T(8,128)(2,1)}, u32[]{:S(2)}) copy-start(bf16[512,512]{1,0:T(8,128)(2,1)} %constant.12.clone.send.refs_6_) | copy-start | bytes 1572868
  1.3 11.9 %copy-start.5 = (bf16[2,2,32,1024]{3,2,1,0:T(8,128)(2,1)S(1)}, bf16[2,2,32,1024]{3,2,1,0:T(8,128)(2,1)}, u32[]{:S(2)}) copy-start(bf16[2,2,32,1024]{3,2,1,0:T(8,128)(2,1)} %launch.1) | copy-start | bytes 786436
  2.4 30.4 %copy-start.1 = (bf16[512,512]{1,0:T(8,128)(2,1)S(1)}, bf16[512,512]{1,0:T(8,128)(2,1)}, u32[]{:S(2)}) copy-start(bf16[512,512]{1,0:T(8,128)(2,1)} %constant.11.clone.refs_5_.back) | copy-start | bytes 1572868
  45.1 27.0 %copy-start.3 = (bf16[512,2048]{1,0:T(8,128)(2,1)S(1)}, bf16[512,2048]{1,0:T(8,128)(2,1)}, u32[]{:S(2)}) copy-start(bf16[512,2048]{1,0:T(8,128)(2,1)} %constant.14.clone.spots) | copy-start | bytes 6291460
  45.1 27.0 %copy-start.4 = (bf16[512,512]{1,0:T(8,128)(2,1)S(1)}, bf16[512,512]{1,0:T(8,128)(2,1)}, u32[]{:S(2)}) copy-start(bf16[512,512]{1,0:T(8,128)(2,1)} %constant.13.clone.back_sub) | copy-start | bytes 1572868
  45.1 27.0 %copy-start.6 = (bf16[1024,16]{0,1:T(8,128)(2,1)S(1)}, bf16[1024,16]{0,1:T(8,128)(2,1)}, u32[]{:S(2)}) copy-start(bf16[1024,16]{0,1:T(8,128)(2,1)} %param.14) | copy-start | bytes 98308

commit v12 on v11

--- a/solution.py
+++ b/solution.py
@@ -231,17 +231,17 @@
 
 
 def first_kernel(launch, shared, twiddle, table, send, out, h):
-    spectra(shared, h)
-    field = lax.axis_index("layer") % 2
-    re, im = quarters(launch[field, 0].astype(F32)), quarters(launch[field, 1].astype(F32))
-    re, im = through_screen(re, im, decoded(shared[0, :, 0:N]))
-    sent(forward(re, im, 0, h, twiddle, table), twiddle, send, out)
     both = jnp.concatenate([shared[1, :, 0:N], shared[3, :, 0:N]], axis=0).astype(F32)
     for block in range(8):
         piece = both[:, 128 * block : 128 * block + 128].T.reshape(4, 2, 16, 64)
         out[4 * block : 4 * block + 4, 16:32, :] = jnp.concatenate(
             [piece[:, 0], piece[:, 1]], axis=2
         ).astype(BF)
+    spectra(shared, h)
+    field = lax.axis_index("layer") % 2
+    re, im = quarters(launch[field, 0].astype(F32)), quarters(launch[field, 1].astype(F32))
+    re, im = through_screen(re, im, decoded(shared[0, :, 0:N]))
+    sent(forward(re, im, 0, h, twiddle, table), twiddle, send, out)
 
 
 def middle(layer, came, phase, h, twiddle, table, back, send, out):
@@ -302,10 +302,17 @@
         ).astype(BF)
         for field in range(2)
     ]
-    spot = jnp.dot(jnp.concatenate(slots, axis=0), spots[...], preferred_element_type=F32)
-    intensity = (spot[:, :1024] * spot[:, :1024] + spot[:, 1024:] * spot[:, 1024:]).astype(BF)
+    picked = jnp.concatenate(slots, axis=0)
+    intensity = []
+    for at in range(0, 1024, 256):
+        re = jnp.dot(picked, spots[:, at : at + 256], preferred_element_type=F32)
+        im = jnp.dot(picked, spots[:, 1024 + at : 1024 + at + 256], preferred_element_type=F32)
+        intensity.append((re * re + im * im).astype(BF))
     total = lax.dot_general(
-        intensity, templates[...], (((1,), (1,)), ((), ())), preferred_element_type=F32
+        jnp.concatenate(intensity, axis=1),
+        templates[...],
+        (((1,), (1,)), ((), ())),
+        preferred_element_type=F32,
     )
     for field in range(2):
         result[:, 16 * field : 16 * field + 16] = total[32 * field : 32 * field + 32]

time: 85.9 us -> 85.9 us (level)
  no operation moved by 1% of the time
where the time goes in v12:
time: 85.9 us; the launch traced here: 85.5 us
  blocking collectives  76.4 us (89%)
  Pallas kernels  7.09 us (8%)
  between operations  1.37 us (2%)
    all_to_all x6, blocking collectives, exchanged(): lax.all_to_all(block, axis, split_axis=0, concat_axis=0, tiled=True, axis...  76.4 us
    pallas_call x6, Pallas kernels, call(): pl.pallas_call(kernel, out_shape=shapes, compiler_params=pltpu.CompilerPa...  7.09 us

profile of v12, /device:TPU:1, one launch (start us, length us, event | category | flops | bytes accessed | tf_op | source)
XLA Modules:
  0.0 85.5 jit_solution(7732972953036733477)
XLA Ops:
  1.3 0.0 copy-start
  1.3 0.0 copy-start.2
  1.3 0.0 copy-start.5
  1.3 1.1 %payload.1 = (bf16[4,32,1152]{2,1,0:T(8,128)(2,1)S(1)}, s32[1,32]{1,0:T(1,128)S(1)}, f32[24,256]{1,0:T(8,128)S(1)}) custom-call(f32[1]{0:T(128)S(6)} %copy.17.distance, f32[1,32,1024]{2,1,0:T(8,128)} %far_screens.1, s32[1,32]{1,0:T(1,128)} %bitcast.9, s32[1,32]{1,0:T(1,128)} %far_counts.1), custom_call_target="tpu_custom_call" | custom-call | flops 1500000000 | bytes 4000000 | tf_op jit(solution)/shard_map/payload/pallas_call | solution.py:328
  2.4 0.0 copy-start.1
  2.4 10.8 %all_to_all.34.shared.refs_1_ = bf16[4,32,1152]{2,1,0:T(8,128)(2,1)S(1)} all-to-all(bf16[4,32,1152]{2,1,0:T(8,128)(2,1)S(1)} %get-tuple-element.9), channel_id=1, replica_groups=mesh['layer'=4,'strip'=32] {'layer'}, dimensions={0} | all-to-all | bytes 589824 | tf_op jit(solution)/shard_map/all_to_all | solution.py:338
  13.2 0.0 copy-done
  13.2 0.0 copy-done.2
  13.2 0.0 copy-done.5
  13.2 0.7 rows0.1
  13.9 18.9 %all_to_all.35.refs_0_.refs_1_ = bf16[32,32,128]{2,1,0:T(8,128)(2,1)S(1)} all-to-all(bf16[32,32,128]{2,1,0:T(8,128)(2,1)S(1)} %get-tuple-element.11), channel_id=1, replica_groups=mesh['layer'=4,'strip'=32] {'strip'}, dimensions={0} | all-to-all | bytes 524288 | tf_op jit(solution)/shard_map/all_to_all | solution.py:338
  32.8 0.0 copy-done.1
  32.8 1.1 %columns01.1 = bf16[32,16,128]{2,1,0:T(8,128)(2,1)S(1)} custom-call(bf16[32,32,128]{2,1,0:T(8,128)(2,1)S(1)} %all_to_all.35.refs_0_.refs_1_, bf16[32,32,128]{2,1,0:T(8,128)(2,1)S(1)} %all_to_all.35.refs_0_.refs_1_, f32[8,1024]{1,0:T(8,128)S(1)} %get-tuple-element.12.refs_2_.h, f32[24,256]{1,0:T(8,128)S(1)} %get-tuple-element.10.twiddle.refs_3_, ...), custom_call_target="tpu_custom_call" | custom-call | tf_op jit(solution)/shard_map/columns01/pallas_call | solution.py:328
  33.9 11.2 %all_to_all.36.refs_0_ = bf16[32,16,128]{2,1,0:T(8,128)(2,1)S(1)} all-to-all(bf16[32,16,128]{2,1,0:T(8,128)(2,1)S(1)} %columns01.1), channel_id=1, replica_groups=mesh['layer'=4,'strip'=32] {'strip'}, dimensions={0} | all-to-all | bytes 262144 | tf_op jit(solution)/shard_map/all_to_all | solution.py:338
  45.1 1.2 %rows12.1 = bf16[32,16,128]{2,1,0:T(8,128)(2,1)S(1)} custom-call(bf16[32,16,128]{2,1,0:T(8,128)(2,1)S(1)} %all_to_all.36.refs_0_, bf16[4,32,1152]{2,1,0:T(8,128)(2,1)S(1)} %all_to_all.34.shared.refs_1_, f32[8,1024]{1,0:T(8,128)S(1)} %get-tuple-element.12.refs_2_.h, f32[24,256]{1,0:T(8,128)S(1)} %get-tuple-element.10.twiddle.refs_3_, ...), custom_call_target="tpu_custom_call" | custom-call | tf_op jit(solution)/shard_map/rows12/pallas_call | solution.py:328
  46.3 11.3 %all_to_all.37.refs_0_ = bf16[32,16,128]{2,1,0:T(8,128)(2,1)S(1)} all-to-all(bf16[32,16,128]{2,1,0:T(8,128)(2,1)S(1)} %rows12.1), channel_id=1, replica_groups=mesh['layer'=4,'strip'=32] {'strip'}, dimensions={0} | all-to-all | bytes 262144 | tf_op jit(solution)/shard_map/all_to_all | solution.py:338
  57.5 1.1 %columns23.1 = bf16[64,16,128]{2,1,0:T(8,128)(2,1)S(1)} custom-call(bf16[32,16,128]{2,1,0:T(8,128)(2,1)S(1)} %all_to_all.37.refs_0_, bf16[32,32,128]{2,1,0:T(8,128)(2,1)S(1)} %all_to_all.35.refs_0_.refs_1_, f32[8,1024]{1,0:T(8,128)S(1)} %get-tuple-element.12.refs_2_.h, f32[24,256]{1,0:T(8,128)S(1)} %get-tuple-element.10.twiddle.refs_3_, ...), custom_call_target="tpu_custom_call" | custom-call | tf_op jit(solution)/shard_map/columns23/pallas_call | solution.py:328
  58.7 13.4 %all_to_all.38.came = bf16[64,16,128]{2,1,0:T(8,128)(2,1)S(1)} all-to-all(bf16[64,16,128]{2,1,0:T(8,128)(2,1)S(1)} %columns23.1), channel_id=1, replica_groups={{0,1,2,3,4,5,6,7,8,9,10,11,12,13,14,15,16,17,18,19,20,21,22,23,24,25,26..., dimensions={0} | all-to-all | bytes 524288 | tf_op jit(solution)/shard_map/all_to_all | solution.py:338
  72.1 0.0 copy-done.3
  72.1 0.0 copy-done.4
  72.1 0.0 copy-done.6
  72.1 1.9 %rows3.1 = (bf16[2,2,32,1024]{3,2,1,0:T(8,128)(2,1)}, f32[32,32]{1,0:T(8,128)S(1)}) custom-call(bf16[64,16,128]{2,1,0:T(8,128)(2,1)S(1)} %all_to_all.38.came, f32[8,1024]{1,0:T(8,128)S(1)} %get-tuple-element.12.refs_2_.h, f32[24,256]{1,0:T(8,128)S(1)} %get-tuple-element.10.twiddle.refs_3_, bf16[512,512]{1,0:T(8,128)(2,1)S(1)} %copy-done, ...), custom_call_target="tpu_custom_call" | custom-call | tf_op jit(solution)/shard_map/rows3/pallas_call | solution.py:328
  74.0 10.9 %all_to_all.39 = f32[32,1,32]{2,1,0:T(1,128)S(1)} all-to-all(f32[32,1,32]{2,1,0:T(1,128)S(1)} %bitcast.7), channel_id=1, replica_groups=mesh['layer'=4,'strip'=32] {'strip'}, dimensions={0} | all-to-all | bytes 8192 | tf_op jit(solution)/shard_map/all_to_all | solution.py:338
  84.9 0.7 copy.16
  (3 shorter events, 0.0 us)
Async XLA Ops:
  1.3 11.9 %copy-start = (bf16[512,512]{1,0:T(8,128)(2,1)S(1)}, bf16[512,512]{1,0:T(8,128)(2,1)}, u32[]{:S(2)}) copy-start(bf16[512,512]{1,0:T(8,128)(2,1)} %constant.10.clone.table.refs_4_) | copy-start | bytes 1572868
  1.3 11.9 %copy-start.2 = (bf16[512,512]{1,0:T(8,128)(2,1)S(1)}, bf16[512,512]{1,0:T(8,128)(2,1)}, u32[]{:S(2)}) copy-start(bf16[512,512]{1,0:T(8,128)(2,1)} %constant.12.clone.send.refs_6_) | copy-start | bytes 1572868
  1.3 11.9 %copy-start.5 = (bf16[2,2,32,1024]{3,2,1,0:T(8,128)(2,1)S(1)}, bf16[2,2,32,1024]{3,2,1,0:T(8,128)(2,1)}, u32[]{:S(2)}) copy-start(bf16[2,2,32,1024]{3,2,1,0:T(8,128)(2,1)} %launch.1) | copy-start | bytes 786436
  2.4 30.4 %copy-start.1 = (bf16[512,512]{1,0:T(8,128)(2,1)S(1)}, bf16[512,512]{1,0:T(8,128)(2,1)}, u32[]{:S(2)}) copy-start(bf16[512,512]{1,0:T(8,128)(2,1)} %constant.11.clone.refs_5_.back) | copy-start | bytes 1572868
  45.1 27.0 %copy-start.3 = (bf16[512,2048]{1,0:T(8,128)(2,1)S(1)}, bf16[512,2048]{1,0:T(8,128)(2,1)}, u32[]{:S(2)}) copy-start(bf16[512,2048]{1,0:T(8,128)(2,1)} %constant.14.clone.spots) | copy-start | bytes 6291460
  45.1 27.0 %copy-start.4 = (bf16[512,512]{1,0:T(8,128)(2,1)S(1)}, bf16[512,512]{1,0:T(8,128)(2,1)}, u32[]{:S(2)}) copy-start(bf16[512,512]{1,0:T(8,128)(2,1)} %constant.13.clone.back_sub) | copy-start | bytes 1572868
  45.1 27.0 %copy-start.6 = (bf16[1024,16]{0,1:T(8,128)(2,1)S(1)}, bf16[1024,16]{0,1:T(8,128)(2,1)}, u32[]{:S(2)}) copy-start(bf16[1024,16]{0,1:T(8,128)(2,1)} %param.14) | copy-start | bytes 98308

commit v13 on v12

--- a/solution.py
+++ b/solution.py
@@ -248,19 +248,21 @@
     re, im = field_of(came)
     spectrum = forward(quarters(re), quarters(im), layer, h, twiddle, table)
     re, im = inverse(spectrum, "plain", twiddle, back)
-    re, im = through_screen(re, im, phase)
+    re, im = through_screen(re, im, phase())
     sent(forward(re, im, layer + 1, h, twiddle, table), twiddle, send, out, BF)
 
 
 def column_kernel(layer, came, carried, *rest):
-    groups = gathered(carried, 0, 16)
-    which = layer // 2
-    phase = decoded(jnp.concatenate([groups[which], groups[2 + which]], axis=0))
+    def phase():
+        groups = gathered(carried, 0, 16)
+        which = layer // 2
+        return decoded(jnp.concatenate([groups[which], groups[2 + which]], axis=0))
+
     middle(layer, came, phase, *rest)
 
 
 def row_kernel(layer, came, shared, *rest):
-    middle(layer, came, decoded(shared[layer + 1, :, 0:N]), *rest)
+    middle(layer, came, lambda: decoded(shared[layer + 1, :, 0:N]), *rest)
 
 
 def last_kernel(

time: 85.9 us -> 85.9 us (level)
  no operation moved by 1% of the time
where the time goes in v13:
time: 85.9 us; the launch traced here: 85.5 us
  blocking collectives  76.4 us (89%)
  Pallas kernels  7.08 us (8%)
  between operations  1.37 us (2%)
    all_to_all x6, blocking collectives, exchanged(): lax.all_to_all(block, axis, split_axis=0, concat_axis=0, tiled=True, axis...  76.4 us
    pallas_call x6, Pallas kernels, call(): pl.pallas_call(kernel, out_shape=shapes, compiler_params=pltpu.CompilerPa...  7.08 us

profile of v13, /device:TPU:1, one launch (start us, length us, event | category | flops | bytes accessed | tf_op | source)
XLA Modules:
  0.0 85.5 jit_solution(6286517046792513159)
XLA Ops:
  1.3 0.0 copy-start
  1.3 0.0 copy-start.2
  1.3 0.0 copy-start.5
  1.3 1.1 %payload.1 = (bf16[4,32,1152]{2,1,0:T(8,128)(2,1)S(1)}, s32[1,32]{1,0:T(1,128)S(1)}, f32[24,256]{1,0:T(8,128)S(1)}) custom-call(f32[1]{0:T(128)S(6)} %copy.17.distance, f32[1,32,1024]{2,1,0:T(8,128)} %far_screens.1, s32[1,32]{1,0:T(1,128)} %bitcast.9, s32[1,32]{1,0:T(1,128)} %far_counts.1), custom_call_target="tpu_custom_call" | custom-call | flops 1500000000 | bytes 4000000 | tf_op jit(solution)/shard_map/payload/pallas_call | solution.py:330
  2.4 0.0 copy-start.1
  2.4 10.8 %all_to_all.34.shared.refs_1_ = bf16[4,32,1152]{2,1,0:T(8,128)(2,1)S(1)} all-to-all(bf16[4,32,1152]{2,1,0:T(8,128)(2,1)S(1)} %get-tuple-element.9), channel_id=1, replica_groups=mesh['layer'=4,'strip'=32] {'layer'}, dimensions={0} | all-to-all | bytes 589824 | tf_op jit(solution)/shard_map/all_to_all | solution.py:340
  13.2 0.0 copy-done
  13.2 0.0 copy-done.2
  13.2 0.0 copy-done.5
  13.2 0.7 rows0.1
  13.9 18.9 %all_to_all.35.refs_0_.refs_1_ = bf16[32,32,128]{2,1,0:T(8,128)(2,1)S(1)} all-to-all(bf16[32,32,128]{2,1,0:T(8,128)(2,1)S(1)} %get-tuple-element.11), channel_id=1, replica_groups=mesh['layer'=4,'strip'=32] {'strip'}, dimensions={0} | all-to-all | bytes 524288 | tf_op jit(solution)/shard_map/all_to_all | solution.py:340
  32.8 0.0 copy-done.1
  32.8 1.1 %columns01.1 = bf16[32,16,128]{2,1,0:T(8,128)(2,1)S(1)} custom-call(bf16[32,32,128]{2,1,0:T(8,128)(2,1)S(1)} %all_to_all.35.refs_0_.refs_1_, bf16[32,32,128]{2,1,0:T(8,128)(2,1)S(1)} %all_to_all.35.refs_0_.refs_1_, f32[8,1024]{1,0:T(8,128)S(1)} %get-tuple-element.12.refs_2_.h, f32[24,256]{1,0:T(8,128)S(1)} %get-tuple-element.10.twiddle.refs_3_, ...), custom_call_target="tpu_custom_call" | custom-call | tf_op jit(solution)/shard_map/columns01/pallas_call | solution.py:330
  33.9 11.2 %all_to_all.36.refs_0_ = bf16[32,16,128]{2,1,0:T(8,128)(2,1)S(1)} all-to-all(bf16[32,16,128]{2,1,0:T(8,128)(2,1)S(1)} %columns01.1), channel_id=1, replica_groups=mesh['layer'=4,'strip'=32] {'strip'}, dimensions={0} | all-to-all | bytes 262144 | tf_op jit(solution)/shard_map/all_to_all | solution.py:340
  45.1 1.2 %rows12.1 = bf16[32,16,128]{2,1,0:T(8,128)(2,1)S(1)} custom-call(bf16[32,16,128]{2,1,0:T(8,128)(2,1)S(1)} %all_to_all.36.refs_0_, bf16[4,32,1152]{2,1,0:T(8,128)(2,1)S(1)} %all_to_all.34.shared.refs_1_, f32[8,1024]{1,0:T(8,128)S(1)} %get-tuple-element.12.refs_2_.h, f32[24,256]{1,0:T(8,128)S(1)} %get-tuple-element.10.twiddle.refs_3_, ...), custom_call_target="tpu_custom_call" | custom-call | tf_op jit(solution)/shard_map/rows12/pallas_call | solution.py:330
  46.3 11.3 %all_to_all.37.refs_0_ = bf16[32,16,128]{2,1,0:T(8,128)(2,1)S(1)} all-to-all(bf16[32,16,128]{2,1,0:T(8,128)(2,1)S(1)} %rows12.1), channel_id=1, replica_groups=mesh['layer'=4,'strip'=32] {'strip'}, dimensions={0} | all-to-all | bytes 262144 | tf_op jit(solution)/shard_map/all_to_all | solution.py:340
  57.5 1.1 %columns23.1 = bf16[64,16,128]{2,1,0:T(8,128)(2,1)S(1)} custom-call(bf16[32,16,128]{2,1,0:T(8,128)(2,1)S(1)} %all_to_all.37.refs_0_, bf16[32,32,128]{2,1,0:T(8,128)(2,1)S(1)} %all_to_all.35.refs_0_.refs_1_, f32[8,1024]{1,0:T(8,128)S(1)} %get-tuple-element.12.refs_2_.h, f32[24,256]{1,0:T(8,128)S(1)} %get-tuple-element.10.twiddle.refs_3_, ...), custom_call_target="tpu_custom_call" | custom-call | tf_op jit(solution)/shard_map/columns23/pallas_call | solution.py:330
  58.7 13.4 %all_to_all.38.came = bf16[64,16,128]{2,1,0:T(8,128)(2,1)S(1)} all-to-all(bf16[64,16,128]{2,1,0:T(8,128)(2,1)S(1)} %columns23.1), channel_id=1, replica_groups={{0,1,2,3,4,5,6,7,8,9,10,11,12,13,14,15,16,17,18,19,20,21,22,23,24,25,26..., dimensions={0} | all-to-all | bytes 524288 | tf_op jit(solution)/shard_map/all_to_all | solution.py:340
  72.1 0.0 copy-done.3
  72.1 0.0 copy-done.4
  72.1 0.0 copy-done.6
  72.1 1.9 %rows3.1 = (bf16[2,2,32,1024]{3,2,1,0:T(8,128)(2,1)}, f32[32,32]{1,0:T(8,128)S(1)}) custom-call(bf16[64,16,128]{2,1,0:T(8,128)(2,1)S(1)} %all_to_all.38.came, f32[8,1024]{1,0:T(8,128)S(1)} %get-tuple-element.12.refs_2_.h, f32[24,256]{1,0:T(8,128)S(1)} %get-tuple-element.10.twiddle.refs_3_, bf16[512,512]{1,0:T(8,128)(2,1)S(1)} %copy-done, ...), custom_call_target="tpu_custom_call" | custom-call | tf_op jit(solution)/shard_map/rows3/pallas_call | solution.py:330
  74.0 10.9 %all_to_all.39 = f32[32,1,32]{2,1,0:T(1,128)S(1)} all-to-all(f32[32,1,32]{2,1,0:T(1,128)S(1)} %bitcast.7), channel_id=1, replica_groups=mesh['layer'=4,'strip'=32] {'strip'}, dimensions={0} | all-to-all | bytes 8192 | tf_op jit(solution)/shard_map/all_to_all | solution.py:340
  84.9 0.7 copy.16
  (3 shorter events, 0.0 us)
Async XLA Ops:
  1.3 11.9 %copy-start = (bf16[512,512]{1,0:T(8,128)(2,1)S(1)}, bf16[512,512]{1,0:T(8,128)(2,1)}, u32[]{:S(2)}) copy-start(bf16[512,512]{1,0:T(8,128)(2,1)} %constant.10.clone.table.refs_4_) | copy-start | bytes 1572868
  1.3 11.9 %copy-start.2 = (bf16[512,512]{1,0:T(8,128)(2,1)S(1)}, bf16[512,512]{1,0:T(8,128)(2,1)}, u32[]{:S(2)}) copy-start(bf16[512,512]{1,0:T(8,128)(2,1)} %constant.12.clone.send.refs_6_) | copy-start | bytes 1572868
  1.3 11.9 %copy-start.5 = (bf16[2,2,32,1024]{3,2,1,0:T(8,128)(2,1)S(1)}, bf16[2,2,32,1024]{3,2,1,0:T(8,128)(2,1)}, u32[]{:S(2)}) copy-start(bf16[2,2,32,1024]{3,2,1,0:T(8,128)(2,1)} %launch.1) | copy-start | bytes 786436
  2.4 30.4 %copy-start.1 = (bf16[512,512]{1,0:T(8,128)(2,1)S(1)}, bf16[512,512]{1,0:T(8,128)(2,1)}, u32[]{:S(2)}) copy-start(bf16[512,512]{1,0:T(8,128)(2,1)} %constant.11.clone.refs_5_.back) | copy-start | bytes 1572868
  45.1 27.0 %copy-start.3 = (bf16[512,2048]{1,0:T(8,128)(2,1)S(1)}, bf16[512,2048]{1,0:T(8,128)(2,1)}, u32[]{:S(2)}) copy-start(bf16[512,2048]{1,0:T(8,128)(2,1)} %constant.14.clone.spots) | copy-start | bytes 6291460
  45.1 27.0 %copy-start.4 = (bf16[512,512]{1,0:T(8,128)(2,1)S(1)}, bf16[512,512]{1,0:T(8,128)(2,1)}, u32[]{:S(2)}) copy-start(bf16[512,512]{1,0:T(8,128)(2,1)} %constant.13.clone.back_sub) | copy-start | bytes 1572868
  45.1 27.0 %copy-start.6 = (bf16[1024,16]{0,1:T(8,128)(2,1)S(1)}, bf16[1024,16]{0,1:T(8,128)(2,1)}, u32[]{:S(2)}) copy-start(bf16[1024,16]{0,1:T(8,128)(2,1)} %param.14) | copy-start | bytes 98308
